TPU v7x, 32 devices: a whole 2x2x4 slice. The times are simulated.
32 devices in a mesh: dp: 4 (over y, x), expert: 8 (over z, core).
Axes of the slice: x: 2, y: 2, z: 4, core: 2. Of those that a mesh axis runs over, the one named last changes fastest.
Arguments:
- tokens: bfloat16 [4, 1536, 1280], P('dp', 'expert'), may hold values from -6 to 6
- cotangent: bfloat16 [4, 1536, 1280], P('dp', 'expert'), may hold values from -6 to 6
- lengths: int32 [4, 4], P('dp'), may hold values from 1 to 1532, as said below
- routes: int32 [4, 1536, 7], P('dp', 'expert'), may hold values from 0 to 15, all different within a row; in each aligned block of 192 rows (0 to 191, 192 to 383, ..., all dimensions but the last counted through in order) at most 120 rows name the same one
- attn_qkv: float32 [1280, 3840], P(('dp', 'expert')), may hold values from -0.25 to 0.25
- attn_out: float32 [1280, 1280], P(None, ('dp', 'expert')), may hold values from -1.25 to 1.25
- shared_gate: float32 [1280, 896], P(('dp', 'expert')), may hold values from -0.15625 to 0.15625
- shared_up: float32 [1280, 896], P(('dp', 'expert')), may hold values from -0.15625 to 0.15625
- shared_down: float32 [896, 1280], P(None, ('dp', 'expert')), may hold values from -0.375 to 0.375
- router: float32 [1280, 16], P(('dp', 'expert')), may hold values from -0.078125 to 0.078125
- gains: float32 [2, 1280], P(None, ('dp', 'expert')), may hold values from 0.5 to 1.5
- expert_gate: float32 [16, 1280, 896], P('expert', 'dp'), may hold values from -0.15625 to 0.15625
- expert_up: float32 [16, 1280, 896], P('expert', 'dp'), may hold values from -0.15625 to 0.15625
- expert_down: float32 [16, 896, 1280], P('expert', None, 'dp'), may hold values from -0.5 to 0.5
Outputs:
- output: bfloat16 [4, 1536, 1280], P('dp', 'expert')
- input_grad: bfloat16 [4, 1536, 1280], P('dp', 'expert')
- grad_attn_qkv: float32 [1280, 3840], P(('dp', 'expert'))
- grad_attn_out: float32 [1280, 1280], P(None, ('dp', 'expert'))
- grad_shared_gate: float32 [1280, 896], P(('dp', 'expert'))
- grad_shared_up: float32 [1280, 896], P(('dp', 'expert'))
- grad_shared_down: float32 [896, 1280], P(None, ('dp', 'expert'))
- grad_router: float32 [1280, 16], P(('dp', 'expert'))
- grad_gains: float32 [2, 1280], P(None, ('dp', 'expert'))
- grad_expert_gate: float32 [16, 1280, 896], P('expert', 'dp')
- grad_expert_up: float32 [16, 1280, 896], P('expert', 'dp')
- grad_expert_down: float32 [16, 896, 1280], P('expert', None, 'dp')
Inputs may be any that keep to these rules, and one draw needn't show every extreme that they name: Each row's lengths sum to less than 1536; one document of each row, at a drawn place, starts among the first 192 positions and ends among the last 192; in one drawn row all other documents have length 1 and one padding position follows. `routes`: each position names 7 different experts; within the 192 positions of one device no expert is named more than 120 times.
All inputs are finite; a program needn't handle non-finite values.
Results may differ from a plain program's by a relative error of at most 0.025.
The roundings to bfloat16 on the way count: a program that leaves them out, or rounds other values in their place, can miss the bound.
Values may be sent and summed in bfloat16 or wider, within the bound.
A program may use at most 320 MiB of HBM per device.

v0:
```python
import jax
import jax.numpy as jnp
from jax import lax
from jax.sharding import PartitionSpec as P

H = 10
HD = 128
TOP = 7
EXP_DEV = 2


epsilon = 1e-06


def segments(lengths, places):
    doc_ends = jnp.cumsum(lengths)
    doc_starts = doc_ends - lengths
    live_total = doc_ends[-1]
    doc_index = jnp.sum((places[:, None] >= doc_ends[None, :]).astype(jnp.int32), axis=1)
    is_live = places < live_total
    segment = jnp.where(is_live, doc_index, lengths.shape[0] + places)
    matches = doc_index[:, None] == jnp.arange(lengths.shape[0], dtype=jnp.int32)[None, :]
    doc_first = jnp.sum(jnp.where(matches, doc_starts[None, :], 0), axis=1)
    rope_pos = places - jnp.where(is_live, doc_first, live_total)
    return (segment, rope_pos)


def rotate(values, rope_pos, direction):
    half_width = values.shape[-1] // 2
    frequency = 10000.0 ** (-jnp.arange(half_width, dtype=jnp.float32) / half_width)
    angles = rope_pos.astype(jnp.float32)[:, None] * frequency[None, :]
    cosine = jnp.cos(angles)[:, None, :]
    sine_row = direction * jnp.sin(angles)[:, None, :]
    front_half = values[..., :half_width]
    rear_half = values[..., half_width:]
    return jnp.concatenate(
        [front_half * cosine - rear_half * sine_row, front_half * sine_row + rear_half * cosine],
        axis=-1,
    )


def inverse_rms(values):
    return lax.rsqrt(jnp.mean(values * values, axis=-1, keepdims=True) + epsilon)


def slots_of(route_rows, expert_total):
    flat_ids = route_rows.reshape(-1)
    onehot = (flat_ids[:, None] == jnp.arange(expert_total, dtype=jnp.int32)[None, :]).astype(
        jnp.int32
    )
    earlier = jnp.cumsum(onehot, axis=0) - onehot
    return jnp.sum(earlier * onehot, axis=1).reshape(route_rows.shape)


def block_length(row_count):
    block_size = row_count
    for candidate in (1024, 512):
        if row_count > candidate and row_count % candidate == 0:
            block_size = candidate
            break
    return block_size


def split_blocks(pieces):
    piece_rows = pieces[0].shape[0]
    block_size = block_length(piece_rows)
    shaped = tuple(
        (
            member.reshape((piece_rows // block_size, block_size) + member.shape[1:])
            for member in pieces
        )
    )
    offsets = jnp.arange(piece_rows // block_size, dtype=jnp.int32) * block_size
    return (shaped, offsets)


def silu_parts(values):
    sigmoid_v = jax.nn.sigmoid(values)
    return (values * sigmoid_v, sigmoid_v * (1.0 + values * (1.0 - sigmoid_v)))


def local(
    tokens,
    cotangent,
    lengths,
    routes,
    attn_qkv,
    attn_out,
    shared_gate,
    shared_up,
    shared_down,
    router,
    gains,
    expert_gate,
    expert_up,
    expert_down,
):
    bfloat = jnp.bfloat16
    single = jnp.float32
    row_count = tokens.shape[1]
    model_width = tokens.shape[2]
    chain_length = lax.axis_size("expert")
    device_index = lax.axis_index("expert")
    expert_total = EXP_DEV * chain_length
    capacity = max(8, 8 * (row_count * TOP * 3 // (expert_total * 16)))
    score_scale = HD ** (-0.5)
    qkv_weight, out_weight, gate_shared, up_shared, down_shared, route_weight, gain_pair = (
        lax.all_gather(attn_qkv.astype(bfloat), ("dp", "expert"), axis=0, tiled=True),
        lax.all_gather(attn_out.astype(bfloat), ("dp", "expert"), axis=1, tiled=True),
        lax.all_gather(shared_gate.astype(bfloat), ("dp", "expert"), axis=0, tiled=True),
        lax.all_gather(shared_up.astype(bfloat), ("dp", "expert"), axis=0, tiled=True),
        lax.all_gather(shared_down.astype(bfloat), ("dp", "expert"), axis=1, tiled=True),
        lax.all_gather(router.astype(bfloat), ("dp", "expert"), axis=0, tiled=True),
        lax.all_gather(gains.astype(bfloat), ("dp", "expert"), axis=1, tiled=True),
    )
    gate_expert, up_expert, down_expert = (
        lax.all_gather(expert_gate.astype(bfloat), "dp", axis=1, tiled=True),
        lax.all_gather(expert_up.astype(bfloat), "dp", axis=1, tiled=True),
        lax.all_gather(expert_down.astype(bfloat), "dp", axis=2, tiled=True),
    )
    inputs = tokens[0].astype(single)
    doc_lengths = lengths[0]
    route_ids = routes[0]
    own_first = device_index * row_count
    places = own_first + jnp.arange(row_count, dtype=jnp.int32)
    segment, rope_pos = segments(doc_lengths, places)
    gain_attn = gain_pair[0].astype(single)
    gain_moe = gain_pair[1].astype(single)
    inverse_one = inverse_rms(inputs)
    unit_one = inputs * inverse_one
    normed = (unit_one * gain_attn).astype(bfloat)
    projected = jnp.dot(normed, qkv_weight, preferred_element_type=single).reshape(
        row_count, 3, H, HD
    )
    queries = rotate(projected[:, 0], rope_pos, 1.0).astype(bfloat)
    key_rows = rotate(projected[:, 1], rope_pos, 1.0).astype(bfloat)
    value_rows = projected[:, 2].astype(bfloat)

    def masked_scores(query_part, query_seg, query_place, key_part, key_first):
        key_place = key_first + jnp.arange(key_part.shape[0], dtype=jnp.int32)
        key_seg, unused = segments(doc_lengths, key_place)
        allowed = (query_seg[:, None] == key_seg[None, :]) & (
            key_place[None, :] <= query_place[:, None]
        )
        products = jnp.einsum("qhd,khd->hqk", query_part, key_part, preferred_element_type=single)
        scores = jnp.where(allowed[None], products * score_scale, -1e30)
        return (scores, allowed[None])

    initial = (
        jnp.full((H, row_count), -1e30, single),
        jnp.zeros((H, row_count), single),
        jnp.zeros((row_count, H, HD), single),
    )
    shaped, offsets = split_blocks(
        (
            lax.all_gather(key_rows, "expert", axis=0, tiled=True),
            lax.all_gather(value_rows, "expert", axis=0, tiled=True),
        )
    )

    def advance(carried, inputs_block):
        row_max, totals, accumulated = carried
        key_part, value_part, offset = inputs_block
        scores, allowed = masked_scores(queries, segment, places, key_part, offset)
        new_max = jnp.maximum(row_max, jnp.max(scores, axis=-1))
        factor = jnp.exp(row_max - new_max)
        weights = jnp.where(allowed, jnp.exp(scores - new_max[:, :, None]), 0.0)
        totals = totals * factor + jnp.sum(weights, axis=-1)
        update = jnp.einsum(
            "hqk,khd->qhd", weights.astype(bfloat), value_part, preferred_element_type=single
        )
        accumulated = accumulated * jnp.transpose(factor)[:, :, None] + update
        return ((new_max, totals, accumulated), None)

    result, unused = lax.scan(advance, initial, (shaped[0], shaped[1], offsets))
    row_max, totals, accumulated = result
    attended_full = accumulated / jnp.transpose(totals)[:, :, None]
    log_total = row_max + jnp.log(totals)
    attended = attended_full.astype(bfloat).reshape(row_count, H * HD)
    middle = inputs + jnp.dot(attended, out_weight, preferred_element_type=single)
    inverse_two = inverse_rms(middle)
    unit_two = middle * inverse_two
    normed_moe = (unit_two * gain_moe).astype(bfloat)
    shared_gate_v = jnp.dot(normed_moe, gate_shared, preferred_element_type=single)
    shared_up_v = jnp.dot(normed_moe, up_shared, preferred_element_type=single)
    shared_act, shared_slope = silu_parts(shared_gate_v)
    shared_mid = (shared_act * shared_up_v).astype(bfloat)
    shared_out = jnp.dot(shared_mid, down_shared, preferred_element_type=single)
    logits = jnp.dot(normed_moe, route_weight, preferred_element_type=single)
    route_probs = jax.nn.softmax(logits, axis=-1)
    onehot = (
        route_ids[:, :, None] == jnp.arange(expert_total, dtype=jnp.int32)[None, None, :]
    ).astype(single)
    chosen = jnp.einsum("tje,te->tj", onehot, route_probs)
    chosen_total = jnp.sum(chosen, axis=1, keepdims=True)
    gates = chosen / chosen_total
    slots = slots_of(route_ids, expert_total)
    destination = (route_ids * capacity + slots).reshape(-1)
    assign_count = row_count * TOP
    assignment = (
        jnp.full((expert_total * capacity,), assign_count, jnp.int32)
        .at[destination]
        .set(jnp.arange(assign_count, dtype=jnp.int32))
    )
    token_of_slot = jnp.where(assignment < assign_count, assignment // TOP, row_count)
    padded_rows = jnp.concatenate([normed_moe, jnp.zeros((1, model_width), bfloat)], axis=0)
    send_rows = padded_rows[token_of_slot].reshape(chain_length, EXP_DEV, capacity, model_width)
    received = lax.all_to_all(send_rows, "expert", split_axis=0, concat_axis=2, tiled=True)[0]
    gate_values = jnp.einsum("erd,edf->erf", received, gate_expert, preferred_element_type=single)
    up_values = jnp.einsum("erd,edf->erf", received, up_expert, preferred_element_type=single)
    expert_act, expert_slope = silu_parts(gate_values)
    expert_mid = (expert_act * up_values).astype(bfloat)
    expert_out = jnp.einsum(
        "erf,efd->erd", expert_mid, down_expert, preferred_element_type=single
    ).astype(bfloat)
    returned = lax.all_to_all(
        expert_out[None], "expert", split_axis=2, concat_axis=0, tiled=True
    ).reshape(expert_total * capacity, model_width)
    picked = returned[destination].reshape(row_count, TOP, model_width).astype(single)
    mixture = jnp.sum(gates[:, :, None] * picked, axis=1)
    output = (middle + shared_out + mixture).astype(bfloat)
    grad_out = cotangent[0].astype(single)
    grad_shared_out = grad_out.astype(bfloat)
    grad_shared_mid = jnp.einsum(
        "td,fd->tf", grad_shared_out, down_shared, preferred_element_type=single
    )
    grad_shared_gate_v = (grad_shared_mid * shared_up_v * shared_slope).astype(bfloat)
    grad_shared_up_v = (grad_shared_mid * shared_act).astype(bfloat)
    grad_down_shared = jnp.einsum(
        "tf,td->fd", shared_mid, grad_shared_out, preferred_element_type=single
    )
    grad_gate_shared = jnp.einsum(
        "td,tf->df", normed_moe, grad_shared_gate_v, preferred_element_type=single
    )
    grad_up_shared = jnp.einsum(
        "td,tf->df", normed_moe, grad_shared_up_v, preferred_element_type=single
    )
    grad_normed_moe = jnp.einsum(
        "tf,df->td", grad_shared_gate_v, gate_shared, preferred_element_type=single
    ) + jnp.einsum("tf,df->td", grad_shared_up_v, up_shared, preferred_element_type=single)
    grad_picked = (gates[:, :, None] * grad_out[:, None, :]).astype(bfloat)
    grad_gates = jnp.sum(picked * grad_out[:, None, :], axis=-1)
    padded_grads = jnp.concatenate(
        [grad_picked.reshape(assign_count, model_width), jnp.zeros((1, model_width), bfloat)],
        axis=0,
    )
    send_grads = padded_grads[assignment].reshape(chain_length, EXP_DEV, capacity, model_width)
    received_grads = lax.all_to_all(send_grads, "expert", split_axis=0, concat_axis=2, tiled=True)[
        0
    ]
    grad_expert_mid = jnp.einsum(
        "erd,efd->erf", received_grads, down_expert, preferred_element_type=single
    )
    grad_gate_values = (grad_expert_mid * up_values * expert_slope).astype(bfloat)
    grad_up_values = (grad_expert_mid * expert_act).astype(bfloat)
    grad_down_expert = jnp.einsum(
        "erf,erd->efd", expert_mid, received_grads, preferred_element_type=single
    )
    grad_gate_expert = jnp.einsum(
        "erd,erf->edf", received, grad_gate_values, preferred_element_type=single
    )
    grad_up_expert = jnp.einsum(
        "erd,erf->edf", received, grad_up_values, preferred_element_type=single
    )
    expert_sums = (
        lax.psum_scatter(
            grad_gate_expert.astype(jnp.bfloat16), "dp", scatter_dimension=1, tiled=True
        ).astype(jnp.float32),
        lax.psum_scatter(
            grad_up_expert.astype(jnp.bfloat16), "dp", scatter_dimension=1, tiled=True
        ).astype(jnp.float32),
        lax.psum_scatter(
            grad_down_expert.astype(jnp.bfloat16), "dp", scatter_dimension=2, tiled=True
        ).astype(jnp.float32),
    )
    grad_received = (
        jnp.einsum("erf,edf->erd", grad_gate_values, gate_expert, preferred_element_type=single)
        + jnp.einsum("erf,edf->erd", grad_up_values, up_expert, preferred_element_type=single)
    ).astype(bfloat)
    grad_returned = lax.all_to_all(
        grad_received[None], "expert", split_axis=2, concat_axis=0, tiled=True
    ).reshape(expert_total * capacity, model_width)
    grad_normed_moe = grad_normed_moe + jnp.sum(
        grad_returned[destination].reshape(row_count, TOP, model_width).astype(single), axis=1
    )
    grad_chosen = (grad_gates - jnp.sum(gates * grad_gates, axis=1, keepdims=True)) / chosen_total
    grad_probs = jnp.einsum("tje,tj->te", onehot, grad_chosen)
    grad_logits = (
        route_probs * (grad_probs - jnp.sum(route_probs * grad_probs, axis=1, keepdims=True))
    ).astype(bfloat)
    grad_route = jnp.einsum("td,te->de", normed_moe, grad_logits, preferred_element_type=single)
    grad_normed_moe = grad_normed_moe + jnp.einsum(
        "te,de->td", grad_logits, route_weight, preferred_element_type=single
    )
    grad_gain_moe = jnp.sum(grad_normed_moe * unit_two, axis=0)
    scaled_two = grad_normed_moe * gain_moe
    grad_middle = grad_out + inverse_two * (
        scaled_two - unit_two * jnp.mean(scaled_two * unit_two, axis=-1, keepdims=True)
    )
    grad_attn = grad_middle.astype(bfloat)
    grad_out_weight = jnp.einsum("tc,td->cd", attended, grad_attn, preferred_element_type=single)
    grad_attended = (
        jnp.einsum("td,cd->tc", grad_attn, out_weight, preferred_element_type=single)
        .astype(bfloat)
        .reshape(row_count, H, HD)
    )
    delta = jnp.transpose(jnp.sum(grad_attended.astype(single) * attended_full, axis=-1))
    all_log_total, all_delta = (
        lax.all_gather(log_total, "expert", axis=1, tiled=True),
        lax.all_gather(delta, "expert", axis=1, tiled=True),
    )
    zero_rows = jnp.zeros((row_count, H, HD), single)
    shaped, offsets = split_blocks(
        (
            lax.all_gather(key_rows, "expert", axis=0, tiled=True),
            lax.all_gather(value_rows, "expert", axis=0, tiled=True),
        )
    )

    def advance(carried, inputs_block):
        key_part, value_part, offset = inputs_block
        scores, allowed = masked_scores(queries, segment, places, key_part, offset)
        weights = jnp.where(allowed, jnp.exp(scores - log_total[:, :, None]), 0.0)
        grad_weights = jnp.einsum(
            "qhd,khd->hqk", grad_attended, value_part, preferred_element_type=single
        )
        grad_scores = (weights * (grad_weights - delta[:, :, None]) * score_scale).astype(bfloat)
        return (
            carried
            + jnp.einsum("hqk,khd->qhd", grad_scores, key_part, preferred_element_type=single),
            None,
        )

    result, unused = lax.scan(advance, zero_rows, (shaped[0], shaped[1], offsets))
    grad_queries = result
    shaped, offsets = split_blocks(
        (
            lax.all_gather(queries, "expert", axis=0, tiled=True),
            lax.all_gather(grad_attended, "expert", axis=0, tiled=True),
        )
    )

    def advance(carried, inputs_block):
        grad_keys, grad_values = carried
        query_part, grad_part, offset = inputs_block
        block_size = query_part.shape[0]
        query_place = offset + jnp.arange(block_size, dtype=jnp.int32)
        query_seg, unused = segments(doc_lengths, query_place)
        scores, allowed = masked_scores(query_part, query_seg, query_place, key_rows, own_first)
        part_log = lax.dynamic_slice_in_dim(all_log_total, offset, block_size, 1)
        part_delta = lax.dynamic_slice_in_dim(all_delta, offset, block_size, 1)
        weights = jnp.where(allowed, jnp.exp(scores - part_log[:, :, None]), 0.0)
        grad_values = grad_values + jnp.einsum(
            "hqk,qhd->khd", weights.astype(bfloat), grad_part, preferred_element_type=single
        )
        grad_weights = jnp.einsum(
            "qhd,khd->hqk", grad_part, value_rows, preferred_element_type=single
        )
        grad_scores = (weights * (grad_weights - part_delta[:, :, None]) * score_scale).astype(
            bfloat
        )
        grad_keys = grad_keys + jnp.einsum(
            "hqk,qhd->khd", grad_scores, query_part, preferred_element_type=single
        )
        return ((grad_keys, grad_values), None)

    result, unused = lax.scan(advance, (zero_rows, zero_rows), (shaped[0], shaped[1], offsets))
    grad_keys, grad_values = result
    grad_projected = (
        jnp.stack(
            [rotate(grad_queries, rope_pos, -1.0), rotate(grad_keys, rope_pos, -1.0), grad_values],
            axis=1,
        )
        .astype(bfloat)
        .reshape(row_count, 3 * H * HD)
    )
    grad_qkv = jnp.einsum("td,tc->dc", normed, grad_projected, preferred_element_type=single)
    grad_normed_one = jnp.einsum(
        "tc,dc->td", grad_projected, qkv_weight, preferred_element_type=single
    )
    grad_gain_attn = jnp.sum(grad_normed_one * unit_one, axis=0)
    scaled_one = grad_normed_one * gain_attn
    grad_inputs = grad_middle + inverse_one * (
        scaled_one - unit_one * jnp.mean(scaled_one * unit_one, axis=-1, keepdims=True)
    )
    grad_gain_pair = jnp.stack([grad_gain_attn, grad_gain_moe], axis=0)
    dense_outs = (
        lax.psum_scatter(grad_qkv, ("dp", "expert"), scatter_dimension=0, tiled=True),
        lax.psum_scatter(grad_out_weight, ("dp", "expert"), scatter_dimension=1, tiled=True),
        lax.psum_scatter(grad_gate_shared, ("dp", "expert"), scatter_dimension=0, tiled=True),
        lax.psum_scatter(grad_up_shared, ("dp", "expert"), scatter_dimension=0, tiled=True),
        lax.psum_scatter(grad_down_shared, ("dp", "expert"), scatter_dimension=1, tiled=True),
        lax.psum_scatter(grad_route, ("dp", "expert"), scatter_dimension=0, tiled=True),
        lax.psum_scatter(grad_gain_pair, ("dp", "expert"), scatter_dimension=1, tiled=True),
    )
    return (
        output[None],
        grad_inputs.astype(bfloat)[None],
        dense_outs[0],
        dense_outs[1],
        dense_outs[2],
        dense_outs[3],
        dense_outs[4],
        dense_outs[5],
        dense_outs[6],
        expert_sums[0],
        expert_sums[1],
        expert_sums[2],
    )


def solution(mesh):
    in_specs = (
        P("dp", "expert", None),
        P("dp", "expert", None),
        P("dp", None),
        P("dp", "expert", None),
        P(("dp", "expert"), None),
        P(None, ("dp", "expert")),
        P(("dp", "expert"), None),
        P(("dp", "expert"), None),
        P(None, ("dp", "expert")),
        P(("dp", "expert"), None),
        P(None, ("dp", "expert")),
        P("expert", "dp", None),
        P("expert", "dp", None),
        P("expert", None, "dp"),
    )
    out_specs = (
        P("dp", "expert", None),
        P("dp", "expert", None),
        P(("dp", "expert"), None),
        P(None, ("dp", "expert")),
        P(("dp", "expert"), None),
        P(("dp", "expert"), None),
        P(None, ("dp", "expert")),
        P(("dp", "expert"), None),
        P(None, ("dp", "expert")),
        P("expert", "dp", None),
        P("expert", "dp", None),
        P("expert", None, "dp"),
    )
    return jax.shard_map(local, mesh=mesh, in_specs=in_specs, out_specs=out_specs, check_vma=False)
```

profile of v0, /device:TPU:0, one launch (start us, length us, event | category | flops | bytes accessed | tf_op | source)
XLA Modules:
  0.0 2054.9 jit_solution(17334526835817032026)
XLA Ops:
  11.2 43.1 %all-gather.1 = bf16[32,40,2]{1,2,0:T(2,128)(2,1)S(1)} all-gather(bf16[1,40,2]{1,2,0:T(2,128)(2,1)S(1)} %convert_bitcast_fusion.2), channel_id=1, replica_groups=mesh['dp'=4,'expert'=8] {'dp','expert'}, dimensions={0}, use_global_device_ids=true | all-gather | bytes 5280 | tf_op jit(solution)/shard_map/all_gather | solution.py:114
  58.9 39.4 %all-gather.18.cloned.1.call-done = bf16[1280,3840]{1,0:T(8,128)(2,1)} async-done(((bf16[40,3840]{1,0:T(8,128)(2,1)}), bf16[1280,3840]{1,0:T(8,128)(2,1)}) %all-gather.18.cloned.1.call-update) | async-done | bytes 9830416 | tf_op jit(solution)/shard_map/all_gather | solution.py:108
  98.2 13.8 copy.117
  128.1 40.8 %all-gather.2 = bf16[32,40,16]{1,2,0:T(8,128)(2,1)S(1)} all-gather(bf16[1,40,16]{1,2,0:T(8,128)(2,1)S(1)} %convert_bitcast_fusion.1), channel_id=1, replica_groups=mesh['dp'=4,'expert'=8] {'dp','expert'}, dimensions={0}, use_global_device_ids=true | all-gather | bytes 42240 | tf_op jit(solution)/shard_map/all_gather | solution.py:113
  200.8 11.5 all-gather.40.cloned.1.call-done
  216.8 38.0 %while.45 = (s32[]{:T(128)}, f32[10,192]{1,0:T(8,128)S(1)}, f32[10,192]{1,0:T(8,128)S(1)}, f32[192,10,128]{2,0,1:T(8,128)S(1)}, s32[192]{0:T(256)S(1)}, /*index=...) while((s32[]{:T(128)}, f32[10,192]{1,0:T(8,128)S(1)}, ...), condition=%wide.region_8.9_spmd.clone, body=%wide.region_4.8_spmd.clone.sunk | while | flops 517148096 | bytes 33138136 | solution.py:175
  258.6 15.4 all-gather.22.cloned.1.call-done
  306.3 100.6 %all-to-all-done.2 = bf16[8,2,120,1280]{3,2,1,0:T(8,128)(2,1)} async-done(((bf16[8,2,120,1280]{3,2,1,0:T(8,128)(2,1)}), bf16[8,2,120,1280]{3,2,1,0:T(8,128)(2,1)}, u32[]{:S(2)}, u32[]{:S(2)}) %all-to-all-start.2) | async-done | bytes 4915232 | tf_op jit(solution)/shard_map/all_to_all | solution.py:248
  418.7 106.9 %all-to-all-done = bf16[8,2,120,1280]{3,2,1,0:T(8,128)(2,1)} async-done(((bf16[8,2,120,1280]{3,2,1,0:T(8,128)(2,1)}), bf16[8,2,120,1280]{3,2,1,0:T(8,128)(2,1)}, u32[]{:S(2)}, u32[]{:S(2)}) %all-to-all-start) | async-done | bytes 4915232 | tf_op jit(solution)/shard_map/all_to_all | solution.py:208
  530.6 10.3 fusion.150
  540.8 10.3 fusion.151
  551.2 14.3 multiply_convert_fusion.1
  617.7 96.2 %all-to-all-done.1 = bf16[1,2,960,1280]{3,1,0,2:T(2,128)(2,1)} async-done(((bf16[1,2,960,1280]{3,1,0,2:T(2,128)(2,1)}), bf16[1,2,960,1280]{3,1,0,2:T(2,128)(2,1)}, u32[]{:S(2)}, u32[]{:S(2)}) %all-to-all-start.1) | async-done | bytes 4915232 | tf_op jit(solution)/shard_map/all_to_all | solution.py:216
  743.8 12.3 gather_fusion.1
  770.1 93.9 %all-to-all-done.3 = bf16[1,2,960,1280]{3,1,0,2:T(2,128)(2,1)} async-done(((bf16[1,2,960,1280]{3,1,0,2:T(2,128)(2,1)}), bf16[1,2,960,1280]{3,1,0,2:T(2,128)(2,1)}, u32[]{:S(2)}, u32[]{:S(2)}) %all-to-all-start.3) | async-done | bytes 4915232 | tf_op jit(solution)/shard_map/all_to_all | solution.py:280
  869.3 11.9 gather_fusion.3
  905.9 10.2 convolution_convert_fusion.1
  926.2 10.1 convolution_convert_fusion.2
  949.7 14.0 all-gather.3
  965.4 14.2 all-gather.4
  986.2 40.7 %while.46 = (s32[]{:T(128)}, f32[192,10,128]{2,0,1:T(8,128)}, bf16[3,512,10,128]{3,1,2,0:T(8,128)(2,1)}, s32[192]{0:T(256)S(1)}, s32[3]{0:T(128)S(1)}, /*index=5...) while((s32[]{:T(128)}, f32[192,10,128]{2,0,1:T(8,128)}, ...), condition=%wide.region_26.27_spmd.clone, body=%wide.region_24.26_spmd.clone.sunk | while | flops 763633856 | bytes 14975939 | solution.py:334
  1027.0 66.3 %while.47 = (s32[]{:T(128)}, f32[192,10,128]{2,0,1:T(8,128)}, f32[192,10,128]{2,0,1:T(8,128)}, bf16[3,512,10,128]{3,1,0,2:T(8,128)(2,1)}, s32[3]{0:T(128)S(1)}, ...) while((s32[]{:T(128)}, f32[192,10,128]{2,0,1:T(8,128)}, ...), condition=%wide.region_30.31_spmd.clone, body=%wide.region_27.30_spmd.clone.sunk | while | flops 1020701696 | bytes 22414856 | solution.py:367
  1101.9 10.3 fusion.121
  1117.2 15.8 reduce-scatter.28.cloned.1.call-done
  1135.7 56.1 %reduce-scatter.24.cloned.1.call-done = bf16[2,320,896]{2,1,0:T(8,128)(2,1)} async-done(((bf16[2,1280,896]{2,1,0:T(8,128)(2,1)}), bf16[2,320,896]{2,1,0:T(8,128)(2,1)}) %reduce-scatter.24.cloned.1.call-update) | async-done | bytes 1146896 | tf_op jit(solution)/shard_map/reduce_scatter | solution.py:266
  1194.6 56.1 %reduce-scatter.26.cloned.1.call-done = bf16[2,320,896]{2,1,0:T(8,128)(2,1)} async-done(((bf16[2,1280,896]{2,1,0:T(8,128)(2,1)}), bf16[2,320,896]{2,1,0:T(8,128)(2,1)}) %reduce-scatter.26.cloned.1.call-update) | async-done | bytes 1146896 | tf_op jit(solution)/shard_map/reduce_scatter | solution.py:269
  1261.4 40.2 %all-reduce.7 = f32[2,1280]{1,0:T(2,128)S(1)} all-reduce(f32[2,1280]{1,0:T(2,128)S(1)} %pad_maximum_fusion.2), channel_id=9, replica_groups=mesh['dp'=4,'expert'=8] {'dp','expert'}, use_global_device_ids=true, to_apply=%region_40.41.clone | all-reduce | flops 2560 | bytes 20480
  1303.3 94.0 %reduce-scatter.30.cloned.1.call-done = f32[40,896]{1,0:T(8,128)} async-done(((f32[1280,896]{1,0:T(8,128)}), f32[40,896]{1,0:T(8,128)}) %reduce-scatter.30.cloned.1.call-update) | async-done | bytes 143376
  1397.3 143.3 %reduce-scatter.32.cloned.1.call-done = f32[40,896]{1,0:T(8,128)} async-done(((f32[1280,896]{1,0:T(8,128)}), f32[40,896]{1,0:T(8,128)}) %reduce-scatter.32.cloned.1.call-update) | async-done | bytes 143376
  1540.6 143.6 %reduce-scatter.34.cloned.1.call-done = f32[896,40]{0,1:T(8,128)} async-done(((f32[896,1280]{0,1:T(8,128)}), f32[896,40]{0,1:T(8,128)}) %reduce-scatter.34.cloned.1.call-update) | async-done | bytes 143376
  1684.1 147.2 %reduce-scatter.22.cloned.1.call-done = f32[1280,40]{0,1:T(8,128)} async-done(((f32[1280,1280]{0,1:T(8,128)}), f32[1280,40]{0,1:T(8,128)}) %reduce-scatter.22.cloned.1.call-update) | async-done | bytes 204816 | tf_op jit(solution)/shard_map/reduce_scatter | solution.py:389
  1831.3 216.3 %reduce-scatter.20.cloned.1.call-done = f32[40,3840]{1,0:T(8,128)} async-done(((f32[1280,3840]{1,0:T(8,128)}), f32[40,3840]{1,0:T(8,128)}) %reduce-scatter.20.cloned.1.call-update) | async-done | bytes 614416 | tf_op jit(solution)/shard_map/reduce_scatter | solution.py:388
  (464 shorter events, 441.0 us)
Async XLA Ops:
  7.2 91.1 %all-gather.18.cloned.1.call-start = ((), (), s32[]{:S(2)}) async-start(), calls=%async_computation.12 | async-start | bytes 10137600 | tf_op jit(solution)/shard_map/all_gather | solution.py:108
  9.1 187.3 %all-gather.20.cloned.1.call-start = ((), (), s32[]{:S(2)}) async-start(), calls=%async_computation.13 | async-start | bytes 4423680 | tf_op jit(solution)/shard_map/all_gather | solution.py:156
  55.0 57.0 %copy-start.48 = (f32[1280]{0:T(1024)}, f32[1280]{0:T(1024)S(1)}, u32[]{:S(2)}) copy-start(f32[1280]{0:T(1024)S(1)} %get-tuple-element.726) | copy-start | bytes 15364
  58.9 59.4 %copy-start.36 = (f32[192,64]{1,0:T(8,128)}, f32[192,64]{1,0:T(8,128)S(1)}, u32[]{:S(2)}) copy-start(f32[192,64]{1,0:T(8,128)S(1)} %get-tuple-element.827) | copy-start | bytes 147460
  121.7 90.6 %all-gather.40.cloned.1.call-start = ((), (), s32[]{:S(2)}) async-start(), calls=%async_computation.28 | async-start | bytes 4423680 | tf_op jit(solution)/shard_map/all_gather | solution.py:157
  122.7 151.3 %all-gather.22.cloned.1.call-start = ((), (), s32[]{:S(2)}) async-start(), calls=%async_computation.14 | async-start | bytes 3379200 | tf_op jit(solution)/shard_map/all_gather | solution.py:109
  124.4 406.2 %all-gather.30.cloned.1.call-start = ((), (), s32[]{:S(2)}) async-start(), calls=%async_computation.18 | async-start | bytes 5734400 | tf_op jit(solution)/shard_map/all_gather | solution.py:117
  128.1 151.3 %copy-start.40 = (s32[1,192,7]{2,1,0:T(8,128)}, s32[1,192,7]{2,1,0:T(8,128)S(1)}, u32[]{:S(2)}) copy-start(s32[1,192,7]{2,1,0:T(8,128)S(1)} %copy.146) | copy-start | bytes 16132
  169.1 108.3 %copy-start.44 = (bf16[1280,16]{0,1:T(8,128)(2,1)}, bf16[1280,16]{0,1:T(8,128)(2,1)S(1)}, u32[]{:S(2)}) copy-start(bf16[1280,16]{0,1:T(8,128)(2,1)S(1)} %reshape.632) | copy-start | bytes 122884
  292.7 114.2 %all-to-all-start.2 = ((bf16[8,2,120,1280]{3,2,1,0:T(8,128)(2,1)}), bf16[8,2,120,1280]{3,2,1,0:T(8,128)(2,1)}, u32[]{:S(2)}, u32[]{:S(2)}) async-start(bf16[8,2,120,1280]{3,2,1,0:T(8,128)(2,1)} %bitcast.375), calls=%async_computation.2 | async-start | bytes 9830400 | tf_op jit(solution)/shard_map/all_to_all | solution.py:248
  297.5 243.4 %all-gather.32.cloned.1.call-start = ((), (), s32[]{:S(2)}) async-start(), calls=%async_computation.19 | async-start | bytes 5734400 | tf_op jit(solution)/shard_map/all_gather | solution.py:118
  406.9 118.8 %all-to-all-start = ((bf16[8,2,120,1280]{3,2,1,0:T(8,128)(2,1)}), bf16[8,2,120,1280]{3,2,1,0:T(8,128)(2,1)}, u32[]{:S(2)}, u32[]{:S(2)}) async-start(bf16[8,2,120,1280]{3,2,1,0:T(8,128)(2,1)} %bitcast.374), calls=%async_computation | async-start | bytes 9830400 | tf_op jit(solution)/shard_map/all_to_all | solution.py:208
  411.7 139.5 %all-gather.34.cloned.1.call-start = ((), (), s32[]{:S(2)}) async-start(), calls=%async_computation.20 | async-start | bytes 5734400 | tf_op jit(solution)/shard_map/all_gather | solution.py:119
  412.9 306.6 %all-gather.24.cloned.1.call-start = ((), (), s32[]{:S(2)}) async-start(), calls=%async_computation.15 | async-start | bytes 2365440 | tf_op jit(solution)/shard_map/all_gather | solution.py:110
  584.3 129.7 %all-to-all-start.1 = ((bf16[1,2,960,1280]{3,1,0,2:T(2,128)(2,1)}), bf16[1,2,960,1280]{3,1,0,2:T(2,128)(2,1)}, u32[]{:S(2)}, u32[]{:S(2)}) async-start(bf16[1,2,960,1280]{3,1,0,2:T(2,128)(2,1)} %copy.126), calls=%async_computation.1 | async-start | bytes 9830400 | tf_op jit(solution)/shard_map/all_to_all | solution.py:216
  589.1 132.8 %all-gather.26.cloned.1.call-start = ((), (), s32[]{:S(2)}) async-start(), calls=%async_computation.16 | async-start | bytes 2365440 | tf_op jit(solution)/shard_map/all_gather | solution.py:111
  589.8 144.5 %all-gather.28.cloned.1.call-start = ((), (), s32[]{:S(2)}) async-start(), calls=%async_computation.17 | async-start | bytes 2365440 | tf_op jit(solution)/shard_map/all_gather | solution.py:112
  617.7 101.7 %copy-start.58 = (s32[1344]{0:T(1024)S(1)}, s32[1344]{0:T(1024)}, u32[]{:S(2)}) copy-start(s32[1344]{0:T(1024)} %copy-done.57) | copy-start | bytes 16132
  714.0 150.0 %all-to-all-start.3 = ((bf16[1,2,960,1280]{3,1,0,2:T(2,128)(2,1)}), bf16[1,2,960,1280]{3,1,0,2:T(2,128)(2,1)}, u32[]{:S(2)}, u32[]{:S(2)}) async-start(bf16[1,2,960,1280]{3,1,0,2:T(2,128)(2,1)} %copy.129), calls=%async_computation.3 | async-start | bytes 9830400 | tf_op jit(solution)/shard_map/all_to_all | solution.py:280
  718.6 308.3 %all-gather.36.cloned.1.call-start = ((), (), s32[]{:S(2)}) async-start(), calls=%async_computation.21 | async-start | bytes 4423680 | tf_op jit(solution)/shard_map/all_gather | solution.py:338
  719.4 307.6 %all-gather.38.cloned.1.call-start = ((), (), s32[]{:S(2)}) async-start(), calls=%async_computation.22 | async-start | bytes 4423680 | tf_op jit(solution)/shard_map/all_gather | solution.py:339
  904.9 210.9 %all-reduce.10.cloned.1.call-start = ((), (), s32[]{:S(2)}) async-start(), calls=%async_computation.29 | async-start | bytes 163840
  905.8 227.1 %reduce-scatter.28.cloned.1.call-start = ((), (), s32[]{:S(2)}) async-start(), calls=%async_computation.27 | async-start | bytes 5734400 | tf_op jit(solution)/shard_map/reduce_scatter | solution.py:272
  916.0 275.8 %reduce-scatter.24.cloned.1.call-start = ((), (), s32[]{:S(2)}) async-start(), calls=%async_computation.25 | async-start | bytes 5734400 | tf_op jit(solution)/shard_map/reduce_scatter | solution.py:266
  926.1 324.6 %reduce-scatter.26.cloned.1.call-start = ((), (), s32[]{:S(2)}) async-start(), calls=%async_computation.26 | async-start | bytes 5734400 | tf_op jit(solution)/shard_map/reduce_scatter | solution.py:269
  936.3 461.0 %reduce-scatter.30.cloned.1.call-start = ((), (), s32[]{:S(2)}) async-start(), calls=%async_computation.30 | async-start | bytes 4730880
  940.3 600.3 %reduce-scatter.32.cloned.1.call-start = ((), (), s32[]{:S(2)}) async-start(), calls=%async_computation.31 | async-start | bytes 4730880
  944.3 739.8 %reduce-scatter.34.cloned.1.call-start = ((), (), s32[]{:S(2)}) async-start(), calls=%async_computation.32 | async-start | bytes 4730880
  947.5 883.9 %reduce-scatter.22.cloned.1.call-start = ((), (), s32[]{:S(2)}) async-start(), calls=%async_computation.24 | async-start | bytes 6758400 | tf_op jit(solution)/shard_map/reduce_scatter | solution.py:389
  985.2 1062.4 %reduce-scatter.20.cloned.1.call-start = ((), (), s32[]{:S(2)}) async-start(), calls=%async_computation.23 | async-start | bytes 20275200 | tf_op jit(solution)/shard_map/reduce_scatter | solution.py:388
  1026.9 66.3 %copy-start.37 = (f32[192,64]{1,0:T(8,128)S(1)}, f32[192,64]{1,0:T(8,128)}, u32[]{:S(2)}) copy-start(f32[192,64]{1,0:T(8,128)} %copy-done.36) | copy-start | bytes 147460
  1027.0 66.3 %copy-start.42 = (f32[192,64]{1,0:T(8,128)S(1)}, f32[192,64]{1,0:T(8,128)}, u32[]{:S(2)}) copy-start(f32[192,64]{1,0:T(8,128)} %get-tuple-element.825) | copy-start | bytes 147460
  (73 other events, 603.5 us)
Sparse Core Ops, SparseCore 0:
  11.6 86.5 all-gather.17
  121.9 44.7 all-gather.19
  168.8 43.4 all-gather.39
  215.6 58.3 all-gather.21
  276.2 54.8 all-gather.29
  333.4 55.9 all-gather.31
  414.4 56.3 all-gather.33
  474.2 70.0 all-gather.23
  593.3 63.2 all-gather.25
  659.9 74.3 all-gather.27
  736.5 108.5 all-gather.35
  905.0 43.0 all-gather.37
  953.7 118.2 all-reduce.9
  1075.0 57.9 reduce-scatter.27
  1135.9 55.9 reduce-scatter.23
  1194.8 55.9 reduce-scatter.25
  1253.4 143.7 reduce-scatter.29
  1400.0 140.5 reduce-scatter.31
  1543.4 140.6 reduce-scatter.33
  1686.9 144.4 reduce-scatter.21
  1838.3 209.2 reduce-scatter.19
where the time goes:
time: 2060 us; the launch traced here: 2050 us
  waiting for transfers between devices  1350 us (66%)
  matrix products  252 us (12%)
  local copies, waits for them, and re-layouts  176 us (9%)
  blocking collectives  152 us (7%)
  other arithmetic  85.1 us (4%)
    unnamed x25, waiting for transfers between devices  382 us
    reduce_scatter x1, waiting for transfers between devices, local(): lax.psum_scatter(grad_qkv, ('dp', 'expert'), scatter_dimension=0, tiled=T...  216 us
    reduce_scatter x1, waiting for transfers between devices, local(): lax.psum_scatter(grad_out_weight, ('dp', 'expert'), scatter_dimension=1,...  147 us
    all_to_all x1, waiting for transfers between devices, local(): lax.all_to_all(send_rows, 'expert', split_axis=0, concat_axis=2, tiled=True)  107 us
    all_to_all x1, waiting for transfers between devices, local(): lax.all_to_all(send_grads, 'expert', split_axis=0, concat_axis=2, tiled=T...  101 us
    all_to_all x1, waiting for transfers between devices, local(): lax.all_to_all(expert_out[None], 'expert', split_axis=2, concat_axis=0, t...  96.2 us
    all_to_all x1, waiting for transfers between devices, local(): lax.all_to_all(grad_received[None], 'expert', split_axis=2, concat_axis=0...  93.9 us
    reduce_scatter x1, waiting for transfers between devices, local(): lax.psum_scatter(grad_up_expert.astype(jnp.bfloat16), 'dp', scatter_dimen...  56.1 us
  transfers between devices with their start and end apart: 25, of which 16 were waited for; matrix products, arithmetic and copies ran while one was open for 23% of the time, Pallas kernels for 0%

commit v1 on v0

v1 whole, which is shorter than its diff:
```python
import functools

import jax
import jax.numpy as jnp
from jax import lax
from jax.experimental import pallas as pl
from jax.experimental.pallas import tpu as pltpu
from jax.sharding import PartitionSpec as P

H = 10
HD = 128
TOP = 7
EXP_DEV = 2
EPS = 1e-06
NEG = -1e30
BF = jnp.bfloat16
F32 = jnp.float32
VMEM_LIMIT = 56 * 1024 * 1024


def params(**kw):
    return pltpu.CompilerParams(vmem_limit_bytes=VMEM_LIMIT, **kw)


def nn(a, b):
    return jnp.dot(a, b, preferred_element_type=F32)


def nt(a, b):
    return lax.dot_general(a, b, (((1,), (1,)), ((), ())), preferred_element_type=F32)


def tn(a, b):
    return lax.dot_general(a, b, (((0,), (0,)), ((), ())), preferred_element_type=F32)


def doc_starts_of(lengths, places):
    doc_ends = jnp.cumsum(lengths)
    doc_starts = doc_ends - lengths
    total = doc_ends[-1]
    doc_index = jnp.sum((places[:, None] >= doc_ends[None, :]).astype(jnp.int32), axis=1)
    live = places < total
    matches = doc_index[:, None] == jnp.arange(lengths.shape[0], dtype=jnp.int32)[None, :]
    first = jnp.sum(jnp.where(matches, doc_starts[None, :], 0), axis=1)
    return jnp.where(live, first, places), places - jnp.where(live, first, total)


def turn_tables(rope_pos):
    half = HD // 2
    frequency = 10000.0 ** (-jnp.arange(half, dtype=F32) / half)
    angles = rope_pos.astype(F32)[:, None] * frequency[None, :]
    cosine = jnp.cos(angles)
    sine = jnp.sin(angles)
    return (
        jnp.concatenate([cosine, cosine], axis=1),
        jnp.concatenate([-sine, sine], axis=1),
    )


def inverse_rms(values):
    return lax.rsqrt(jnp.mean(values * values, axis=-1, keepdims=True) + EPS)


MESH = pl.DeviceIdType.MESH


def sent(src, dst, send_sem, recv_sem, device):
    return pltpu.make_async_remote_copy(
        src_ref=src,
        dst_ref=dst,
        send_sem=send_sem,
        recv_sem=recv_sem,
        device_id=device,
        device_id_type=MESH,
    )


class Place:
    def __init__(self, chips):
        self.d = lax.axis_index("dp")
        self.e = lax.axis_index("expert")
        self.z = self.e // 2
        self.c = self.e % 2
        self.y = self.d // 2
        self.x = self.d % 2
        self.chips = chips
        self.sibling = (self.d, self.e + 1 - 2 * self.c)
        self.across_x = (self.d + 1 - 2 * self.x, self.e)
        self.across_y = (self.d + 2 - 4 * self.y, self.e)
        self.up = (self.d, self.e + 2)
        self.down = (self.d, self.e - 2)


def greet(devices, conditions):
    barrier = pltpu.get_barrier_semaphore()
    count = 0
    for device, condition in zip(devices, conditions):
        if condition is None:
            pl.semaphore_signal(barrier, inc=1, device_id=device, device_id_type=MESH)
            count = count + 1
        else:

            @pl.when(condition)
            def _(device=device):
                pl.semaphore_signal(barrier, inc=1, device_id=device, device_id_type=MESH)

            count = count + condition.astype(jnp.int32)
    pl.semaphore_wait(barrier, count)


def gather_kernel(chips, n_full, n_chain, *refs):
    n = n_full + n_chain
    ins, outs, sems = refs[:n], refs[n : 2 * n], refs[2 * n :]
    at = Place(chips)
    chain = 2 * chips
    z, c = at.z, at.c
    has_up, has_down = z < chips - 1, z > 0
    devices = [at.sibling, at.up, at.down]
    conditions = [None, has_up, has_down]
    if n_full:
        devices += [at.across_x, at.across_y]
        conditions += [None, None]
    greet(devices, conditions)
    x_dp, y_dp = at.across_x[0], at.across_y[0]
    far_dp = 3 - at.d

    class Array:
        pass

    arrays = []
    position = 0
    for i in range(n):
        a = Array()
        a.full = i < n_full
        a.own, a.out = ins[i], outs[i]
        a.local, a.s_chain, a.r_chain, a.s_core, a.r_core = sems[position : position + 5]
        position += 5
        if a.full:
            a.s_side, a.r_side, a.s_half, a.r_half = sems[position : position + 4]
            position += 4
            half = a.own.shape[-1] // 2
            a.halves = (pl.ds(0, half), pl.ds(half, half))
        arrays.append(a)

    def slot(a, dd, zz, cc):
        return a.out.at[dd * chain + 2 * zz + cc] if a.full else a.out.at[2 * zz + cc]

    def core_index(a, dd, zz):
        return dd * chips + zz if a.full else zz

    def to_core(a, dd, zz, src=None):
        ref = slot(a, dd, zz, c)
        k = core_index(a, dd, zz)
        return sent(ref if src is None else src, ref, a.s_core.at[k], a.r_core.at[k], at.sibling)

    def from_core(a, dd, zz):
        ref = slot(a, dd, zz, 1 - c)
        k = core_index(a, dd, zz)
        return sent(ref, ref, a.s_core.at[k], a.r_core.at[k], at.sibling)

    def along(a, zz, direction, src=None):
        ref = slot(a, at.d, zz, c)
        device = at.up if direction == 0 else at.down
        return sent(ref if src is None else src, ref, a.s_chain.at[direction, zz], a.r_chain.at[zz], device)

    def side(a, dd, zz, axis, src=None):
        ref = slot(a, dd, zz, c)
        device = at.across_x if axis == 0 else at.across_y
        return sent(
            ref if src is None else src, ref, a.s_side.at[axis, zz], a.r_side.at[axis, zz], device
        )

    def half(a, dd, zz, which):
        ref = slot(a, dd, zz, c).at[:, a.halves[which]]
        device = at.across_y if which == 0 else at.across_x
        return sent(ref, ref, a.s_half.at[which, zz], a.r_half.at[which, zz], device)

    def present(zz):
        return (zz >= 0) & (zz < chips)

    def block_here(zz, distance, direction):
        for a in arrays:
            along(a, zz, direction).wait_recv()
            if direction == 0:

                @pl.when(has_up)
                def _(a=a):
                    along(a, zz, 0).start()
            else:

                @pl.when(has_down)
                def _(a=a):
                    along(a, zz, 1).start()

            if a.full:
                side(a, at.d, zz, 0).start()
                side(a, at.d, zz, 1).start()
            to_core(a, at.d, zz).start()

    def side_here(zz):
        for a in arrays[:n_full]:
            side(a, x_dp, zz, 0).wait_recv()
            half(a, x_dp, zz, 0).start()
            to_core(a, x_dp, zz).start()
            side(a, y_dp, zz, 1).wait_recv()
            half(a, y_dp, zz, 1).start()
            to_core(a, y_dp, zz).start()

    def far_here(zz):
        for a in arrays[:n_full]:
            half(a, far_dp, zz, 0).wait_recv()
            half(a, far_dp, zz, 1).wait_recv()
            to_core(a, far_dp, zz).start()

    for a in arrays:

        @pl.when(has_up)
        def _(a=a):
            along(a, z, 0, a.own).start()

        @pl.when(has_down)
        def _(a=a):
            along(a, z, 1, a.own).start()

        if a.full:
            side(a, at.d, z, 0, a.own).start()
            side(a, at.d, z, 1, a.own).start()
        to_core(a, at.d, z, a.own).start()
    for a in arrays:
        pltpu.make_async_copy(a.own, slot(a, at.d, z, c), a.local).start()

    def at_distance(k, fn):
        @pl.when((k >= 0) & present(z - k))
        def _():
            fn(z - k)

        @pl.when((k >= 1) & present(z + k))
        def _():
            fn(z + k)

    def step(k, carry):
        @pl.when(present(z - k))
        def _():
            block_here(z - k, k, 0)

        @pl.when(present(z + k))
        def _():
            block_here(z + k, k, 1)

        if n_full:
            at_distance(k - 1, side_here)
            at_distance(k - 2, far_here)
        return carry

    lax.fori_loop(1, chips + (2 if n_full else 0), step, 0)

    def finish(zz, carry):
        for a in arrays:
            for dd in range(4) if a.full else (0,):
                from_core(a, dd, zz).wait_recv()
                to_core(a, dd, zz).wait_send()

            @pl.when((zz <= z) & has_up)
            def _(a=a):
                along(a, zz, 0).wait_send()

            @pl.when((zz >= z) & has_down)
            def _(a=a):
                along(a, zz, 1).wait_send()

            if a.full:
                for axis in (0, 1):
                    side(a, at.d, zz, axis).wait_send()
                half(a, x_dp, zz, 0).wait_send()
                half(a, y_dp, zz, 1).wait_send()
        return carry

    lax.fori_loop(0, chips, finish, 0)
    for a in arrays:
        pltpu.make_async_copy(a.own, slot(a, at.d, z, c), a.local).wait()


def gather(full, chained, collective_id):
    chain = lax.axis_size("expert")
    chips = chain // 2
    spread = lax.axis_size("dp")
    assert spread == 4 and chain % 2 == 0
    dma = pltpu.SemaphoreType.DMA
    scratch = []
    for array in full:
        scratch += [dma, dma((2, chips)), dma((chips,)), dma((4 * chips,)), dma((4 * chips,))]
        scratch += [dma((2, chips))] * 4
    for array in chained:
        scratch += [dma, dma((2, chips)), dma((chips,)), dma((chips,)), dma((chips,))]
    shapes = [jax.ShapeDtypeStruct((spread * chain,) + a.shape, a.dtype) for a in full]
    shapes += [jax.ShapeDtypeStruct((chain,) + a.shape, a.dtype) for a in chained]
    n = len(full) + len(chained)
    moved = sum(s.size * s.dtype.itemsize for s in shapes)
    return pl.pallas_call(
        functools.partial(gather_kernel, chips, len(full), len(chained)),
        out_shape=shapes,
        in_specs=[pl.BlockSpec(memory_space=pl.ANY)] * n,
        out_specs=[pl.BlockSpec(memory_space=pl.ANY)] * n,
        scratch_shapes=scratch,
        compiler_params=params(collective_id=collective_id, has_side_effects=True),
        cost_estimate=pl.CostEstimate(flops=0, bytes_accessed=16 * moved, transcendentals=0),
    )(*full, *chained)


def to_owner_kernel(chips, wide_ref, thin_ref, out_ref, thin_out, mine, other, came, sems_in, s_core, r_core, s_chain, r_chain, s_thin, r_thin):
    at = Place(chips)
    chain = 2 * chips
    z, c = at.z, at.c
    devices = [(at.d, lax.rem(at.e + k, chain)) for k in range(1, chain)]
    greet(devices, [None] * (chain - 1))

    def load(zz):
        return pltpu.make_async_copy(wide_ref.at[2 * zz + c], mine.at[zz], sems_in.at[zz])

    def to_core(zz):
        return sent(
            wide_ref.at[2 * zz + 1 - c], other.at[zz], s_core.at[zz], r_core.at[zz], at.sibling
        )

    def thin(k):
        target = lax.rem(at.e + k, chain)
        return sent(
            thin_ref.at[target], thin_out.at[at.e], s_thin.at[k], r_thin.at[k], (at.d, target)
        )

    def over(k):
        zz = lax.rem(z + k, chips)
        return sent(
            mine.at[zz], came.at[k], s_chain.at[k], r_chain.at[k], (at.d, 2 * zz + c)
        )

    order = [lax.rem(z + k, chips) for k in range(1, chips)] + [z]
    for zz in order:
        to_core(zz).start()
        load(zz).start()
    for k in range(1, chain):
        thin(k).start()
    own_thin = pltpu.make_async_copy(thin_ref.at[at.e], thin_out.at[at.e], s_thin.at[0])
    own_thin.start()
    for k, zz in enumerate(order):
        to_core(zz).wait_recv()
        load(zz).wait()
        total = mine[zz].astype(F32) + other[zz].astype(F32)
        if k < chips - 1:
            mine[zz] = total.astype(BF)
            over(k + 1).start()
        else:
            out_ref[...] = total
    for k in range(1, chips):
        over(k).wait_recv()
        out_ref[...] += came[k].astype(F32)
    for k in range(1, chips):
        over(k).wait_send()
    for zz in order:
        to_core(zz).wait_send()
    own_thin.wait()
    for k in range(1, chain):
        thin(k).wait()


def to_owner(wide, thin, collective_id):
    chain, rows, width = wide.shape
    chips = chain // 2
    dma = pltpu.SemaphoreType.DMA
    return pl.pallas_call(
        functools.partial(to_owner_kernel, chips),
        out_shape=[
            jax.ShapeDtypeStruct((rows, width), F32),
            jax.ShapeDtypeStruct(thin.shape, thin.dtype),
        ],
        in_specs=[pl.BlockSpec(memory_space=pl.ANY), pl.BlockSpec(memory_space=pltpu.VMEM)],
        out_specs=[pl.BlockSpec(memory_space=pltpu.VMEM), pl.BlockSpec(memory_space=pltpu.VMEM)],
        scratch_shapes=[
            pltpu.VMEM((chips, rows, width), BF),
            pltpu.VMEM((chips, rows, width), BF),
            pltpu.VMEM((chips, rows, width), BF),
            dma((chips,)),
            dma((chips,)),
            dma((chips,)),
            dma((chips,)),
            dma((chips,)),
            dma((chain,)),
            dma((chain,)),
        ],
        compiler_params=params(collective_id=collective_id, has_side_effects=True),
        cost_estimate=pl.CostEstimate(
            flops=0, bytes_accessed=16 * wide.size * 2, transcendentals=0
        ),
    )(wide, thin)


def sum_dense_kernel(chips, chunks, n_in, *refs):
    ins, outs = refs[:n_in], refs[n_in : 2 * n_in]
    n_chunks = len(chunks)
    rest = refs[2 * n_in :]
    sems = rest[:10]
    s_in, s_core, r_core, s_one, r_one, s_two, r_two, s_end, r_end = sems[:9]
    buffers = rest[9:]
    at = Place(chips)
    z, c, x, y = at.z, at.c, at.x, at.y
    others = [(at.d, 2 * lax.rem(z + k, chips) + c) for k in range(1, chips)]
    devices = [at.sibling, at.across_x, at.across_y] + others
    greet(devices, [None] * len(devices))

    class Chunk:
        def __init__(self, q):
            i, first, wide = chunks[q]
            self.i, self.first, self.wide = i, first, wide
            self.q = q
            self.mine, self.other, self.one, self.two, self.end = buffers[5 * q : 5 * q + 5]
            self.cols = pl.ds(first, wide)
            self.half = (pl.ds(0, wide // 2), pl.ds(wide // 2, wide // 2))

        def load(self):
            return pltpu.make_async_copy(
                ins[self.i].at[:, :, :, c, :, self.cols], self.mine, s_in.at[self.q]
            )

        def core(self):
            return sent(
                ins[self.i].at[:, :, :, 1 - c, :, self.cols],
                self.other,
                s_core.at[self.q],
                r_core.at[self.q],
                at.sibling,
            )

        def first_x(self):
            return sent(
                self.mine.at[:, 1 - x, :, :, self.half[0]],
                self.one.at[0],
                s_one.at[self.q, 0],
                r_one.at[self.q, 0],
                at.across_x,
            )

        def first_y(self):
            return sent(
                self.mine.at[1 - y, :, :, :, self.half[1]],
                self.one.at[1],
                s_one.at[self.q, 1],
                r_one.at[self.q, 1],
                at.across_y,
            )

        def second_y(self):
            return sent(
                self.mine.at[1 - y, x, :, :, self.half[0]],
                self.two.at[0],
                s_two.at[self.q, 0],
                r_two.at[self.q, 0],
                at.across_y,
            )

        def second_x(self):
            return sent(
                self.mine.at[y, 1 - x, :, :, self.half[1]],
                self.two.at[1],
                s_two.at[self.q, 1],
                r_two.at[self.q, 1],
                at.across_x,
            )

        def last(self, k):
            zz = lax.rem(z + k, chips)
            return sent(
                self.mine.at[y, x, zz],
                self.end.at[k - 1],
                s_end.at[self.q, k - 1],
                r_end.at[self.q, k - 1],
                (at.d, 2 * zz + c),
            )

    parts = [Chunk(q) for q in range(n_chunks)]

    def add(ref, place, more):
        ref[place] = (ref[place].astype(F32) + more.astype(F32)).astype(BF)

    def stage_one(p):
        p.core().wait_recv()
        p.load().wait()

        def body(k, carry):
            yy, xx, zz = k // (2 * chips), (k // chips) % 2, k % chips
            p.mine[yy, xx, zz] = (
                p.mine[yy, xx, zz].astype(F32) + p.other[yy, xx, zz].astype(F32)
            ).astype(BF)
            return carry

        lax.fori_loop(0, 4 * chips, body, 0)
        p.first_x().start()
        p.first_y().start()

    def stage_two(p):
        p.first_x().wait_recv()
        p.first_y().wait_recv()

        def body(k, carry):
            v, zz = k // chips, k % chips
            a, b = p.half
            p.mine[v, x, zz, :, a] = (
                p.mine[v, x, zz, :, a].astype(F32) + p.one[0, v, zz].astype(F32)
            ).astype(BF)
            p.mine[y, v, zz, :, b] = (
                p.mine[y, v, zz, :, b].astype(F32) + p.one[1, v, zz].astype(F32)
            ).astype(BF)
            return carry

        lax.fori_loop(0, 2 * chips, body, 0)
        p.second_y().start()
        p.second_x().start()

    def stage_three(p):
        p.second_y().wait_recv()
        p.second_x().wait_recv()

        def body(zz, carry):
            for w in (0, 1):
                s = p.half[w]
                p.mine[y, x, zz, :, s] = (
                    p.mine[y, x, zz, :, s].astype(F32) + p.two[w, zz].astype(F32)
                ).astype(BF)
            return carry

        lax.fori_loop(0, chips, body, 0)
        for k in range(1, chips):
            p.last(k).start()

    def stage_four(p):
        total = p.mine[y, x, z].astype(F32)
        for k in range(1, chips):
            p.last(k).wait_recv()
            total = total + p.end[k - 1].astype(F32)
        outs[p.i][:, p.first : p.first + p.wide] = total

    for p in parts:
        p.core().start()
        p.load().start()
    stages = (stage_one, stage_two, stage_three, stage_four)
    for t in range(n_chunks + len(stages) - 1):
        for s, stage in enumerate(stages):
            if 0 <= t - s < n_chunks:
                stage(parts[t - s])
    for p in parts:
        p.core().wait_send()
        p.first_x().wait_send()
        p.first_y().wait_send()
        p.second_x().wait_send()
        p.second_y().wait_send()
        for k in range(1, chips):
            p.last(k).wait_send()


def sum_dense(arrays, chunk_widths, collective_id):
    chain = lax.axis_size("expert")
    chips = chain // 2
    assert lax.axis_size("dp") == 4
    block = arrays[0].shape[0] // (4 * chain)
    dma = pltpu.SemaphoreType.DMA
    chunks = []
    for i, (array, wide) in enumerate(zip(arrays, chunk_widths)):
        assert array.shape[1] % wide == 0 and wide % 256 == 0
        chunks += [(i, first, wide) for first in range(0, array.shape[1], wide)]
    q = len(chunks)
    scratch = [dma((q,)), dma((q,)), dma((q,))] + [dma((q, 2))] * 4 + [dma((q, max(1, chips - 1)))] * 2
    for i, first, wide in chunks:
        scratch += [
            pltpu.VMEM((2, 2, chips, block, wide), BF),
            pltpu.VMEM((2, 2, chips, block, wide), BF),
            pltpu.VMEM((2, 2, chips, block, wide // 2), BF),
            pltpu.VMEM((2, chips, block, wide // 2), BF),
            pltpu.VMEM((max(1, chips - 1), block, wide), BF),
        ]
    n = len(arrays)
    return pl.pallas_call(
        functools.partial(sum_dense_kernel, chips, tuple(chunks), n),
        out_shape=[jax.ShapeDtypeStruct((block, a.shape[1]), F32) for a in arrays],
        in_specs=[pl.BlockSpec(memory_space=pl.ANY)] * n,
        out_specs=[pl.BlockSpec(memory_space=pltpu.VMEM)] * n,
        scratch_shapes=scratch,
        compiler_params=params(collective_id=collective_id, has_side_effects=True),
        cost_estimate=pl.CostEstimate(
            flops=0, bytes_accessed=16 * sum(a.size for a in arrays), transcendentals=0
        ),
    )(*[a.reshape(2, 2, chips, 2, block, a.shape[1]) for a in arrays])


def qkv_kernel(per_block, x_ref, w_ref, cos_ref, sin_ref, o_ref):
    column = pl.program_id(1)
    product = nn(x_ref[...], w_ref[...])
    for k in range(per_block):
        part = product[:, k * HD : (k + 1) * HD]
        head = column * per_block + k
        turned = part * cos_ref[...] + pltpu.roll(part, HD // 2, 1) * sin_ref[...]
        o_ref[:, k * HD : (k + 1) * HD] = jnp.where(head < 2 * H, turned, part).astype(BF)


def project_qkv(normed, weight, cosine, sine):
    rows, width = normed.shape
    columns = weight.shape[1]
    per_block = 2
    tile_m = min(rows, 1536)
    return pl.pallas_call(
        functools.partial(qkv_kernel, per_block),
        out_shape=jax.ShapeDtypeStruct((rows, columns), BF),
        grid=(rows // tile_m, columns // (per_block * HD)),
        in_specs=[
            pl.BlockSpec((tile_m, width), lambda m, n: (m, 0)),
            pl.BlockSpec((width, per_block * HD), lambda m, n: (0, n)),
            pl.BlockSpec((tile_m, HD), lambda m, n: (m, 0)),
            pl.BlockSpec((tile_m, HD), lambda m, n: (m, 0)),
        ],
        out_specs=pl.BlockSpec((tile_m, per_block * HD), lambda m, n: (m, n)),
        compiler_params=params(),
        cost_estimate=pl.CostEstimate(
            flops=2 * rows * width * columns,
            bytes_accessed=2 * (rows * width + width * columns + rows * columns),
            transcendentals=0,
        ),
    )(normed, weight, cosine, sine)


def attend_kernel(scale, me_ref, q_ref, k_ref, v_ref, first_ref, o_ref, log_ref, bias):
    rows, keys = bias.shape

    @pl.when(pl.program_id(0) == 0)
    def _():
        key_place = lax.broadcasted_iota(jnp.int32, (rows, keys), 1)
        query_place = me_ref[0] * rows + lax.broadcasted_iota(jnp.int32, (rows, keys), 0)
        allowed = (key_place <= query_place) & (key_place >= first_ref[...])
        bias[...] = jnp.where(allowed, 0.0, NEG)

    scores = nt(q_ref[...], k_ref[...]) * scale + bias[...]
    top = jnp.max(scores, axis=-1, keepdims=True)
    weights = jnp.exp(scores - top)
    total = jnp.sum(weights, axis=-1, keepdims=True)
    o_ref[...] = nn(weights.astype(BF), v_ref[...]) / total
    log_ref[...] = jnp.broadcast_to(top + jnp.log(total), (rows, 8))[None]


def attend(me, qkv, first_own):
    keys = qkv.shape[0]
    rows = first_own.shape[0]
    return pl.pallas_call(
        functools.partial(attend_kernel, HD**-0.5),
        out_shape=[
            jax.ShapeDtypeStruct((rows, H * HD), F32),
            jax.ShapeDtypeStruct((H, rows, 8), F32),
        ],
        grid_spec=pltpu.PrefetchScalarGridSpec(
            num_scalar_prefetch=1,
            grid=(H,),
            in_specs=[
                pl.BlockSpec((rows, HD), lambda h, me: (me[0], h)),
                pl.BlockSpec((keys, HD), lambda h, me: (0, H + h)),
                pl.BlockSpec((keys, HD), lambda h, me: (0, 2 * H + h)),
                pl.BlockSpec((rows, 1), lambda h, me: (0, 0)),
            ],
            out_specs=[
                pl.BlockSpec((rows, HD), lambda h, me: (0, h)),
                pl.BlockSpec((1, rows, 8), lambda h, me: (h, 0, 0)),
            ],
            scratch_shapes=[pltpu.VMEM((rows, keys), F32)],
        ),
        compiler_params=params(),
        cost_estimate=pl.CostEstimate(
            flops=4 * rows * keys * H * HD,
            bytes_accessed=4 * keys * H * HD,
            transcendentals=H * rows * keys,
        ),
    )(me, qkv, qkv, qkv, first_own[:, None])


def attend_back_kernel(
    scale,
    me_ref,
    q_ref,
    k_ref,
    v_ref,
    qa_ref,
    ko_ref,
    vo_ref,
    do_ref,
    da_ref,
    log_ref,
    delta_ref,
    loga_ref,
    deltaa_ref,
    first_ref,
    firsta_ref,
    cos_ref,
    sin_ref,
    o_ref,
    bias,
    biast,
):
    rows, keys = bias.shape

    @pl.when(pl.program_id(0) == 0)
    def _():
        place = lax.broadcasted_iota(jnp.int32, (rows, keys), 1)
        own = me_ref[0] * rows + lax.broadcasted_iota(jnp.int32, (rows, keys), 0)
        bias[...] = jnp.where((place <= own) & (place >= first_ref[...]), 0.0, NEG)
        biast[...] = jnp.where((own <= place) & (own >= firsta_ref[...]), 0.0, NEG)

    def unturn(value):
        return value * cos_ref[...] - pltpu.roll(value, HD // 2, 1) * sin_ref[...]

    log_own = log_ref[0][:, :1]
    delta_own = delta_ref[0][:, :1]
    weights = jnp.exp(nt(q_ref[...], k_ref[...]) * scale + bias[...] - log_own)
    back = nt(do_ref[...], v_ref[...])
    grad = (weights * (back - delta_own) * scale).astype(BF)
    o_ref[0] = unturn(nn(grad, k_ref[...])).astype(BF)

    weights = jnp.exp(nt(ko_ref[...], qa_ref[...]) * scale + biast[...] - loga_ref[0])
    o_ref[2] = nn(weights.astype(BF), da_ref[...]).astype(BF)
    back = nt(vo_ref[...], da_ref[...])
    grad = (weights * (back - deltaa_ref[0]) * scale).astype(BF)
    o_ref[1] = unturn(nn(grad, qa_ref[...])).astype(BF)


def attend_back(me, qkv, grad_own, grad_all, log_own, delta_own, log_all, delta_all, first, cosine, sine):
    keys = qkv.shape[0]
    rows = grad_own.shape[0]
    first_own, first_all = first
    return pl.pallas_call(
        functools.partial(attend_back_kernel, HD**-0.5),
        out_shape=jax.ShapeDtypeStruct((3, rows, H * HD), BF),
        grid_spec=pltpu.PrefetchScalarGridSpec(
            num_scalar_prefetch=1,
            grid=(H,),
            in_specs=[
                pl.BlockSpec((rows, HD), lambda h, me: (me[0], h)),
                pl.BlockSpec((keys, HD), lambda h, me: (0, H + h)),
                pl.BlockSpec((keys, HD), lambda h, me: (0, 2 * H + h)),
                pl.BlockSpec((keys, HD), lambda h, me: (0, h)),
                pl.BlockSpec((rows, HD), lambda h, me: (me[0], H + h)),
                pl.BlockSpec((rows, HD), lambda h, me: (me[0], 2 * H + h)),
                pl.BlockSpec((rows, HD), lambda h, me: (0, h)),
                pl.BlockSpec((keys, HD), lambda h, me: (0, h)),
                pl.BlockSpec((1, rows, 8), lambda h, me: (h, 0, 0)),
                pl.BlockSpec((1, rows, 8), lambda h, me: (h, 0, 0)),
                pl.BlockSpec((1, 1, keys), lambda h, me: (h, 0, 0)),
                pl.BlockSpec((1, 1, keys), lambda h, me: (h, 0, 0)),
                pl.BlockSpec((rows, 1), lambda h, me: (0, 0)),
                pl.BlockSpec((1, keys), lambda h, me: (0, 0)),
                pl.BlockSpec((rows, HD), lambda h, me: (0, 0)),
                pl.BlockSpec((rows, HD), lambda h, me: (0, 0)),
            ],
            out_specs=pl.BlockSpec((3, rows, HD), lambda h, me: (0, 0, h)),
            scratch_shapes=[pltpu.VMEM((rows, keys), F32)] * 2,
        ),
        compiler_params=params(),
        cost_estimate=pl.CostEstimate(
            flops=14 * rows * keys * H * HD,
            bytes_accessed=8 * keys * H * HD,
            transcendentals=2 * H * rows * keys,
        ),
    )(
        me,
        qkv,
        qkv,
        qkv,
        qkv,
        qkv,
        qkv,
        grad_own,
        grad_all,
        log_own,
        delta_own,
        log_all,
        delta_all,
        first_own[:, None],
        first_all[None, :],
        cosine,
        sine,
    )


def silu_parts(values):
    s = jax.nn.sigmoid(values)
    return values * s, s * (1.0 + values * (1.0 - s))


def local(
    tokens,
    cotangent,
    lengths,
    routes,
    attn_qkv,
    attn_out,
    shared_gate,
    shared_up,
    shared_down,
    router,
    gains,
    expert_gate,
    expert_up,
    expert_down,
):
    rows = tokens.shape[1]
    width = tokens.shape[2]
    hidden = shared_gate.shape[1]
    chain = lax.axis_size("expert")
    index = lax.axis_index("expert")
    experts = EXP_DEV * chain
    everyone = ("dp", "expert")
    keys = rows * chain
    own_first = index * rows
    me = index.reshape(1).astype(jnp.int32)

    route_pad = 128 * (-(-(experts + 2) // 128))
    misc = jnp.concatenate([router.astype(BF), gains.astype(BF).T], axis=1)
    misc = jnp.pad(misc, ((0, 0), (0, route_pad - experts - 2)))
    rest = jnp.concatenate(
        [
            misc,
            attn_out.astype(BF).T,
            shared_gate.astype(BF),
            shared_up.astype(BF),
            shared_down.astype(BF).T,
        ],
        axis=1,
    )
    qkv_weight, rest, tokens_all, routes_all, grads_all = gather(
        [attn_qkv.astype(BF), rest], [tokens[0], routes[0], cotangent[0]], 0
    )
    qkv_weight = qkv_weight.reshape(width, 3 * H * HD)
    rest = rest.reshape(width, rest.shape[-1])
    tokens_all = tokens_all.reshape(keys, width)
    routes_all = routes_all.reshape(keys, TOP)
    grads_all = grads_all.reshape(keys, width)
    cuts = [route_pad, route_pad + width]
    cuts += [cuts[-1] + hidden, cuts[-1] + 2 * hidden]
    misc, out_t, gate_shared, up_shared, down_t = jnp.split(rest, cuts, axis=1)
    route_weight = misc[:, :experts]
    gain_attn = misc[:, experts].astype(F32)
    gain_moe = misc[:, experts + 1].astype(F32)
    expert_shard = jnp.stack(
        [expert_gate.astype(BF), expert_up.astype(BF), jnp.swapaxes(expert_down.astype(BF), 1, 2)]
    )
    expert_shard, tokens_all = lax.optimization_barrier((expert_shard, tokens_all))
    expert_weight = lax.all_gather(expert_shard, "dp", axis=2, tiled=True)

    first_all, rope_all = doc_starts_of(lengths[0], jnp.arange(keys, dtype=jnp.int32))
    first_own = lax.dynamic_slice_in_dim(first_all, own_first, rows, 0)
    cosine, sine = turn_tables(rope_all)
    cosine_own = lax.dynamic_slice_in_dim(cosine, own_first, rows, 0)
    sine_own = lax.dynamic_slice_in_dim(sine, own_first, rows, 0)
    wide = tokens_all.astype(F32)
    normed_all = (wide * inverse_rms(wide) * gain_attn).astype(BF)
    inputs = tokens[0].astype(F32)
    inverse_one = inverse_rms(inputs)
    unit_one = inputs * inverse_one
    normed = (unit_one * gain_attn).astype(BF)
    qkv = project_qkv(normed_all, qkv_weight, cosine, sine)
    attended_full, log_own = attend(me, qkv, first_own)
    attended = attended_full.astype(BF)
    middle = inputs + nt(attended, out_t)
    inverse_two = inverse_rms(middle)
    unit_two = middle * inverse_two
    normed_moe = (unit_two * gain_moe).astype(BF)
    moe_all = gather([], [normed_moe], 1)[0].reshape(keys, width)

    def routing(activations, route_ids):
        logits = nn(activations, route_weight)
        probs = jax.nn.softmax(logits, axis=-1)
        named = route_ids[:, :, None] == jnp.arange(experts, dtype=jnp.int32)[None, None, :]
        named = jnp.any(named, axis=1)
        chosen = jnp.where(named, probs, 0.0)
        total = jnp.sum(chosen, axis=1, keepdims=True)
        return probs, named, chosen / total, total

    probs, named, gates, chosen_total = routing(normed_moe, routes[0])
    unused, unused, gates_all, unused = routing(moe_all, routes_all)
    gates_here = lax.dynamic_slice_in_dim(gates_all, index * EXP_DEV, EXP_DEV, 1)

    shared_gate_v = nn(normed_moe, gate_shared)
    shared_up_v = nn(normed_moe, up_shared)
    shared_act, shared_slope = silu_parts(shared_gate_v)
    shared_mid = (shared_act * shared_up_v).astype(BF)
    shared_out = nt(shared_mid, down_t)
    grad_out = cotangent[0].astype(F32)
    grad_bf = cotangent[0]
    grad_shared_mid = nn(grad_bf, down_t)
    grad_shared_gate_v = (grad_shared_mid * shared_up_v * shared_slope).astype(BF)
    grad_shared_up_v = (grad_shared_mid * shared_act).astype(BF)
    grad_down_t = tn(grad_bf, shared_mid)
    grad_gate_shared = tn(normed_moe, grad_shared_gate_v)
    grad_up_shared = tn(normed_moe, grad_shared_up_v)
    grad_normed_moe = nt(grad_shared_gate_v, gate_shared) + nt(grad_shared_up_v, up_shared)

    mixture = jnp.zeros((keys, width), F32)
    row_grads = jnp.zeros((keys, width), F32)
    wide_grads = grads_all.astype(F32)
    gate_grads = []
    weight_grads = []
    for e in range(EXP_DEV):
        gate_w, up_w, down_w = expert_weight[0, e], expert_weight[1, e], expert_weight[2, e]
        weight = gates_here[:, e : e + 1]
        gate_v = nn(moe_all, gate_w)
        up_v = nn(moe_all, up_w)
        act, slope = silu_parts(gate_v)
        mid = (act * up_v).astype(BF)
        branch = (weight * wide_grads).astype(BF)
        grad_mid = nn(branch, down_w)
        grad_gate_v = (grad_mid * up_v * slope).astype(BF)
        grad_up_v = (grad_mid * act).astype(BF)
        row = (nt(grad_gate_v, gate_w) + nt(grad_up_v, up_w)).astype(BF)
        row_grads = row_grads + row.astype(F32)
        out = nt(mid, down_w).astype(BF).astype(F32)
        mixture = mixture + weight * out
        gate_grads.append(jnp.sum(out * wide_grads, axis=1))
        weight_grads.append(
            jnp.stack(
                [
                    tn(moe_all, grad_gate_v).astype(BF),
                    tn(moe_all, grad_up_v).astype(BF),
                    tn(branch, mid).astype(BF),
                ]
            )
        )
    gate_grads = jnp.transpose(jnp.stack(gate_grads, axis=0).reshape(EXP_DEV, chain, rows), (1, 0, 2))
    row_sum, gate_grads = to_owner(
        row_grads.astype(BF).reshape(chain, rows, width), gate_grads, 2
    )
    mixture_own = lax.psum_scatter(mixture.astype(BF), "expert", scatter_dimension=0, tiled=True)
    gate_grads = gate_grads.reshape(experts, rows).T
    expert_sum = lax.psum_scatter(
        jnp.stack(weight_grads, axis=1), "dp", scatter_dimension=2, tiled=True
    ).astype(F32)
    output = (middle + shared_out + mixture_own.astype(F32)).astype(BF)

    grad_chosen = (gate_grads - jnp.sum(gates * gate_grads, axis=1, keepdims=True)) / chosen_total
    grad_probs = jnp.where(named, grad_chosen, 0.0)
    grad_logits = (
        probs * (grad_probs - jnp.sum(probs * grad_probs, axis=1, keepdims=True))
    ).astype(BF)
    grad_route = tn(normed_moe, grad_logits)
    grad_normed_moe = grad_normed_moe + row_sum + nt(grad_logits, route_weight)
    grad_gain_moe = jnp.sum(grad_normed_moe * unit_two, axis=0)
    scaled_two = grad_normed_moe * gain_moe
    grad_middle = grad_out + inverse_two * (
        scaled_two - unit_two * jnp.mean(scaled_two * unit_two, axis=-1, keepdims=True)
    )
    grad_attn = grad_middle.astype(BF)
    grad_attended = nn(grad_attn, out_t).astype(BF)
    grad_out_t = tn(grad_attn, attended)

    delta = jnp.sum((grad_attended.astype(F32) * attended_full).reshape(rows, H, HD), axis=-1).T
    side = jnp.concatenate([log_own[:, :, 0], delta], axis=0)
    grad_all, side_all = gather([], [grad_attended, side], 3)
    grad_all = grad_all.reshape(keys, H * HD)
    side_all = jnp.transpose(side_all, (1, 0, 2)).reshape(2, H, 1, keys)
    grads = attend_back(
        me,
        qkv,
        grad_attended,
        grad_all,
        log_own,
        jnp.broadcast_to(delta[:, :, None], (H, rows, 8)),
        side_all[0],
        side_all[1],
        (first_own, first_all),
        cosine_own,
        sine_own,
    )
    grad_projected = jnp.concatenate([grads[0], grads[1], grads[2]], axis=1)
    grad_qkv = tn(normed, grad_projected)
    grad_normed_one = nt(grad_projected, qkv_weight)
    grad_gain_attn = jnp.sum(grad_normed_one * unit_one, axis=0)
    scaled_one = grad_normed_one * gain_attn
    grad_inputs = grad_middle + inverse_one * (
        scaled_one - unit_one * jnp.mean(scaled_one * unit_one, axis=-1, keepdims=True)
    )

    grad_misc = jnp.concatenate([grad_route, grad_gain_attn[:, None], grad_gain_moe[:, None]], axis=1)
    grad_misc = jnp.pad(grad_misc, ((0, 0), (0, route_pad - experts - 2)))
    rest_sum, qkv_sum = sum_dense(
        [
            jnp.concatenate(
                [
                    grad_misc.astype(BF),
                    grad_out_t.astype(BF),
                    grad_gate_shared.astype(BF),
                    grad_up_shared.astype(BF),
                    grad_down_t.astype(BF),
                ],
                axis=1,
            ),
            grad_qkv.astype(BF),
        ],
        (1024, 768),
        4,
    )
    misc_sum, out_sum, gate_sum, up_sum, down_sum = jnp.split(rest_sum, cuts, axis=1)
    return (
        output[None],
        grad_inputs.astype(BF)[None],
        qkv_sum,
        out_sum.T,
        gate_sum,
        up_sum,
        down_sum.T,
        misc_sum[:, :experts],
        misc_sum[:, experts : experts + 2].T,
        expert_sum[0],
        expert_sum[1],
        jnp.swapaxes(expert_sum[2], 1, 2),
    )


def solution(mesh):
    everyone = ("dp", "expert")
    in_specs = (
        P("dp", "expert", None),
        P("dp", "expert", None),
        P("dp", None),
        P("dp", "expert", None),
        P(everyone, None),
        P(None, everyone),
        P(everyone, None),
        P(everyone, None),
        P(None, everyone),
        P(everyone, None),
        P(None, everyone),
        P("expert", "dp", None),
        P("expert", "dp", None),
        P("expert", None, "dp"),
    )
    out_specs = (
        P("dp", "expert", None),
        P("dp", "expert", None),
        P(everyone, None),
        P(None, everyone),
        P(everyone, None),
        P(everyone, None),
        P(None, everyone),
        P(everyone, None),
        P(None, everyone),
        P("expert", "dp", None),
        P("expert", "dp", None),
        P("expert", None, "dp"),
    )
    return jax.shard_map(local, mesh=mesh, in_specs=in_specs, out_specs=out_specs, check_vma=False)
```

time: 2060 us -> 749 us (0.36)
  waiting for transfers between devices: 1350 us -> 24.2 us
  Pallas kernels: 0 us -> 422 us
  blocking collectives: 152 us -> 0 us
  local copies, waits for them, and re-layouts: 176 us -> 47.2 us
  matrix products: 252 us -> 183 us
  other arithmetic: 85.1 us -> 46.4 us
    reduce_scatter x5 -> x2, waiting for transfers between devices: 491 us -> 0.01 us  [the longest x1 0.01 us: local(): lax.psum_scatter(mixture.astype(BF), 'expert', scatter_dimension=0, tiled...]
    pallas_call x0 -> x8, Pallas kernels: none -> 422 us  [the longest x3 225 us: gather(): pl.pallas_call(functools.partial(gather_kernel, chips, len(full), len(cha...]
    all_to_all x4 -> x0, waiting for transfers between devices: 398 us -> none  [the longest x1 107 us: local(): lax.all_to_all(send_rows, 'expert', split_axis=0, concat_axis=2, tiled=True)]
    unnamed x25 -> x3, waiting for transfers between devices: 382 us -> 0.05 us
    all_gather x4 -> x0, blocking collectives: 112 us -> none  [the longest x1 43.1 us: local(): lax.all_gather(gains.astype(bfloat), ('dp', 'expert'), axis=1, tiled=True)]
    dot_general x50 -> x36, matrix products: 252 us -> 183 us  [the longest x12 71 us: nt(): lax.dot_general(a, b, (((1,), (1,)), ((), ())), preferred_element_type=F32)]
    all_gather x12 -> x1, waiting for transfers between devices: 76.3 us -> 24.2 us  [local(): expert_weight = lax.all_gather(expert_shard, 'dp', axis=2, tiled=True)]
    unnamed x1 -> x0, blocking collectives: 40.2 us -> none
  transfers between devices with their start and end apart: 25 -> 3, of which waited for: 16 -> 1; matrix products, arithmetic and copies ran while one was open for 23% -> 26% of each run, Pallas kernels for 0% -> 39%
where the time goes in v1:
time: 749 us; the launch traced here: 738 us
  Pallas kernels  422 us (56%)
  matrix products  183 us (24%)
  local copies, waits for them, and re-layouts  47.2 us (6%)
  other arithmetic  46.4 us (6%)
  waiting for transfers between devices  24.2 us (3%)
  between operations  14.9 us (2%)
    pallas_call x3, Pallas kernels, gather(): pl.pallas_call(functools.partial(gather_kernel, chips, len(full), len(cha...  225 us
    pallas_call x1, Pallas kernels, sum_dense(): pl.pallas_call(functools.partial(sum_dense_kernel, chips, tuple(chunks),...  101 us
    dot_general x12, matrix products, nt(): lax.dot_general(a, b, (((1,), (1,)), ((), ())), preferred_element_type=F32)  71 us
    dot_general x12, matrix products, nn(): return jnp.dot(a, b, preferred_element_type=F32)  66 us
    dot_general x12, matrix products, tn(): lax.dot_general(a, b, (((0,), (0,)), ((), ())), preferred_element_type=F32)  46.4 us
    pallas_call x1, Pallas kernels, to_owner(): pl.pallas_call(functools.partial(to_owner_kernel, chips), out_shape=[jax....  40.9 us
    all_gather x1, waiting for transfers between devices, local(): expert_weight = lax.all_gather(expert_shard, 'dp', axis=2, tiled=True)  24.2 us
    pallas_call x1, Pallas kernels, project_qkv(): pl.pallas_call(functools.partial(qkv_kernel, per_block), out_shape=jax.Sh...  23.7 us
  transfers between devices with their start and end apart: 3, of which 1 were waited for; matrix products, arithmetic and copies ran while one was open for 26% of the time, Pallas kernels for 39%

profile of v1, /device:TPU:0, one launch (start us, length us, event | category | flops | bytes accessed | tf_op | source)
XLA Modules:
  0.0 738.3 jit_solution(6098536474444620630)
XLA Ops:
  16.9 134.4 %shard_map.229 = (bf16[32,40,3840]{2,1,0:T(8,128)(2,1)}, bf16[32,40,4096]{2,1,0:T(8,128)(2,1)}, bf16[8,192,1280]{2,1,0:T(8,128)(2,1)}, s32[8,192,7]{2,1,0:T(8,128)}, bf16[8,192,1280]{2,1,0:T(8,128)(2,1)}) custom-call(bf16[40,3840]{1,0:T(8,128)(2,1)} %convert_element_type.233.refs_0_, bf16[40,4096]{1,0:T(8,128)(2,1)} %copy-done.28, ...), custom_call_target="tpu_custom_call" | custom-call | bytes 451575808 | tf_op jit(solution)/shard_map/pallas_call | solution.py:299
  168.9 23.7 %shard_map.230.q_ref.k_ref.v_ref.qa_ref.ko_ref.vo_ref = bf16[1536,3840]{1,0:T(8,128)(2,1)} custom-call(bf16[1536,1280]{1,0:T(8,128)(2,1)} %fusion.2.x_ref, bf16[1280,3840]{1,0:T(8,128)(2,1)} %bitcast.243, f32[1536,128]{1,0:T(8,128)} %get-tuple-element.142.cos_ref, f32[1536,128]{1,0:T(8,128)} %get-tuple-element.143.sin_ref), custom_call_target="tpu_custom_call" | custom-call | flops 15099494400 | bytes 25559040 | tf_op jit(solution)/shard_map/pallas_call | solution.py:608
  192.6 12.0 %shard_map.231 = (f32[192,1280]{1,0:T(8,128)}, f32[10,192,8]{2,1,0:T(8,128)}) custom-call(s32[1]{0:T(128)} %bitcast.1.me_ref, bf16[1536,3840]{1,0:T(8,128)(2,1)} %shard_map.230.q_ref.k_ref.v_ref.qa_ref.ko_ref.vo_ref, bf16[1536,3840]{1,0:T(8,128)(2,1)} %shard_map.230.q_ref.k_ref.v_ref.qa_ref.ko_ref.vo_ref, ...), custom_call_target="tpu_custom_call" | custom-call | flops 1509949440 | bytes 7864320 | tf_op jit(solution)/shard_map/pallas_call | solution.py:649
  210.0 39.8 %shard_map.232 = bf16[8,192,1280]{2,1,0:T(8,128)(2,1)} custom-call(bf16[192,1280]{1,0:T(8,128)(2,1)} %multiply_convert_fusion.6.refs_0_), custom_call_target="tpu_custom_call" | custom-call | bytes 62914560 | tf_op jit(solution)/shard_map/pallas_call | solution.py:299
  253.8 5.2 fusion.8
  259.1 24.2 %all-gather.2.cloned.1.call-done = bf16[3,2,1280,896]{3,2,1,0:T(8,128)(2,1)} async-done(((bf16[3,2,320,896]{3,2,1,0:T(8,128)(2,1)}), bf16[3,2,1280,896]{3,2,1,0:T(8,128)(2,1)}) %all-gather.2.cloned.1.call-update) | async-done | bytes 13762576 | tf_op jit(solution)/shard_map/all_gather | solution.py:849
  283.2 9.6 %fusion.42 = f32[1536,896]{1,0:T(8,128)} fusion(bf16[1536,1280]{1,0:T(8,128)(2,1)} %bitcast.205, bf16[3,2,1280,896]{3,2,1,0:T(8,128)(2,1)} %all-gather.2.cloned.1.call-done), kind=kOutput, calls=%fused_computation.89 | convolution fusion | flops 3523215360 | bytes 11730944 | tf_op jit(solution)/shard_map/dot_general | solution.py:26
  292.9 5.9 fusion.41
  298.8 5.9 fusion.46
  304.7 5.9 fusion.45
  310.6 10.7 %multiply_convert_fusion = (bf16[1536,896]{1,0:T(8,128)(2,1)}, bf16[1536,896]{1,0:T(8,128)(2,1)S(1)}, bf16[1536,896]{1,0:T(8,128)(2,1)}) fusion(f32[1536,896]{1,0:T(8,128)} %fusion.45, f32[1536,896]{1,0:T(8,128)} %fusion.46, bf16[1536,1280]{1,0:T(8,128)(2,1)S(1)} %bitcast.231, bf16[3,2,1280,896]{3,2,1,0:T(8,128)(2,1)S(1)} %copy-done.45), kind=kOutput, calls=%fused_computation.34 | convolution fusion | flops 3543859200 | bytes 25493504 | tf_op jit(solution)/shard_map/dot_general | solution.py:26
  321.3 7.1 convolution_convert_fusion.2
  328.4 11.1 %multiply_convert_fusion.2 = (bf16[1536,896]{1,0:T(8,128)(2,1)}, bf16[1536,896]{1,0:T(8,128)(2,1)}, bf16[1536,896]{1,0:T(8,128)(2,1)S(1)}) fusion(f32[1536,896]{1,0:T(8,128)} %fusion.41, f32[1536,896]{1,0:T(8,128)} %fusion.42, bf16[1536,1280]{1,0:T(8,128)(2,1)S(1)} %bitcast.230, bf16[3,2,1280,896]{3,2,1,0:T(8,128)(2,1)} %all-gather.2.cloned.1.call-done), kind=kOutput, calls=%fused_computation.36 | convolution fusion | flops 3543859200 | bytes 25493504 | tf_op jit(solution)/shard_map/dot_general | solution.py:26
  339.5 11.5 %fusion.5 = (f32[1536]{0:T(1024)S(1)}, f32[1536]{0:T(1024)S(1)}, bf16[1536,1280]{1,0:T(8,128)(2,1)}, bf16[1536,1280]{1,0:T(8,128)(2,1)}, bf16[1536,1280]{1,0:T(8,128)(2,1)}) fusion(bf16[8,192,1280]{2,1,0:T(8,128)(2,1)S(1)} %copy-done.16, bf16[1536,1280]{1,0:T(8,128)(2,1)S(1)} %convolution_convert_fusion.2, f32[1536]{0:T(1024)S(1)} %get-tuple-element.97, ...), kind=kOutput, calls=%fused_computation.15 | convolution fusion | flops 3554669568 | bytes 24731648 | tf_op jit(solution)/shard_map/dot_general | solution.py:30
  351.1 7.4 %fusion.22 = bf16[1,1280,896]{2,1,0:T(8,128)(2,1)S(1)} fusion(bf16[1536,1280]{1,0:T(8,128)(2,1)} %get-tuple-element.112, bf16[1536,896]{1,0:T(8,128)(2,1)} %copy-done.53), kind=kOutput, calls=%fused_computation.60 | convolution fusion | flops 3524362240 | bytes 8978432 | tf_op jit(solution)/shard_map/dot_general | solution.py:34
  358.5 4.7 fusion.20
  363.3 4.5 fusion.21
  370.8 4.5 fusion.25
  375.4 4.5 fusion.23
  379.9 4.5 fusion.24
  385.5 6.5 pad_maximum_fusion
  411.2 6.9 fusion.40
  418.2 6.2 fusion.44
  424.4 7.7 %fusion.11 = bf16[1536,1280]{1,0:T(8,128)(2,1)} fusion(f32[1536,1280]{1,0:T(8,128)S(1)} %fusion.40, bf16[1536,896]{1,0:T(8,128)(2,1)S(1)} %copy-done.57, bf16[3,2,1280,896]{3,2,1,0:T(8,128)(2,1)} %all-gather.2.cloned.1.call-done), kind=kOutput, calls=%fused_computation.26 | convolution fusion | flops 3527147520 | bytes 16842752 | tf_op jit(solution)/shard_map/dot_general | solution.py:30
  432.1 9.0 %add_convert_fusion = bf16[1536,1280]{1,0:T(8,128)(2,1)} fusion(bf16[1536,1280]{1,0:T(8,128)(2,1)} %fusion.11, f32[1536,1280]{1,0:T(8,128)S(1)} %fusion.44, bf16[1536,896]{1,0:T(8,128)(2,1)S(1)} %copy-done.55, bf16[3,2,1280,896]{3,2,1,0:T(8,128)(2,1)} %all-gather.2.cloned.1.call-done), kind=kOutput, calls=%fused_computation.25 | convolution fusion | flops 3535011840 | bytes 20774912 | tf_op jit(solution)/shard_map/dot_general | solution.py:30
  441.2 40.9 %shard_map.233 = (f32[192,1280]{1,0:T(8,128)}, f32[8,2,192]{2,1,0:T(2,128)}) custom-call(bf16[8,192,1280]{2,1,0:T(8,128)(2,1)} %bitcast.232, f32[8,2,192]{2,1,0:T(2,128)} %maximum_bitcast_fusion.2.thin_ref), custom_call_target="tpu_custom_call" | custom-call | bytes 62914560 | tf_op jit(solution)/shard_map/pallas_call | solution.py:370
  496.9 51.1 %shard_map.234 = (bf16[8,192,1280]{2,1,0:T(8,128)(2,1)}, f32[8,20,192]{2,1,0:T(8,128)}) custom-call(bf16[192,1280]{1,0:T(8,128)(2,1)} %get-tuple-element.138.refs_0_.do_ref, f32[20,192]{1,0:T(8,128)} %pad_maximum_fusion.7.refs_1_), custom_call_target="tpu_custom_call" | custom-call | bytes 64880640 | tf_op jit(solution)/shard_map/pallas_call | solution.py:299
  552.0 18.7 %shard_map.235 = bf16[3,192,1280]{2,1,0:T(8,128)(2,1)} custom-call(s32[1]{0:T(128)} %bitcast.1.me_ref, bf16[1536,3840]{1,0:T(8,128)(2,1)} %shard_map.230.q_ref.k_ref.v_ref.qa_ref.ko_ref.vo_ref, bf16[1536,3840]{1,0:T(8,128)(2,1)} %shard_map.230.q_ref.k_ref.v_ref.qa_ref.ko_ref.vo_ref, bf16[1536,3840]{1,0:T(8,128)(2,1)} %shard_map.230.q_ref.k_ref.v_ref.qa_ref.ko_ref.vo_ref, ...), custom_call_target="tpu_custom_call" | custom-call | flops 5284823040 | bytes 15728640 | tf_op jit(solution)/shard_map/pallas_call | solution.py:732
  572.1 8.4 %fusion.70 = (bf16[1280]{0:T(1024)(128)(2,1)S(1)}, f32[192]{0:T(256)S(1)}, f32[192,1280]{1,0:T(8,128)}) fusion(f32[192]{0:T(256)S(1)} %add_rsqrt_fusion.1, bf16[1,192,1280]{2,1,0:T(8,128)(2,1)S(1)} %copy-done.6, f32[1280]{0:T(1024)S(1)} %copy-done.34, bf16[1280,3840]{1,0:T(8,128)(2,1)} %bitcast.244, bf16[192,1280]{1,0:T(8,128)(2,1)S(1)} %get-tuple-element.117, ...), kind=kOutput, calls=%fused_computation.123 | convolution fusion | flops 1893579264 | bytes 12788736 | tf_op jit(solution)/shard_map/dot_general | solution.py:30
  591.0 14.3 %copy.86 = bf16[1280,4096]{1,0:T(8,128)(2,1)} copy(bf16[1280,4096]{0,1:T(8,128)(2,1)} %fusion.19) | data formatting | bytes 20971520 | tf_op jit(solution)/shard_map/concatenate | solution.py:987
  605.4 6.5 convolution_convert_fusion
  611.9 101.4 %shard_map.236 = (f32[40,4096]{1,0:T(8,128)}, f32[40,3840]{1,0:T(8,128)}) custom-call(bf16[2,2,4,2,40,4096]{5,4,3,2,1,0:T(8,128)(2,1)} %bitcast.202, bf16[2,2,4,2,40,3840]{5,4,3,2,1,0:T(8,128)(2,1)} %bitcast.203), custom_call_target="tpu_custom_call" | custom-call | bytes 162529280 | tf_op jit(solution)/shard_map/pallas_call | solution.py:580
  (231 shorter events, 108.4 us)
Async XLA Ops:
  7.2 7.1 copy-start.35
  7.2 7.1 copy-start.36
  7.2 7.2 copy-start.37
  7.2 7.2 copy-start.19
  7.2 276.0 %all-gather.2.cloned.1.call-start = ((), (), s32[]{:S(2)}) async-start(), calls=%async_computation.2 | async-start | bytes 17203200 | tf_op jit(solution)/shard_map/all_gather | solution.py:849
  16.9 134.5 %copy-start.46 = (s32[1,4]{1,0:T(1,128)S(1)}, s32[1,4]{1,0:T(1,128)}, u32[]{:S(2)}) copy-start(s32[1,4]{1,0:T(1,128)} %param.16) | copy-start | bytes 52
  151.3 570.6 %reduce-scatter.3.cloned.1.call-start = ((), (), s32[]{:S(2)}) async-start(), calls=%async_computation.3 | async-start | bytes 4423680 | tf_op jit(solution)/shard_map/reduce_scatter | solution.py:933
  154.5 11.5 %copy-start.40 = (s32[1536]{0:T(1024)}, s32[1536]{0:T(1024)S(1)}, u32[]{:S(2)}) copy-start(s32[1536]{0:T(1024)S(1)} %select_reduce_fusion) | copy-start | bytes 18436
  155.6 10.4 %copy-start.33 = (f32[1280]{0:T(1024)}, f32[1280]{0:T(1024)S(1)}, u32[]{:S(2)}) copy-start(f32[1280]{0:T(1024)S(1)} %convert_reduce_fusion.2) | copy-start | bytes 15364
  155.6 52.6 %copy-start.38 = (f32[1280]{0:T(1024)}, f32[1280]{0:T(1024)S(1)}, u32[]{:S(2)}) copy-start(f32[1280]{0:T(1024)S(1)} %convert_reduce_fusion.1) | copy-start | bytes 15364
  192.6 12.0 %copy-start.5 = (bf16[1,192,1280]{2,1,0:T(8,128)(2,1)S(1)}, bf16[1,192,1280]{2,1,0:T(8,128)(2,1)}, u32[]{:S(2)}) copy-start(bf16[1,192,1280]{2,1,0:T(8,128)(2,1)} %param.14) | copy-start | bytes 1474564
  208.2 41.7 %copy-start.26 = (s32[8,192,7]{2,1,0:T(8,128)S(1)}, s32[8,192,7]{2,1,0:T(8,128)}, u32[]{:S(2)}) copy-start(s32[8,192,7]{2,1,0:T(8,128)} %get-tuple-element.32) | copy-start | bytes 129028
  208.2 41.7 %copy-start.43 = (f32[192]{0:T(256)}, f32[192]{0:T(256)S(1)}, u32[]{:S(2)}) copy-start(f32[192]{0:T(256)S(1)} %add_rsqrt_fusion.2) | copy-start | bytes 2308
  283.2 9.6 %copy-start = (bf16[8,192,1280]{2,1,0:T(8,128)(2,1)S(1)}, bf16[8,192,1280]{2,1,0:T(8,128)(2,1)}, u32[]{:S(2)}) copy-start(bf16[8,192,1280]{2,1,0:T(8,128)(2,1)} %shard_map.232) | copy-start | bytes 11796484
  283.2 9.6 %copy-start.45 = (bf16[3,2,1280,896]{3,2,1,0:T(8,128)(2,1)S(1)}, bf16[3,2,1280,896]{3,2,1,0:T(8,128)(2,1)}, u32[]{:S(2)}) copy-start(bf16[3,2,1280,896]{3,2,1,0:T(8,128)(2,1)} %all-gather.2.cloned.1.call-done) | copy-start | bytes 41287684
  321.3 54.1 %copy-start.49 = (bf16[1536,896]{1,0:T(8,128)(2,1)}, bf16[1536,896]{1,0:T(8,128)(2,1)S(1)}, u32[]{:S(2)}) copy-start(bf16[1536,896]{1,0:T(8,128)(2,1)S(1)} %get-tuple-element.101) | copy-start | bytes 8257540
  328.4 11.1 %copy-start.16 = (bf16[8,192,1280]{2,1,0:T(8,128)(2,1)S(1)}, bf16[8,192,1280]{2,1,0:T(8,128)(2,1)}, u32[]{:S(2)}) copy-start(bf16[8,192,1280]{2,1,0:T(8,128)(2,1)} %get-tuple-element.34) | copy-start | bytes 11796484
  339.5 11.5 %copy-start.53 = (bf16[1536,896]{1,0:T(8,128)(2,1)}, bf16[1536,896]{1,0:T(8,128)(2,1)S(1)}, u32[]{:S(2)}) copy-start(bf16[1536,896]{1,0:T(8,128)(2,1)S(1)} %get-tuple-element.105) | copy-start | bytes 8257540
  351.0 374.2 %reduce-scatter.5.cloned.1.call-start = ((), (), s32[]{:S(2)}) async-start(), calls=%async_computation.4 | async-start | bytes 17203200 | tf_op jit(solution)/shard_map/reduce_scatter | solution.py:935
  351.1 7.4 %copy-start.1 = (bf16[8,192,1280]{2,1,0:T(8,128)(2,1)S(1)}, bf16[8,192,1280]{2,1,0:T(8,128)(2,1)}, u32[]{:S(2)}) copy-start(bf16[8,192,1280]{2,1,0:T(8,128)(2,1)} %shard_map.232) | copy-start | bytes 11796484
  351.1 7.4 %copy-start.51 = (bf16[1536,896]{1,0:T(8,128)(2,1)S(1)}, bf16[1536,896]{1,0:T(8,128)(2,1)}, u32[]{:S(2)}) copy-start(bf16[1536,896]{1,0:T(8,128)(2,1)} %get-tuple-element.104) | copy-start | bytes 8257540
  407.8 10.3 %copy-start.47 = (bf16[192,896]{1,0:T(8,128)(2,1)}, bf16[192,896]{1,0:T(8,128)(2,1)S(1)}, u32[]{:S(2)}) copy-start(bf16[192,896]{1,0:T(8,128)(2,1)S(1)} %get-tuple-element.120) | copy-start | bytes 1032196
  424.4 7.8 %copy-start.55 = (bf16[1536,896]{1,0:T(8,128)(2,1)S(1)}, bf16[1536,896]{1,0:T(8,128)(2,1)}, u32[]{:S(2)}) copy-start(bf16[1536,896]{1,0:T(8,128)(2,1)} %get-tuple-element.100) | copy-start | bytes 8257540
  441.2 44.8 %copy-start.4 = (f32[192,1280]{1,0:T(8,128)S(1)}, f32[192,1280]{1,0:T(8,128)}, u32[]{:S(2)}) copy-start(f32[192,1280]{1,0:T(8,128)} %copy-done.3) | copy-start | bytes 2949124
  441.2 44.8 %copy-start.39 = (f32[1280]{0:T(1024)S(1)}, f32[1280]{0:T(1024)}, u32[]{:S(2)}) copy-start(f32[1280]{0:T(1024)} %copy-done.38) | copy-start | bytes 15364
  441.2 44.8 %copy-start.44 = (f32[192]{0:T(256)S(1)}, f32[192]{0:T(256)}, u32[]{:S(2)}) copy-start(f32[192]{0:T(256)} %copy-done.43) | copy-start | bytes 2308
  552.0 20.2 %copy-start.34 = (f32[1280]{0:T(1024)S(1)}, f32[1280]{0:T(1024)}, u32[]{:S(2)}) copy-start(f32[1280]{0:T(1024)} %copy-done.33) | copy-start | bytes 15364
  572.1 8.4 %copy-start.21 = (bf16[192,1280]{1,0:T(8,128)(2,1)}, bf16[192,1280]{1,0:T(8,128)(2,1)S(1)}, u32[]{:S(2)}) copy-start(bf16[192,1280]{1,0:T(8,128)(2,1)S(1)} %get-tuple-element.117) | copy-start | bytes 1474564
  572.1 8.4 %copy-start.23 = (bf16[192,1280]{1,0:T(8,128)(2,1)}, bf16[192,1280]{1,0:T(8,128)(2,1)S(1)}, u32[]{:S(2)}) copy-start(bf16[192,1280]{1,0:T(8,128)(2,1)S(1)} %get-tuple-element.118) | copy-start | bytes 1474564
  572.1 9.4 %copy-start.15 = (f32[192,1280]{1,0:T(8,128)S(1)}, f32[192,1280]{1,0:T(8,128)}, u32[]{:S(2)}) copy-start(f32[192,1280]{1,0:T(8,128)} %get-tuple-element.31) | copy-start | bytes 2949124
  591.0 14.3 %copy-start.22 = (bf16[192,1280]{1,0:T(8,128)(2,1)S(1)}, bf16[192,1280]{1,0:T(8,128)(2,1)}, u32[]{:S(2)}) copy-start(bf16[192,1280]{1,0:T(8,128)(2,1)} %copy-done.21) | copy-start | bytes 1474564
  713.3 8.6 %copy-start.30 = (bf16[192,896]{1,0:T(8,128)(2,1)S(1)}, bf16[192,896]{1,0:T(8,128)(2,1)}, u32[]{:S(2)}) copy-start(bf16[192,896]{1,0:T(8,128)(2,1)} %get-tuple-element.121) | copy-start | bytes 1032196
  (30 other events, 117.1 us)
Sparse Core Ops, SparseCore 0:
  151.4 131.7 all-gather.1
  351.2 47.5 reduce-scatter.2
  401.8 128.5 reduce-scatter.4

commit v2 on v1

--- a/solution.py
+++ b/solution.py
@@ -16,6 +16,7 @@
 BF = jnp.bfloat16
 F32 = jnp.float32
 VMEM_LIMIT = 56 * 1024 * 1024
+MOE_VMEM = 62 * 1024 * 1024
 
 
 def params(**kw):
@@ -138,8 +139,8 @@
         if a.full:
             a.s_side, a.r_side, a.s_half, a.r_half = sems[position : position + 4]
             position += 4
-            half = a.own.shape[-1] // 2
-            a.halves = (pl.ds(0, half), pl.ds(half, half))
+            cut = a.own.shape[-1] // 256 * 128
+            a.halves = (pl.ds(0, cut), pl.ds(cut, a.own.shape[-1] - cut))
         arrays.append(a)
 
     def slot(a, dd, zz, cc):
@@ -412,9 +413,11 @@
             i, first, wide = chunks[q]
             self.i, self.first, self.wide = i, first, wide
             self.q = q
-            self.mine, self.other, self.one, self.two, self.end = buffers[5 * q : 5 * q + 5]
+            self.mine, self.other, one_x, one_y, two_x, two_y, self.end = buffers[7 * q : 7 * q + 7]
+            self.one, self.two = (one_x, one_y), (two_x, two_y)
             self.cols = pl.ds(first, wide)
-            self.half = (pl.ds(0, wide // 2), pl.ds(wide // 2, wide // 2))
+            cut = wide // 256 * 128
+            self.half = (pl.ds(0, cut), pl.ds(cut, wide - cut))
 
         def load(self):
             return pltpu.make_async_copy(
@@ -433,7 +436,7 @@
         def first_x(self):
             return sent(
                 self.mine.at[:, 1 - x, :, :, self.half[0]],
-                self.one.at[0],
+                self.one[0],
                 s_one.at[self.q, 0],
                 r_one.at[self.q, 0],
                 at.across_x,
@@ -442,7 +445,7 @@
         def first_y(self):
             return sent(
                 self.mine.at[1 - y, :, :, :, self.half[1]],
-                self.one.at[1],
+                self.one[1],
                 s_one.at[self.q, 1],
                 r_one.at[self.q, 1],
                 at.across_y,
@@ -451,7 +454,7 @@
         def second_y(self):
             return sent(
                 self.mine.at[1 - y, x, :, :, self.half[0]],
-                self.two.at[0],
+                self.two[0],
                 s_two.at[self.q, 0],
                 r_two.at[self.q, 0],
                 at.across_y,
@@ -460,7 +463,7 @@
         def second_x(self):
             return sent(
                 self.mine.at[y, 1 - x, :, :, self.half[1]],
-                self.two.at[1],
+                self.two[1],
                 s_two.at[self.q, 1],
                 r_two.at[self.q, 1],
                 at.across_x,
@@ -504,10 +507,10 @@
             v, zz = k // chips, k % chips
             a, b = p.half
             p.mine[v, x, zz, :, a] = (
-                p.mine[v, x, zz, :, a].astype(F32) + p.one[0, v, zz].astype(F32)
+                p.mine[v, x, zz, :, a].astype(F32) + p.one[0][v, zz].astype(F32)
             ).astype(BF)
             p.mine[y, v, zz, :, b] = (
-                p.mine[y, v, zz, :, b].astype(F32) + p.one[1, v, zz].astype(F32)
+                p.mine[y, v, zz, :, b].astype(F32) + p.one[1][v, zz].astype(F32)
             ).astype(BF)
             return carry
 
@@ -523,7 +526,7 @@
             for w in (0, 1):
                 s = p.half[w]
                 p.mine[y, x, zz, :, s] = (
-                    p.mine[y, x, zz, :, s].astype(F32) + p.two[w, zz].astype(F32)
+                    p.mine[y, x, zz, :, s].astype(F32) + p.two[w][zz].astype(F32)
                 ).astype(BF)
             return carry
 
@@ -564,16 +567,19 @@
     dma = pltpu.SemaphoreType.DMA
     chunks = []
     for i, (array, wide) in enumerate(zip(arrays, chunk_widths)):
-        assert array.shape[1] % wide == 0 and wide % 256 == 0
+        assert array.shape[1] % wide == 0 and wide % 128 == 0 and wide >= 256
         chunks += [(i, first, wide) for first in range(0, array.shape[1], wide)]
     q = len(chunks)
     scratch = [dma((q,)), dma((q,)), dma((q,))] + [dma((q, 2))] * 4 + [dma((q, max(1, chips - 1)))] * 2
     for i, first, wide in chunks:
+        cut = wide // 256 * 128
         scratch += [
             pltpu.VMEM((2, 2, chips, block, wide), BF),
             pltpu.VMEM((2, 2, chips, block, wide), BF),
-            pltpu.VMEM((2, 2, chips, block, wide // 2), BF),
-            pltpu.VMEM((2, chips, block, wide // 2), BF),
+            pltpu.VMEM((2, chips, block, cut), BF),
+            pltpu.VMEM((2, chips, block, wide - cut), BF),
+            pltpu.VMEM((chips, block, cut), BF),
+            pltpu.VMEM((chips, block, wide - cut), BF),
             pltpu.VMEM((max(1, chips - 1), block, wide), BF),
         ]
     n = len(arrays)
@@ -783,6 +789,870 @@
     )
 
 
+def moe_kernel(
+    chips,
+    experts,
+    x_own,
+    routes,
+    grads,
+    misc,
+    weights,
+    row_out,
+    thin_out,
+    mid_out,
+    grad_out,
+    x_all,
+    g_all,
+    w,
+    hid,
+    part,
+    other,
+    came,
+    thin,
+    dots,
+    s_load,
+    s_x,
+    r_x,
+    s_fwd,
+    r_fwd,
+    s_part,
+    r_part,
+    s_came,
+    r_came,
+    s_thin,
+    r_thin,
+):
+    at = Place(chips)
+    z, c = at.z, at.c
+    chain = 2 * chips
+    rows, width = x_own.shape
+    both = w.shape[2]
+    tiles = both // 256
+    per_expert = both // 256
+    greet([(at.d, lax.rem(at.e + k, chain)) for k in range(1, chain)], [None] * (chain - 1))
+
+    near = jnp.minimum(z, chips - 1 - z)
+
+    def order(j):
+        step = (j + 1) // 2
+        around = jnp.where(j % 2 == 1, z - step, z + step)
+        return jnp.where(j <= 2 * near, around, jnp.where(2 * z < chips, j, chips - 1 - j))
+
+    def own_load():
+        return pltpu.make_async_copy(x_own, x_all.at[z, c], s_load.at[0])
+
+    hidden = both // EXP_DEV
+
+    def weight_load(k, e):
+        return pltpu.make_async_copy(
+            weights.at[k, e], w.at[k, :, pl.ds(e * hidden, hidden)], s_load.at[2 + 2 * k + e]
+        )
+
+    def grad_store(k, e):
+        return pltpu.make_async_copy(
+            w.at[k, :, pl.ds(e * hidden, hidden)], grad_out.at[k, e], s_load.at[2 + 2 * k + e]
+        )
+
+    def grads_load():
+        return pltpu.make_async_copy(grads, g_all, s_load.at[1])
+
+    def x_send(zz):
+        return sent(x_own, x_all.at[z, c], s_x.at[zz], r_x.at[z], (at.d, 2 * zz + c))
+
+    def x_came(zz):
+        ref = x_all.at[zz, c]
+        return sent(ref, ref, s_x.at[zz], r_x.at[zz], (at.d, 2 * zz + c))
+
+    def forward(zz):
+        ref = x_all.at[zz, c]
+        return sent(ref, ref, s_fwd.at[zz], r_fwd.at[zz], at.sibling)
+
+    def forwarded(zz):
+        ref = x_all.at[zz, 1 - c]
+        return sent(ref, ref, s_fwd.at[zz], r_fwd.at[zz], at.sibling)
+
+    def part_send(zz):
+        return sent(part.at[zz, 1 - c], other.at[zz], s_part.at[zz], r_part.at[zz], at.sibling)
+
+    def came_send(zz):
+        return sent(part.at[zz, c], came.at[z], s_came.at[zz], r_came.at[z], (at.d, 2 * zz + c))
+
+    def came_here(zz):
+        return sent(part.at[zz, c], came.at[zz], s_came.at[zz], r_came.at[zz], (at.d, 2 * zz + c))
+
+    def thin_send(zz, cc):
+        return sent(
+            thin.at[zz], thin_out.at[at.e], s_thin.at[2 * zz + cc], r_thin.at[at.e], (at.d, 2 * zz + cc)
+        )
+
+    def thin_here(e):
+        return sent(thin.at[0], thin_out.at[e], s_thin.at[e], r_thin.at[e], (at.d, e))
+
+    own_load().start()
+    sent(x_own, x_all.at[z, c], s_fwd.at[z], r_fwd.at[z], at.sibling).start()
+    for j in range(1, chips):
+        x_send(order(j)).start()
+    for k in range(3):
+        for e in range(EXP_DEV):
+            weight_load(k, e).start()
+    grads_load().start()
+    own_load().wait()
+
+    lanes = lax.broadcasted_iota(jnp.int32, (2 * rows, 128), 1)
+
+    def gates_of(zz, x):
+        logits = jnp.where(lanes < experts, nn(x, misc[...]), NEG)
+        powers = jnp.exp(logits - jnp.max(logits, axis=1, keepdims=True))
+        probs = powers / jnp.sum(powers, axis=1, keepdims=True)
+        named = routes[zz][:, 0:1] == lanes
+        for j in range(1, TOP):
+            named = named | (routes[zz][:, j : j + 1] == lanes)
+        chosen = jnp.where(named, probs, 0.0)
+        gates = chosen / jnp.sum(chosen, axis=1, keepdims=True)
+        return [
+            jnp.sum(jnp.where(lanes == EXP_DEV * at.e + k, gates, 0.0), axis=1, keepdims=True)
+            for k in range(EXP_DEV)
+        ]
+
+    def settle(zz):
+        part_send(zz).wait_recv()
+        total = part[zz, c].astype(F32) + other[zz].astype(F32)
+
+        @pl.when(zz == z)
+        def _():
+            row_out[...] = total
+
+        @pl.when(zz != z)
+        def _():
+            part[zz, c] = total.astype(BF)
+            came_send(zz).start()
+
+    def block(j, carry):
+        zz = order(j)
+        forwarded(zz).wait_recv()
+        here = pl.ds(pl.multiple_of(zz * 2 * rows, 2 * rows), 2 * rows)
+        x = x_all[zz].reshape(2 * rows, width)
+        first, second = gates_of(zz, x)
+        dots[...] = jnp.zeros_like(dots)
+
+        @pl.when(j == 0)
+        def _():
+            for k in range(3):
+                for e in range(EXP_DEV):
+                    weight_load(k, e).wait()
+            grads_load().wait()
+
+        def tile(n, carry):
+            cols = pl.ds(pl.multiple_of(n * 256, 256), 256)
+            x = x_all[zz].reshape(2 * rows, width)
+            g = g_all[zz].reshape(2 * rows, width)
+            gate_v = nn(x, w[0, :, cols])
+            up_v = nn(x, w[1, :, cols])
+            back = nn(g, w[2, :, cols])
+            for half in (0, 1):
+                s = slice(half * 128, half * 128 + 128)
+                is_first = 2 * n + half < per_expert
+                gate = jnp.where(is_first, first, second)
+                v, u, b = gate_v[:, s], up_v[:, s], back[:, s]
+                sig = jax.nn.sigmoid(v)
+                act = v * sig
+                mid = act * u
+                dots[0] += mid * b * is_first.astype(F32)
+                dots[1] += mid * b * (1.0 - is_first.astype(F32))
+                b = gate * b
+                to = pl.ds(pl.multiple_of(n * 256 + half * 128, 128), 128)
+                hid[2, here, to] = (gate * mid).astype(BF)
+                hid[0, here, to] = (b * u * (sig * (1.0 + v * (1.0 - sig)))).astype(BF)
+                hid[1, here, to] = (b * act).astype(BF)
+            return carry
+
+        early = (tiles + 1) // 2
+        lax.fori_loop(0, early, tile, 0, unroll=True)
+
+        @pl.when(j + 1 < chips)
+        def _():
+            x_came(order(j + 1)).wait_recv()
+            forward(order(j + 1)).start()
+
+        @pl.when(j > 0)
+        def _():
+            settle(order(j - 1))
+
+        lax.fori_loop(early, tiles, tile, 0, unroll=True)
+
+        def row_tile(n, carry):
+            cols = pl.ds(pl.multiple_of(n * 256, 256), 256)
+            row = nt(hid[0, here, :], w[0, cols, :]) + nt(hid[1, here, :], w[1, cols, :])
+            part[zz, 0, :, cols] = row[:rows].astype(BF)
+            part[zz, 1, :, cols] = row[rows:].astype(BF)
+            return carry
+
+        lax.fori_loop(0, width // 256, row_tile, 0, unroll=True)
+        part_send(zz).start()
+        column = jnp.where(
+            lanes == 0,
+            jnp.sum(dots[0], axis=1, keepdims=True),
+            jnp.sum(dots[1], axis=1, keepdims=True),
+        )
+        thin[zz] = column.T[:8]
+
+        @pl.when(zz == z)
+        def _():
+            thin_out[at.e] = thin[zz]
+
+        for cc in (0, 1):
+
+            @pl.when(2 * zz + cc != at.e)
+            def _(cc=cc):
+                thin_send(zz, cc).start()
+
+        return carry
+
+    lax.fori_loop(0, chips, block, 0)
+    settle(order(chips - 1))
+    mid_store = pltpu.make_async_copy(hid.at[2], mid_out, s_load.at[0])
+    mid_store.start()
+    for k in (2, 0, 1):
+
+        def grad_tile(n, carry, k=k):
+            cols = pl.ds(pl.multiple_of(n * 256, 256), 256)
+            left = g_all if k == 2 else x_all
+            left = left[...].reshape(chain * rows, width)
+            w[k, :, cols] = tn(left, hid[k, :, cols]).astype(BF)
+            return carry
+
+        lax.fori_loop(0, tiles, grad_tile, 0, unroll=True)
+        for e in range(EXP_DEV):
+            grad_store(k, e).start()
+
+    for zz in range(chips):
+
+        @pl.when(zz != z)
+        def _(zz=zz):
+            came_here(zz).wait_recv()
+            row_out[...] += came[zz].astype(F32)
+            came_send(zz).wait_send()
+            x_send(zz).wait_send()
+
+        part_send(zz).wait_send()
+        forward(zz).wait_send()
+        for cc in (0, 1):
+
+            @pl.when(2 * zz + cc != at.e)
+            def _(zz=zz, cc=cc):
+                thin_here(2 * zz + cc).wait_recv()
+                thin_send(zz, cc).wait_send()
+
+    mid_store.wait()
+    for k in range(3):
+        for e in range(EXP_DEV):
+            grad_store(k, e).wait()
+
+
+def moe_fused(normed, routes_all, grads_all, misc, weights, experts, collective_id):
+    rows, width = normed.shape
+    chain = routes_all.shape[0] // rows
+    chips = chain // 2
+    both = EXP_DEV * weights.shape[3]
+    dma = pltpu.SemaphoreType.DMA
+    blocks = (chips, 2, rows, width)
+    anywhere = pl.BlockSpec(memory_space=pl.ANY)
+    vmem = pl.BlockSpec(memory_space=pltpu.VMEM)
+    return pl.pallas_call(
+        functools.partial(moe_kernel, chips, experts),
+        out_shape=[
+            jax.ShapeDtypeStruct((rows, width), F32),
+            jax.ShapeDtypeStruct((chain, 8, 2 * rows), F32),
+            jax.ShapeDtypeStruct((chain * rows, both), BF),
+            jax.ShapeDtypeStruct(weights.shape, BF),
+        ],
+        in_specs=[anywhere, vmem, anywhere, vmem, anywhere],
+        out_specs=[vmem, vmem, anywhere, anywhere],
+        scratch_shapes=[
+            pltpu.VMEM(blocks, BF),
+            pltpu.VMEM(blocks, BF),
+            pltpu.VMEM((3, width, both), BF),
+            pltpu.VMEM((3, chain * rows, both), BF),
+            pltpu.VMEM(blocks, BF),
+            pltpu.VMEM((chips, rows, width), BF),
+            pltpu.VMEM((chips, rows, width), BF),
+            pltpu.VMEM((chips, 8, 2 * rows), F32),
+            pltpu.VMEM((2, 2 * rows, 128), F32),
+            dma((8,)),
+        ]
+        + [dma((chips,))] * 8
+        + [dma((chain,))] * 2,
+        compiler_params=pltpu.CompilerParams(
+            vmem_limit_bytes=MOE_VMEM, collective_id=collective_id, has_side_effects=True
+        ),
+        cost_estimate=pl.CostEstimate(
+            flops=16 * chain * rows * width * both,
+            bytes_accessed=4 * weights.size + 4 * chain * rows * both,
+            transcendentals=chain * rows * both,
+        ),
+    )(
+        normed,
+        routes_all.reshape(chips, 2 * rows, TOP),
+        grads_all.reshape(blocks),
+        misc,
+        weights,
+    )
+
+
+def moe_plain(moe_all, gates_here, grads_all, weights):
+    keys, width = moe_all.shape
+    hidden = weights.shape[3]
+    at_once = 768 if keys % 768 == 0 else keys
+
+    def some(rows):
+        x, gates, g = rows
+        row = jnp.zeros(x.shape, F32)
+        dots, mids, gate_vs, up_vs = [], [], [], []
+        for e in range(EXP_DEV):
+            scale = gates[:, e : e + 1]
+            gate_v = nn(x, weights[0, e])
+            up_v = nn(x, weights[1, e])
+            back = nn(g, weights[2, e])
+            act, slope = silu_parts(gate_v)
+            mid = act * up_v
+            dots.append(jnp.sum(mid * back, axis=1))
+            back = back * scale
+            gate_vs.append((back * up_v * slope).astype(BF))
+            up_vs.append((back * act).astype(BF))
+            mids.append((mid * scale).astype(BF))
+            row = row + nt(gate_vs[e], weights[0, e]) + nt(up_vs[e], weights[1, e])
+        return (
+            row.astype(BF),
+            jnp.stack(dots, axis=1),
+            jnp.concatenate(mids, axis=1),
+            jnp.concatenate(gate_vs, axis=1),
+            jnp.concatenate(up_vs, axis=1),
+        )
+
+    cut = jax.tree.map(
+        lambda a: a.reshape((keys // at_once, at_once) + a.shape[1:]), (moe_all, gates_here, grads_all)
+    )
+    row, dots, mid, gate_v, up_v = jax.tree.map(
+        lambda a: a.reshape((keys,) + a.shape[2:]), lax.map(some, cut)
+    )
+
+    def grad_of(x, h):
+        grad = tn(x, h).astype(BF).reshape(width, EXP_DEV, hidden)
+        return jnp.swapaxes(grad, 0, 1)
+
+    weight_grads = jnp.stack(
+        [grad_of(moe_all, gate_v), grad_of(moe_all, up_v), grad_of(grads_all, mid)]
+    )
+    return row, dots, mid, weight_grads
+
+
+def spread_kernel(
+    chips,
+    own,
+    side,
+    mid,
+    weights,
+    rows_in,
+    gate_in,
+    up_in,
+    cot_in,
+    shared_in,
+    attn_in,
+    attended_in,
+    all_out,
+    side_out,
+    mix_out,
+    gate_out,
+    up_out,
+    down_out,
+    out_out,
+    mids,
+    w,
+    mix,
+    dense,
+    wide,
+    s_load,
+    s_dense,
+    s_chain,
+    r_chain,
+    s_core,
+    r_core,
+    s_side,
+    r_side,
+    s_score,
+    r_score,
+):
+    at = Place(chips)
+    z, c = at.z, at.c
+    hidden = gate_in.shape[1]
+    rows = own.shape[0]
+    others = [(at.d, 2 * lax.rem(z + k, chips) + c) for k in range(1, chips)]
+    greet([at.sibling] + others, [None] * chips)
+
+    pairs = ((own, all_out, s_chain, r_chain, s_core, r_core), (side, side_out, s_side, r_side, s_score, r_score))
+
+    def along(p, k, src=None):
+        source, out, ss, rs = pairs[p][:4]
+        zz = lax.rem(z + k, chips)
+        ref = out.at[2 * z + c]
+        return sent(source if src is None else src, ref, ss.at[zz], rs.at[z], (at.d, 2 * zz + c))
+
+    def along_here(p, zz):
+        source, out, ss, rs = pairs[p][:4]
+        ref = out.at[2 * zz + c]
+        return sent(ref, ref, ss.at[zz], rs.at[zz], (at.d, 2 * zz + c))
+
+    def over(p, zz, core, src=None):
+        out, ss, rs = pairs[p][1], pairs[p][4], pairs[p][5]
+        ref = out.at[2 * zz + core]
+        return sent(ref if src is None else src, ref, ss.at[zz], rs.at[zz], at.sibling)
+
+    near = jnp.minimum(z, chips - 1 - z)
+
+    def order(j):
+        step = (j + 1) // 2
+        around = jnp.where(j % 2 == 1, z - step, z + step)
+        return jnp.where(j <= 2 * near, around, jnp.where(2 * z < chips, j, chips - 1 - j))
+
+    for j in range(1, chips):
+        for p in (1, 0):
+            along(p, lax.rem(order(j) - z + chips, chips)).start()
+    locals_ = []
+    for p in (1, 0):
+        over(p, z, c, pairs[p][0]).start()
+        copy = pltpu.make_async_copy(pairs[p][0], pairs[p][1].at[2 * z + c], s_load.at[p])
+        copy.start()
+        locals_.append(copy)
+    loads = [
+        pltpu.make_async_copy(weights.at[2, e], w.at[:, pl.ds(e * hidden, hidden)], s_load.at[2 + e])
+        for e in range(EXP_DEV)
+    ]
+    loads.append(pltpu.make_async_copy(mid, mids, s_load.at[2 + EXP_DEV]))
+    for copy in loads:
+        copy.start()
+
+    stores = []
+    dense[0] = tn(rows_in[...], gate_in[...]).astype(BF)
+    dense[1] = tn(rows_in[...], up_in[...]).astype(BF)
+    dense[2] = tn(cot_in[...], shared_in[...]).astype(BF)
+    wide[...] = tn(attn_in[...], attended_in[...]).astype(BF)
+    for k, (src, dst) in enumerate(
+        ((dense.at[0], gate_out), (dense.at[1], up_out), (dense.at[2], down_out), (wide, out_out))
+    ):
+        copy = pltpu.make_async_copy(src, dst, s_dense.at[k])
+        copy.start()
+        stores.append(copy)
+    for copy in loads:
+        copy.wait()
+
+    def mix_chip(zz):
+        here = pl.ds(zz * 2 * rows, 2 * rows)
+        for n in range(0, own.shape[1], 256):
+            tile = nt(mids[here, :], w[n : n + 256, :]).astype(BF)
+            mix[zz, 0, :, n : n + 256] = tile[:rows]
+            mix[zz, 1, :, n : n + 256] = tile[rows:]
+        copy = pltpu.make_async_copy(mix.at[zz], mix_out.at[zz], s_dense.at[4 + zz])
+        copy.start()
+        stores.append(copy)
+
+    for j in range(chips):
+        mix_chip(j)
+        if j >= 1:
+            zz = order(j)
+            for p in (1, 0):
+                along_here(p, zz).wait_recv()
+                over(p, zz, c).start()
+    for p in (1, 0):
+        for zz in range(chips):
+            over(p, zz, 1 - c).wait_recv()
+            over(p, zz, c).wait_send()
+
+            @pl.when(zz != z)
+            def _(p=p, zz=zz):
+                along_here(p, zz).wait_send()
+
+    for copy in locals_ + stores:
+        copy.wait()
+
+
+def spread(own, side, mid, weights, normed, gate_grad, up_grad, cot, shared_mid, attn, attended, collective_id):
+    rows, width = own.shape
+    keys, both = mid.shape
+    chain = keys // rows
+    chips = chain // 2
+    hidden = gate_grad.shape[1]
+    dma = pltpu.SemaphoreType.DMA
+    anywhere = pl.BlockSpec(memory_space=pl.ANY)
+    vmem = pl.BlockSpec(memory_space=pltpu.VMEM)
+    return pl.pallas_call(
+        functools.partial(spread_kernel, chips),
+        out_shape=[
+            jax.ShapeDtypeStruct((chain,) + own.shape, BF),
+            jax.ShapeDtypeStruct((chain,) + side.shape, F32),
+            jax.ShapeDtypeStruct((chips, 2, rows, width), BF),
+            jax.ShapeDtypeStruct((width, hidden), BF),
+            jax.ShapeDtypeStruct((width, hidden), BF),
+            jax.ShapeDtypeStruct((width, hidden), BF),
+            jax.ShapeDtypeStruct((width, width), BF),
+        ],
+        in_specs=[anywhere] * 4 + [vmem] * 7,
+        out_specs=[anywhere] * 7,
+        scratch_shapes=[
+            pltpu.VMEM((keys, both), BF),
+            pltpu.VMEM((width, both), BF),
+            pltpu.VMEM((chips, 2, rows, width), BF),
+            pltpu.VMEM((3, width, hidden), BF),
+            pltpu.VMEM((width, width), BF),
+            dma((3 + EXP_DEV,)),
+            dma((4 + chips,)),
+        ]
+        + [dma((chips,))] * 8,
+        compiler_params=params(collective_id=collective_id, has_side_effects=True),
+        cost_estimate=pl.CostEstimate(
+            flops=2 * keys * both * width, bytes_accessed=64 * keys * width, transcendentals=0
+        ),
+    )(own, side, mid, weights, normed, gate_grad, up_grad, cot, shared_mid, attn, attended)
+
+
+def finish_kernel(chips, chunks, n_in, experts, *refs):
+    ins = refs[:n_in]
+    normed, projected, weight_in, misc_in, unit, inverse, gain, grad_middle, mix_in, base = refs[
+        n_in : n_in + 10
+    ]
+    n_out = n_in + 2
+    outs = refs[n_in + 10 : n_in + 10 + n_out]
+    input_out, output_out = refs[n_in + 10 + n_out : n_in + 12 + n_out]
+    rest = refs[n_in + 12 + n_out :]
+    s_in, s_core, r_core, s_one, r_one, s_two, r_two, s_end, r_end = rest[:9]
+    s_mix, s_mcore, r_mcore, s_mchain, r_mchain, s_weight = rest[9:15]
+    weight, grad_ref, tile_ref, mix_mine, mix_other, mix_came = rest[15:21]
+    buffers = rest[21:]
+    n_chunks = len(chunks)
+    at = Place(chips)
+    z, c, x, y = at.z, at.c, at.x, at.y
+    chain = 2 * chips
+    others = [(at.d, 2 * lax.rem(z + k, chips) + c) for k in range(1, chips)]
+    devices = [at.sibling, at.across_x, at.across_y] + others
+    greet(devices, [None] * len(devices))
+
+    class Chunk:
+        def __init__(self, q):
+            self.i, self.first, self.wide = chunks[q]
+            self.q = q
+            self.made = self.i >= n_in
+            self.mine, self.other, one_x, one_y, two_x, two_y, self.end, self.give = buffers[
+                8 * q : 8 * q + 8
+            ]
+            self.one, self.two = (one_x, one_y), (two_x, two_y)
+            self.cols = pl.ds(self.first, self.wide)
+            cut = self.wide // 256 * 128
+            self.half = (pl.ds(0, cut), pl.ds(cut, self.wide - cut))
+
+        def load(self):
+            return pltpu.make_async_copy(
+                ins[self.i].at[:, :, :, c, :, self.cols], self.mine, s_in.at[self.q]
+            )
+
+        def core(self):
+            source = self.give if self.made else ins[self.i].at[:, :, :, 1 - c, :, self.cols]
+            return sent(source, self.other, s_core.at[self.q], r_core.at[self.q], at.sibling)
+
+        def first_x(self):
+            return sent(
+                self.mine.at[:, 1 - x, :, :, self.half[0]],
+                self.one[0],
+                s_one.at[self.q, 0],
+                r_one.at[self.q, 0],
+                at.across_x,
+            )
+
+        def first_y(self):
+            return sent(
+                self.mine.at[1 - y, :, :, :, self.half[1]],
+                self.one[1],
+                s_one.at[self.q, 1],
+                r_one.at[self.q, 1],
+                at.across_y,
+            )
+
+        def second_y(self):
+            return sent(
+                self.mine.at[1 - y, x, :, :, self.half[0]],
+                self.two[0],
+                s_two.at[self.q, 0],
+                r_two.at[self.q, 0],
+                at.across_y,
+            )
+
+        def second_x(self):
+            return sent(
+                self.mine.at[y, 1 - x, :, :, self.half[1]],
+                self.two[1],
+                s_two.at[self.q, 1],
+                r_two.at[self.q, 1],
+                at.across_x,
+            )
+
+        def last(self, k):
+            zz = lax.rem(z + k, chips)
+            return sent(
+                self.mine.at[y, x, zz],
+                self.end.at[k - 1],
+                s_end.at[self.q, k - 1],
+                r_end.at[self.q, k - 1],
+                (at.d, 2 * zz + c),
+            )
+
+        def take(self):
+            block = self.mine.shape[3]
+
+            def body(k, carry):
+                yy, xx, zz = k // (2 * chips), (k // chips) % 2, k % chips
+                row = (2 * yy + xx) * chain + 2 * zz
+                keep = pl.ds(pl.multiple_of((row + c) * block, block), block)
+                away = pl.ds(pl.multiple_of((row + 1 - c) * block, block), block)
+                self.mine[yy, xx, zz] = tile_ref[keep, : self.wide].astype(BF)
+                self.give[yy, xx, zz] = tile_ref[away, : self.wide].astype(BF)
+                return carry
+
+            lax.fori_loop(0, 4 * chips, body, 0)
+            self.core().start()
+
+    parts = [Chunk(q) for q in range(n_chunks)]
+
+    def stage_one(p):
+        p.core().wait_recv()
+        if not p.made:
+            p.load().wait()
+
+        def body(k, carry):
+            yy, xx, zz = k // (2 * chips), (k // chips) % 2, k % chips
+            p.mine[yy, xx, zz] = (
+                p.mine[yy, xx, zz].astype(F32) + p.other[yy, xx, zz].astype(F32)
+            ).astype(BF)
+            return carry
+
+        lax.fori_loop(0, 4 * chips, body, 0)
+        p.first_x().start()
+        p.first_y().start()
+
+    def stage_two(p):
+        p.first_x().wait_recv()
+        p.first_y().wait_recv()
+
+        def body(k, carry):
+            v, zz = k // chips, k % chips
+            a, b = p.half
+            p.mine[v, x, zz, :, a] = (
+                p.mine[v, x, zz, :, a].astype(F32) + p.one[0][v, zz].astype(F32)
+            ).astype(BF)
+            p.mine[y, v, zz, :, b] = (
+                p.mine[y, v, zz, :, b].astype(F32) + p.one[1][v, zz].astype(F32)
+            ).astype(BF)
+            return carry
+
+        lax.fori_loop(0, 2 * chips, body, 0)
+        p.second_y().start()
+        p.second_x().start()
+
+    def stage_three(p):
+        p.second_y().wait_recv()
+        p.second_x().wait_recv()
+
+        def body(zz, carry):
+            for w in (0, 1):
+                s = p.half[w]
+                p.mine[y, x, zz, :, s] = (
+                    p.mine[y, x, zz, :, s].astype(F32) + p.two[w][zz].astype(F32)
+                ).astype(BF)
+            return carry
+
+        lax.fori_loop(0, chips, body, 0)
+        for k in range(1, chips):
+            p.last(k).start()
+
+    def stage_four(p):
+        total = p.mine[y, x, z].astype(F32)
+        for k in range(1, chips):
+            p.last(k).wait_recv()
+            total = total + p.end[k - 1].astype(F32)
+        outs[p.i][:, p.first : p.first + p.wide] = total
+
+    def mix_load(zz):
+        return pltpu.make_async_copy(mix_in.at[zz, c], mix_mine.at[zz], s_mix.at[zz])
+
+    def mix_core(zz):
+        return sent(
+            mix_in.at[zz, 1 - c], mix_other.at[zz], s_mcore.at[zz], r_mcore.at[zz], at.sibling
+        )
+
+    def mix_over(k):
+        zz = lax.rem(z + k, chips)
+        return sent(
+            mix_mine.at[zz], mix_came.at[k], s_mchain.at[k], r_mchain.at[k], (at.d, 2 * zz + c)
+        )
+
+    def mix_settle():
+        for k in range(1, chips):
+            zz = lax.rem(z + k, chips)
+            mix_core(zz).wait_recv()
+            mix_load(zz).wait()
+            mix_mine[zz] = (mix_mine[zz].astype(F32) + mix_other[zz].astype(F32)).astype(BF)
+            mix_over(k).start()
+        mix_core(z).wait_recv()
+        mix_load(z).wait()
+
+    part = projected.shape[2]
+
+    def weight_load(k):
+        return pltpu.make_async_copy(
+            weight_in.at[:, pl.ds(k * part, part)], weight, s_weight.at[0]
+        )
+
+    def input_grads(k):
+        weight_load(k).wait()
+        if k == 0:
+            grad_ref[...] = nt(projected[0], weight[...])
+        else:
+            grad_ref[...] += nt(projected[k], weight[...])
+        if k < 2:
+            weight_load(k + 1).start()
+            return
+        grad = grad_ref[...]
+        gains = jnp.sum(grad * unit[...], axis=0, keepdims=True)
+        column = jnp.broadcast_to(gains, (8, part)).T[:, :1]
+        lanes = lax.broadcasted_iota(jnp.int32, misc_in.shape, 1)
+        tile_ref[:, : misc_in.shape[1]] = jnp.where(lanes == experts, column, misc_in[...])
+        scaled = grad * gain[...]
+        mean = jnp.mean(scaled * unit[...], axis=1, keepdims=True)
+        input_out[...] = (grad_middle[...] + inverse[...] * (scaled - unit[...] * mean)).astype(BF)
+
+    for p in parts:
+        if not p.made:
+            p.core().start()
+            p.load().start()
+    weight_load(0).start()
+    for zz in range(chips):
+        mix_core(zz).start()
+        mix_load(zz).start()
+    n_known = sum(not p.made for p in parts)
+    for p in parts[n_known:-1]:
+        k, first = p.first // projected.shape[2], p.first % projected.shape[2]
+        tile_ref[:, : p.wide] = tn(normed[...], projected[k, :, first : first + p.wide])
+        p.take()
+    stages = (stage_one, stage_two, stage_three, stage_four)
+    for t in range(n_chunks + len(stages) - 1):
+        for s, stage in enumerate(stages):
+            if 0 <= t - s < n_chunks:
+                stage(parts[t - s])
+        if t == 1:
+            mix_settle()
+        if t < 3:
+            input_grads(t)
+        if t == 2:
+            parts[-1].take()
+    total = base[...] + mix_mine[z].astype(F32) + mix_other[z].astype(F32)
+    for k in range(1, chips):
+        mix_over(k).wait_recv()
+        total = total + mix_came[k].astype(F32)
+    output_out[...] = total.astype(BF)
+    for p in parts:
+        p.core().wait_send()
+        p.first_x().wait_send()
+        p.first_y().wait_send()
+        p.second_x().wait_send()
+        p.second_y().wait_send()
+        for k in range(1, chips):
+            p.last(k).wait_send()
+    for k in range(1, chips):
+        mix_over(k).wait_send()
+    for zz in range(chips):
+        mix_core(zz).wait_send()
+
+
+def finish(
+    arrays,
+    chunk_widths,
+    experts,
+    normed,
+    projected,
+    qkv_weight,
+    misc,
+    unit,
+    inverse,
+    gain,
+    grad_middle,
+    mix,
+    base,
+    collective_id,
+):
+    chain = lax.axis_size("expert")
+    chips = chain // 2
+    width = arrays[0].shape[0]
+    block = width // (4 * chain)
+    rows = normed.shape[0]
+    columns = qkv_weight.shape[1]
+    n = len(arrays)
+    dma = pltpu.SemaphoreType.DMA
+    sizes = [a.shape[1] for a in arrays] + [columns, misc.shape[1]]
+    chunks = []
+    for i, (size, wide) in enumerate(zip(sizes, chunk_widths)):
+        assert size % wide == 0 and wide % 128 == 0 and wide >= 256
+        chunks += [(i, first, wide) for first in range(0, size, wide)]
+    q = len(chunks)
+    scratch = [dma((q,)), dma((q,)), dma((q,))] + [dma((q, 2))] * 4 + [dma((q, chips - 1))] * 2
+    scratch += [dma((chips,))] * 5 + [dma((1,))]
+    scratch += [
+        pltpu.VMEM((width, columns // 3), BF),
+        pltpu.VMEM((rows, width), F32),
+        pltpu.VMEM((width, max(chunk_widths[n:])), F32),
+        pltpu.VMEM((chips, rows, width), BF),
+        pltpu.VMEM((chips, rows, width), BF),
+        pltpu.VMEM((chips, rows, width), BF),
+    ]
+    for i, first, wide in chunks:
+        cut = wide // 256 * 128
+        scratch += [
+            pltpu.VMEM((2, 2, chips, block, wide), BF),
+            pltpu.VMEM((2, 2, chips, block, wide), BF),
+            pltpu.VMEM((2, chips, block, cut), BF),
+            pltpu.VMEM((2, chips, block, wide - cut), BF),
+            pltpu.VMEM((chips, block, cut), BF),
+            pltpu.VMEM((chips, block, wide - cut), BF),
+            pltpu.VMEM((chips - 1, block, wide), BF),
+            pltpu.VMEM((2, 2, chips, block, wide) if i >= n else (16, 128), BF),
+        ]
+    anywhere = pl.BlockSpec(memory_space=pl.ANY)
+    vmem = pl.BlockSpec(memory_space=pltpu.VMEM)
+    return pl.pallas_call(
+        functools.partial(finish_kernel, chips, tuple(chunks), n, experts),
+        out_shape=[jax.ShapeDtypeStruct((block, size), F32) for size in sizes]
+        + [jax.ShapeDtypeStruct((rows, width), BF)] * 2,
+        in_specs=[anywhere] * n
+        + [vmem, vmem, anywhere, vmem, vmem, vmem, vmem, vmem, anywhere, vmem],
+        out_specs=[vmem] * (n + 4),
+        scratch_shapes=scratch,
+        compiler_params=pltpu.CompilerParams(
+            vmem_limit_bytes=MOE_VMEM, collective_id=collective_id, has_side_effects=True
+        ),
+        cost_estimate=pl.CostEstimate(
+            flops=4 * rows * width * columns, bytes_accessed=64 * width * columns, transcendentals=0
+        ),
+    )(
+        *[a.reshape(2, 2, chips, 2, block, a.shape[1]) for a in arrays],
+        normed,
+        projected,
+        qkv_weight,
+        misc,
+        unit,
+        inverse,
+        gain,
+        grad_middle,
+        mix,
+        base,
+    )
+
+
 def silu_parts(values):
     s = jax.nn.sigmoid(values)
     return values * s, s * (1.0 + values * (1.0 - s))
@@ -818,36 +1688,28 @@
     route_pad = 128 * (-(-(experts + 2) // 128))
     misc = jnp.concatenate([router.astype(BF), gains.astype(BF).T], axis=1)
     misc = jnp.pad(misc, ((0, 0), (0, route_pad - experts - 2)))
-    rest = jnp.concatenate(
-        [
-            misc,
-            attn_out.astype(BF).T,
-            shared_gate.astype(BF),
-            shared_up.astype(BF),
-            shared_down.astype(BF).T,
-        ],
-        axis=1,
+    near = jnp.concatenate([misc, attn_out.astype(BF).T], axis=1)
+    expert_shard = jnp.stack(
+        [expert_gate.astype(BF), expert_up.astype(BF), jnp.swapaxes(expert_down.astype(BF), 1, 2)]
     )
-    qkv_weight, rest, tokens_all, routes_all, grads_all = gather(
-        [attn_qkv.astype(BF), rest], [tokens[0], routes[0], cotangent[0]], 0
+    expert_weight = lax.all_gather(expert_shard, "dp", axis=2, tiled=True)
+    qkv_weight, near, tokens_all, routes_all, grads_all = gather(
+        [attn_qkv.astype(BF), near], [tokens[0], routes[0], cotangent[0]], 0
     )
+    grads_all = grads_all.reshape(keys, width)
     qkv_weight = qkv_weight.reshape(width, 3 * H * HD)
-    rest = rest.reshape(width, rest.shape[-1])
+    near = near.reshape(width, near.shape[-1])
     tokens_all = tokens_all.reshape(keys, width)
     routes_all = routes_all.reshape(keys, TOP)
-    grads_all = grads_all.reshape(keys, width)
     cuts = [route_pad, route_pad + width]
     cuts += [cuts[-1] + hidden, cuts[-1] + 2 * hidden]
-    misc, out_t, gate_shared, up_shared, down_t = jnp.split(rest, cuts, axis=1)
+    misc, out_t = jnp.split(near, cuts[:1], axis=1)
     route_weight = misc[:, :experts]
     gain_attn = misc[:, experts].astype(F32)
     gain_moe = misc[:, experts + 1].astype(F32)
-    expert_shard = jnp.stack(
-        [expert_gate.astype(BF), expert_up.astype(BF), jnp.swapaxes(expert_down.astype(BF), 1, 2)]
+    shared = jnp.concatenate(
+        [shared_gate.astype(BF), shared_up.astype(BF), shared_down.astype(BF).T], axis=1
     )
-    expert_shard, tokens_all = lax.optimization_barrier((expert_shard, tokens_all))
-    expert_weight = lax.all_gather(expert_shard, "dp", axis=2, tiled=True)
-
     first_all, rope_all = doc_starts_of(lengths[0], jnp.arange(keys, dtype=jnp.int32))
     first_own = lax.dynamic_slice_in_dim(first_all, own_first, rows, 0)
     cosine, sine = turn_tables(rope_all)
@@ -866,7 +1728,9 @@
     inverse_two = inverse_rms(middle)
     unit_two = middle * inverse_two
     normed_moe = (unit_two * gain_moe).astype(BF)
-    moe_all = gather([], [normed_moe], 1)[0].reshape(keys, width)
+    shared, expert_weight, normed_moe = lax.optimization_barrier((shared, expert_weight, normed_moe))
+    shared = lax.all_gather(shared, everyone, axis=0, tiled=True)
+    gate_shared, up_shared, down_t = jnp.split(shared, [hidden, 2 * hidden], axis=1)
 
     def routing(activations, route_ids):
         logits = nn(activations, route_weight)
@@ -878,8 +1742,6 @@
         return probs, named, chosen / total, total
 
     probs, named, gates, chosen_total = routing(normed_moe, routes[0])
-    unused, unused, gates_all, unused = routing(moe_all, routes_all)
-    gates_here = lax.dynamic_slice_in_dim(gates_all, index * EXP_DEV, EXP_DEV, 1)
 
     shared_gate_v = nn(normed_moe, gate_shared)
     shared_up_v = nn(normed_moe, up_shared)
@@ -891,52 +1753,27 @@
     grad_shared_mid = nn(grad_bf, down_t)
     grad_shared_gate_v = (grad_shared_mid * shared_up_v * shared_slope).astype(BF)
     grad_shared_up_v = (grad_shared_mid * shared_act).astype(BF)
-    grad_down_t = tn(grad_bf, shared_mid)
-    grad_gate_shared = tn(normed_moe, grad_shared_gate_v)
-    grad_up_shared = tn(normed_moe, grad_shared_up_v)
     grad_normed_moe = nt(grad_shared_gate_v, gate_shared) + nt(grad_shared_up_v, up_shared)
 
-    mixture = jnp.zeros((keys, width), F32)
-    row_grads = jnp.zeros((keys, width), F32)
-    wide_grads = grads_all.astype(F32)
-    gate_grads = []
-    weight_grads = []
-    for e in range(EXP_DEV):
-        gate_w, up_w, down_w = expert_weight[0, e], expert_weight[1, e], expert_weight[2, e]
-        weight = gates_here[:, e : e + 1]
-        gate_v = nn(moe_all, gate_w)
-        up_v = nn(moe_all, up_w)
-        act, slope = silu_parts(gate_v)
-        mid = (act * up_v).astype(BF)
-        branch = (weight * wide_grads).astype(BF)
-        grad_mid = nn(branch, down_w)
-        grad_gate_v = (grad_mid * up_v * slope).astype(BF)
-        grad_up_v = (grad_mid * act).astype(BF)
-        row = (nt(grad_gate_v, gate_w) + nt(grad_up_v, up_w)).astype(BF)
-        row_grads = row_grads + row.astype(F32)
-        out = nt(mid, down_w).astype(BF).astype(F32)
-        mixture = mixture + weight * out
-        gate_grads.append(jnp.sum(out * wide_grads, axis=1))
-        weight_grads.append(
-            jnp.stack(
-                [
-                    tn(moe_all, grad_gate_v).astype(BF),
-                    tn(moe_all, grad_up_v).astype(BF),
-                    tn(branch, mid).astype(BF),
-                ]
-            )
+    fits = 2 * (2 * expert_weight.size // 2 + 3 * keys * EXP_DEV * hidden + 5 * keys * width) < MOE_VMEM
+    if fits:
+        row_sum, gate_grads, expert_mid, expert_grads = moe_fused(
+            normed_moe, routes_all, grads_all, misc, expert_weight, experts, 1
         )
-    gate_grads = jnp.transpose(jnp.stack(gate_grads, axis=0).reshape(EXP_DEV, chain, rows), (1, 0, 2))
-    row_sum, gate_grads = to_owner(
-        row_grads.astype(BF).reshape(chain, rows, width), gate_grads, 2
-    )
-    mixture_own = lax.psum_scatter(mixture.astype(BF), "expert", scatter_dimension=0, tiled=True)
+        core = index % 2
+        gate_grads = gate_grads[:, :EXP_DEV].reshape(chain, EXP_DEV, 2, rows)
+        gate_grads = jnp.where(core == 0, gate_grads[:, :, 0], gate_grads[:, :, 1])
+    else:
+        moe_all = gather([], [normed_moe], 1)[0].reshape(keys, width)
+        unused, unused, gates_all, unused = routing(moe_all, routes_all)
+        gates_here = lax.dynamic_slice_in_dim(gates_all, index * EXP_DEV, EXP_DEV, 1)
+        row_part, gate_grads, expert_mid, expert_grads = moe_plain(
+            moe_all, gates_here, grads_all, expert_weight
+        )
+        gate_grads = jnp.transpose(gate_grads.T.reshape(EXP_DEV, chain, rows), (1, 0, 2))
+        row_sum, gate_grads = to_owner(row_part.reshape(chain, rows, width), gate_grads, 2)
     gate_grads = gate_grads.reshape(experts, rows).T
-    expert_sum = lax.psum_scatter(
-        jnp.stack(weight_grads, axis=1), "dp", scatter_dimension=2, tiled=True
-    ).astype(F32)
-    output = (middle + shared_out + mixture_own.astype(F32)).astype(BF)
-
+    expert_sum = lax.psum_scatter(expert_grads, "dp", scatter_dimension=2, tiled=True)
     grad_chosen = (gate_grads - jnp.sum(gates * gate_grads, axis=1, keepdims=True)) / chosen_total
     grad_probs = jnp.where(named, grad_chosen, 0.0)
     grad_logits = (
@@ -951,11 +1788,26 @@
     )
     grad_attn = grad_middle.astype(BF)
     grad_attended = nn(grad_attn, out_t).astype(BF)
-    grad_out_t = tn(grad_attn, attended)
 
     delta = jnp.sum((grad_attended.astype(F32) * attended_full).reshape(rows, H, HD), axis=-1).T
     side = jnp.concatenate([log_own[:, :, 0], delta], axis=0)
-    grad_all, side_all = gather([], [grad_attended, side], 3)
+    if fits:
+        grad_all, side_all, mixture, grad_gate_shared, grad_up_shared, grad_down_t, grad_out_t = spread(
+            grad_attended,
+            side,
+            expert_mid,
+            expert_weight,
+            normed_moe,
+            grad_shared_gate_v,
+            grad_shared_up_v,
+            grad_bf,
+            shared_mid,
+            grad_attn,
+            attended,
+            3,
+        )
+    else:
+        grad_all, side_all = gather([], [grad_attended, side], 3)
     grad_all = grad_all.reshape(keys, H * HD)
     side_all = jnp.transpose(side_all, (1, 0, 2)).reshape(2, H, 1, keys)
     grads = attend_back(
@@ -971,38 +1823,58 @@
         cosine_own,
         sine_own,
     )
-    grad_projected = jnp.concatenate([grads[0], grads[1], grads[2]], axis=1)
-    grad_qkv = tn(normed, grad_projected)
-    grad_normed_one = nt(grad_projected, qkv_weight)
-    grad_gain_attn = jnp.sum(grad_normed_one * unit_one, axis=0)
-    scaled_one = grad_normed_one * gain_attn
-    grad_inputs = grad_middle + inverse_one * (
-        scaled_one - unit_one * jnp.mean(scaled_one * unit_one, axis=-1, keepdims=True)
+    grad_misc = jnp.concatenate(
+        [grad_route, jnp.zeros((width, 1), F32), grad_gain_moe[:, None]], axis=1
     )
-
-    grad_misc = jnp.concatenate([grad_route, grad_gain_attn[:, None], grad_gain_moe[:, None]], axis=1)
-    grad_misc = jnp.pad(grad_misc, ((0, 0), (0, route_pad - experts - 2)))
-    rest_sum, qkv_sum = sum_dense(
-        [
-            jnp.concatenate(
-                [
-                    grad_misc.astype(BF),
-                    grad_out_t.astype(BF),
-                    grad_gate_shared.astype(BF),
-                    grad_up_shared.astype(BF),
-                    grad_down_t.astype(BF),
-                ],
-                axis=1,
-            ),
-            grad_qkv.astype(BF),
-        ],
-        (1024, 768),
-        4,
-    )
-    misc_sum, out_sum, gate_sum, up_sum, down_sum = jnp.split(rest_sum, cuts, axis=1)
+    grad_misc = jnp.pad(grad_misc, ((0, 0), (0, 256 - experts - 2)))
+    if fits:
+        out_sum, gate_sum, up_sum, down_sum, qkv_sum, misc_sum, grad_inputs, output = finish(
+            [grad_out_t, grad_gate_shared, grad_up_shared, grad_down_t],
+            (640, hidden, hidden, hidden, 640, 256),
+            experts,
+            normed,
+            grads,
+            qkv_weight,
+            grad_misc,
+            unit_one,
+            inverse_one,
+            gain_attn[None, :],
+            grad_middle,
+            mixture,
+            middle + shared_out,
+            4,
+        )
+    else:
+        down = expert_weight[2]
+        mixture = nt(expert_mid[:, :hidden], down[0])
+        for e in range(1, EXP_DEV):
+            mixture = mixture + nt(expert_mid[:, e * hidden : (e + 1) * hidden], down[e])
+        mixture = lax.psum_scatter(mixture.astype(BF), "expert", scatter_dimension=0, tiled=True)
+        output = (middle + shared_out + mixture.astype(F32)).astype(BF)
+        grad_projected = jnp.concatenate([grads[0], grads[1], grads[2]], axis=1)
+        grad_normed_one = nt(grad_projected, qkv_weight)
+        grad_gain_attn = jnp.sum(grad_normed_one * unit_one, axis=0)
+        scaled_one = grad_normed_one * gain_attn
+        grad_inputs = grad_middle + inverse_one * (
+            scaled_one - unit_one * jnp.mean(scaled_one * unit_one, axis=-1, keepdims=True)
+        )
+        grad_inputs = grad_inputs.astype(BF)
+        out_sum, gate_sum, up_sum, down_sum, qkv_sum, misc_sum = sum_dense(
+            [
+                tn(grad_attn, attended).astype(BF),
+                tn(normed_moe, grad_shared_gate_v).astype(BF),
+                tn(normed_moe, grad_shared_up_v).astype(BF),
+                tn(grad_bf, shared_mid).astype(BF),
+                tn(normed, grad_projected).astype(BF),
+                grad_misc.at[:, experts].set(grad_gain_attn).astype(BF),
+            ],
+            (640, hidden, hidden, hidden, 768, 256),
+            4,
+        )
+    expert_sum = expert_sum.astype(F32)
     return (
         output[None],
-        grad_inputs.astype(BF)[None],
+        grad_inputs[None],
         qkv_sum,
         out_sum.T,
         gate_sum,

time: 749 us -> 615 us (0.82)
  matrix products: 183 us -> 19.3 us
  Pallas kernels: 422 us -> 509 us
  waiting for transfers between devices: 24.2 us -> 0.06 us
  local copies, waits for them, and re-layouts: 47.2 us -> 28.5 us
  other arithmetic: 46.4 us -> 33.3 us
    pallas_call x2 -> x3, Pallas kernels: 142 us -> 328 us  [the longest x1 147 us: finish(): pl.pallas_call(functools.partial(finish_kernel, chips, tuple(chunks), n,...]
    pallas_call x3 -> x1, Pallas kernels: 225 us -> 127 us  [gather(): pl.pallas_call(functools.partial(gather_kernel, chips, len(full), len(cha...]
    dot_general x12 -> x5, matrix products: 71 us -> 7.07 us  [nt(): lax.dot_general(a, b, (((1,), (1,)), ((), ())), preferred_element_type=F32)]
    dot_general x12 -> x5, matrix products: 66 us -> 10.3 us  [nn(): return jnp.dot(a, b, preferred_element_type=F32)]
    dot_general x12 -> x1, matrix products: 46.4 us -> 1.86 us  [tn(): lax.dot_general(a, b, (((0,), (0,)), ((), ())), preferred_element_type=F32)]
    all_gather x1, waiting for transfers between devices: 24.2 us -> 0.01 us  [local(): expert_weight = lax.all_gather(expert_shard, 'dp', axis=2, tiled=True)]
    concatenate x1 -> x2, local copies, waits for them, and re-layouts: 14.3 us -> 0.33 us  [local(): jnp.concatenate([grad_route, jnp.zeros((width, 1), F32), grad_gain_moe[:,...]
    another operation x4 -> x1, other arithmetic: 8.7 us -> 0.18 us  [the longest x3 8.52 us: local(): jnp.stack(weight_grads, axis=1)]
  transfers between devices with their start and end apart: 3 -> 3, of which waited for: 1 -> 0; matrix products, arithmetic and copies ran while one was open for 26% -> 10% of each run, Pallas kernels for 39% -> 84%
where the time goes in v2:
time: 615 us; the launch traced here: 605 us
  Pallas kernels  509 us (83%)
  other arithmetic  33.3 us (5%)
  local copies, waits for them, and re-layouts  28.5 us (5%)
  matrix products  19.3 us (3%)
  between operations  14.6 us (2%)
    pallas_call x1, Pallas kernels, finish(): pl.pallas_call(functools.partial(finish_kernel, chips, tuple(chunks), n,...  147 us
    pallas_call x1, Pallas kernels, gather(): pl.pallas_call(functools.partial(gather_kernel, chips, len(full), len(cha...  127 us
    pallas_call x1, Pallas kernels, moe_fused(): pl.pallas_call(functools.partial(moe_kernel, chips, experts), out_shape=[...  126 us
    pallas_call x1, Pallas kernels, spread(): pl.pallas_call(functools.partial(spread_kernel, chips), out_shape=[jax.Sh...  54.4 us
    pallas_call x1, Pallas kernels, project_qkv(): pl.pallas_call(functools.partial(qkv_kernel, per_block), out_shape=jax.Sh...  23.6 us
    pallas_call x1, Pallas kernels, attend_back(): pl.pallas_call(functools.partial(attend_back_kernel, HD ** (-0.5)), out_s...  19.2 us
  transfers between devices with their start and end apart: 3, of which 0 were waited for; matrix products, arithmetic and copies ran while one was open for 10% of the time, Pallas kernels for 84%

profile of v2, /device:TPU:0, one launch (start us, length us, event | category | flops | bytes accessed | tf_op | source)
XLA Modules:
  0.0 605.3 jit_solution(11500005595760598469)
XLA Ops:
  7.2 1.9 convert_bitcast_fusion
  9.5 1.9 convert_bitcast_fusion.1
  11.4 2.0 pad_maximum_fusion
  19.2 126.6 %shard_map.229 = (bf16[32,40,3840]{2,1,0:T(8,128)(2,1)}, bf16[32,40,1408]{2,1,0:T(8,128)(2,1)}, bf16[8,192,1280]{2,1,0:T(8,128)(2,1)}, s32[8,192,7]{2,1,0:T(8,128)}, bf16[8,192,1280]{2,1,0:T(8,128)(2,1)}) custom-call(bf16[40,3840]{1,0:T(8,128)(2,1)} %convert_element_type.126.refs_0_, bf16[40,1408]{1,0:T(8,128)(2,1)} %pad_maximum_fusion.5.refs_1_, ...), custom_call_target="tpu_custom_call" | custom-call | bytes 341475328 | tf_op jit(solution)/shard_map/pallas_call | solution.py:300
  145.8 3.0 multiply_reduce_fusion
  148.9 1.7 convert_reduce_fusion
  151.3 2.8 fusion.31
  155.0 1.6 pad_maximum_fusion.1
  156.6 2.8 fusion.1.x_ref
  159.4 23.6 %shard_map.230.q_ref.k_ref.v_ref.qa_ref.ko_ref.vo_ref = bf16[1536,3840]{1,0:T(8,128)(2,1)} custom-call(bf16[1536,1280]{1,0:T(8,128)(2,1)} %fusion.1.x_ref, bf16[1280,3840]{1,0:T(8,128)(2,1)} %bitcast.101, f32[1536,128]{1,0:T(8,128)} %get-tuple-element.156.cos_ref, f32[1536,128]{1,0:T(8,128)} %get-tuple-element.157.sin_ref), custom_call_target="tpu_custom_call" | custom-call | flops 15099494400 | bytes 25559040 | tf_op jit(solution)/shard_map/pallas_call | solution.py:614
  183.1 12.1 %shard_map.231 = (f32[192,1280]{1,0:T(8,128)}, f32[10,192,8]{2,1,0:T(8,128)}) custom-call(s32[1]{0:T(128)} %bitcast.2.me_ref, bf16[1536,3840]{1,0:T(8,128)(2,1)} %shard_map.230.q_ref.k_ref.v_ref.qa_ref.ko_ref.vo_ref, bf16[1536,3840]{1,0:T(8,128)(2,1)} %shard_map.230.q_ref.k_ref.v_ref.qa_ref.ko_ref.vo_ref, ...), custom_call_target="tpu_custom_call" | custom-call | flops 1509949440 | bytes 7864320 | tf_op jit(solution)/shard_map/pallas_call | solution.py:655
  196.5 1.3 multiply_reduce_fusion.3
  199.7 1.7 split.24.misc
  201.5 126.1 %shard_map.232 = (f32[192,1280]{1,0:T(8,128)}, f32[8,8,384]{2,1,0:T(8,128)}, bf16[1536,1792]{1,0:T(8,128)(2,1)}, bf16[3,2,1280,896]{3,2,1,0:T(8,128)(2,1)}) custom-call(bf16[192,1280]{1,0:T(8,128)(2,1)} %multiply_convert_fusion.1.x_own.rows_in, s32[4,384,7]{2,1,0:T(8,128)} %bitcast.132, bf16[4,2,192,1280]{3,2,1,0:T(8,128)(2,1)} %bitcast.131, ...), custom_call_target="tpu_custom_call" | custom-call | flops 56371445760 | bytes 38535168 | tf_op jit(solution)/shard_map/pallas_call | solution.py:1061
  329.6 1.8 copy.81
  331.5 1.8 fusion.33
  333.2 1.3 compare_select_fusion.firsta_ref
  334.5 1.3 convert_multiply_fusion
  337.0 1.4 fusion.49
  338.5 1.9 fusion.50
  340.4 2.9 fusion.15
  343.3 2.8 fusion.23
  346.2 1.6 multiply_convert_fusion.2
  351.3 1.3 fusion.47
  352.6 1.7 convert_multiply_fusion.2
  355.4 54.4 %shard_map.233 = (bf16[8,192,1280]{2,1,0:T(8,128)(2,1)}, f32[8,20,192]{2,1,0:T(8,128)}, bf16[4,2,192,1280]{3,2,1,0:T(8,128)(2,1)}, bf16[1280,896]{1,0:T(8,128)(2...) custom-call(bf16[192,1280]{1,0:T(8,128)(2,1)} %get-tuple-element.155.own.do_ref, ...), custom_call_target="tpu_custom_call" | custom-call | flops 7046430720 | bytes 125829120 | tf_op jit(solution)/shard_map/pallas_call | solution.py:1287
  413.9 3.5 convolution_add_fusion.refs_13_
  417.3 1.3 broadcast_in_dim.38.delta_ref
  418.6 19.2 %shard_map.234.refs_5_ = bf16[3,192,1280]{2,1,0:T(8,128)(2,1)} custom-call(s32[1]{0:T(128)} %bitcast.2.me_ref, bf16[1536,3840]{1,0:T(8,128)(2,1)} %shard_map.230.q_ref.k_ref.v_ref.qa_ref.ko_ref.vo_ref, bf16[1536,3840]{1,0:T(8,128)(2,1)} %shard_map.230.q_ref.k_ref.v_ref.qa_ref.ko_ref.vo_ref, ...), custom_call_target="tpu_custom_call" | custom-call | flops 5284823040 | bytes 15728640 | tf_op jit(solution)/shard_map/pallas_call | solution.py:738
  437.8 147.3 %shard_map.235 = (f32[40,1280]{1,0:T(8,128)}, f32[40,896]{1,0:T(8,128)}, f32[40,896]{1,0:T(8,128)}, f32[40,896]{1,0:T(8,128)}, f32[40,3840]{1,0:T(8,128)}, /*ind...) custom-call(bf16[2,2,4,2,40,1280]{5,4,3,2,1,0:T(8,128)(2,1)} %bitcast.112, ...), custom_call_target="tpu_custom_call" | custom-call | flops 3774873600 | bytes 314572800 | tf_op jit(solution)/shard_map/pallas_call | solution.py:1627
  588.0 2.4 convert_element_type.158
  590.4 3.0 slice_bitcast_fusion
  (153 shorter events, 30.8 us)
Async XLA Ops:
  7.2 2.3 copy-start.11
  7.2 192.3 %all-gather.3.cloned.1.call-start = ((), (), s32[]{:S(2)}) async-start(), calls=%async_computation.1 | async-start | bytes 17203200 | tf_op jit(solution)/shard_map/all_gather | solution.py:1695
  13.4 1.5 copy-start.32
  13.4 1.7 copy-start.25
  13.4 1.7 copy-start.26
  13.4 3.5 copy-start.31
  13.4 4.2 copy-start.15
  13.4 5.1 copy-start.23
  13.5 327.0 %all-gather.5.cloned.1.call-start = ((), (), s32[]{:S(2)}) async-start(), calls=%async_computation.2 | async-start | bytes 7096320 | tf_op jit(solution)/shard_map/all_gather | solution.py:1732
  148.8 7.8 %copy-start = (bf16[8,192,1280]{2,1,0:T(8,128)(2,1)S(1)}, bf16[8,192,1280]{2,1,0:T(8,128)(2,1)}, u32[]{:S(2)}) copy-start(bf16[8,192,1280]{2,1,0:T(8,128)(2,1)} %get-tuple-element.41) | copy-start | bytes 11796484
  154.1 2.5 copy-start.3
  183.1 13.4 %copy-start.4 = (bf16[32,40,1408]{2,1,0:T(8,128)(2,1)S(1)}, bf16[32,40,1408]{2,1,0:T(8,128)(2,1)}, u32[]{:S(2)}) copy-start(bf16[32,40,1408]{2,1,0:T(8,128)(2,1)} %get-tuple-element.42) | copy-start | bytes 10813444
  183.1 13.4 %copy-start.6 = (bf16[1,192,1280]{2,1,0:T(8,128)(2,1)S(1)}, bf16[1,192,1280]{2,1,0:T(8,128)(2,1)}, u32[]{:S(2)}) copy-start(bf16[1,192,1280]{2,1,0:T(8,128)(2,1)} %param.14) | copy-start | bytes 1474564
  199.5 388.5 %reduce-scatter.2.cloned.1.call-start = ((), (), s32[]{:S(2)}) async-start(), calls=%async_computation.3 | async-start | bytes 17203200 | tf_op jit(solution)/shard_map/reduce_scatter | solution.py:1776
  327.6 3.9 copy-start.2
  334.5 8.8 %copy-start.12 = (bf16[1,192,1280]{2,1,0:T(8,128)(2,1)S(1)}, bf16[1,192,1280]{2,1,0:T(8,128)(2,1)}, u32[]{:S(2)}) copy-start(bf16[1,192,1280]{2,1,0:T(8,128)(2,1)} %param.15) | copy-start | bytes 1474564
  340.4 5.7 copy-start.8
  340.4 5.7 copy-start.10
  347.8 2.3 copy-start.21
  347.8 2.3 copy-start.35
  348.6 2.1 copy-start.5
  350.7 1.9 copy-start.9
  352.6 1.7 copy-start.13
  355.4 57.0 %copy-start.22 = (f32[1280,16]{0,1:T(8,128)S(1)}, f32[1280,16]{0,1:T(8,128)}, u32[]{:S(2)}) copy-start(f32[1280,16]{0,1:T(8,128)} %fusion.50) | copy-start | bytes 245764
  409.7 4.1 copy-start.20
  590.4 3.1 copy-start.19
  590.4 3.9 copy-start.18
  590.4 4.6 copy-start.16
  590.4 5.5 copy-start.24
  593.5 3.1 copy-start.30
  593.5 3.7 copy-start.29
  593.5 4.4 copy-start.28
  (7 other events, 8.2 us)
Sparse Core Ops, SparseCore 0:
  13.6 177.0 all-gather.2
  199.6 101.1 all-gather.4
  327.7 131.1 reduce-scatter.1

commit v3 on v2

--- a/solution.py
+++ b/solution.py
@@ -179,8 +179,8 @@
     def present(zz):
         return (zz >= 0) & (zz < chips)
 
-    def block_here(zz, distance, direction):
-        for a in arrays:
+    def block_here(some, zz, direction):
+        for a in some:
             along(a, zz, direction).wait_recv()
             if direction == 0:
 
@@ -213,22 +213,22 @@
             half(a, far_dp, zz, 1).wait_recv()
             to_core(a, far_dp, zz).start()
 
-    for a in arrays:
-
-        @pl.when(has_up)
-        def _(a=a):
-            along(a, z, 0, a.own).start()
-
-        @pl.when(has_down)
-        def _(a=a):
-            along(a, z, 1, a.own).start()
-
-        if a.full:
-            side(a, at.d, z, 0, a.own).start()
-            side(a, at.d, z, 1, a.own).start()
-        to_core(a, at.d, z, a.own).start()
-    for a in arrays:
-        pltpu.make_async_copy(a.own, slot(a, at.d, z, c), a.local).start()
+    def own_here(some):
+        for a in some:
+
+            @pl.when(has_up)
+            def _(a=a):
+                along(a, z, 0, a.own).start()
+
+            @pl.when(has_down)
+            def _(a=a):
+                along(a, z, 1, a.own).start()
+
+            if a.full:
+                side(a, at.d, z, 0, a.own).start()
+                side(a, at.d, z, 1, a.own).start()
+            to_core(a, at.d, z, a.own).start()
+            pltpu.make_async_copy(a.own, slot(a, at.d, z, c), a.local).start()
 
     def at_distance(k, fn):
         @pl.when((k >= 0) & present(z - k))
@@ -239,17 +239,31 @@
         def _():
             fn(z + k)
 
-    def step(k, carry):
+    def chain_step(some, k):
         @pl.when(present(z - k))
         def _():
-            block_here(z - k, k, 0)
+            block_here(some, z - k, 0)
 
         @pl.when(present(z + k))
         def _():
-            block_here(z + k, k, 1)
-
+            block_here(some, z + k, 1)
+
+    full, chained = arrays[:n_full], arrays[n_full:]
+    if n_full:
+        own_here(full)
+
+        def first_step(k, carry):
+            chain_step(full, k)
+            return carry
+
+        lax.fori_loop(1, chips, first_step, 0)
+    own_here(chained)
+
+    def step(k, carry):
         if n_full:
             at_distance(k - 1, side_here)
+        chain_step(chained, k)
+        if n_full:
             at_distance(k - 2, far_here)
         return carry
 
@@ -598,18 +612,27 @@
 
 def qkv_kernel(per_block, x_ref, w_ref, cos_ref, sin_ref, o_ref):
     column = pl.program_id(1)
-    product = nn(x_ref[...], w_ref[...])
-    for k in range(per_block):
-        part = product[:, k * HD : (k + 1) * HD]
-        head = column * per_block + k
-        turned = part * cos_ref[...] + pltpu.roll(part, HD // 2, 1) * sin_ref[...]
-        o_ref[:, k * HD : (k + 1) * HD] = jnp.where(head < 2 * H, turned, part).astype(BF)
+    rows = x_ref.shape[0]
+    step = 384 if rows % 384 == 0 else rows
+    for first in range(0, per_block, 2):
+        for r in range(0, rows, step):
+            product = nn(x_ref[r : r + step, :], w_ref[:, first * HD : (first + 2) * HD])
+            for k in (0, 1):
+                part = product[:, k * HD : (k + 1) * HD]
+                head = column * per_block + first + k
+                turned = (
+                    part * cos_ref[r : r + step, :]
+                    + pltpu.roll(part, HD // 2, 1) * sin_ref[r : r + step, :]
+                )
+                o_ref[r : r + step, (first + k) * HD : (first + k + 1) * HD] = jnp.where(
+                    head < 2 * H, turned, part
+                ).astype(BF)
 
 
 def project_qkv(normed, weight, cosine, sine):
     rows, width = normed.shape
     columns = weight.shape[1]
-    per_block = 2
+    per_block = 6
     tile_m = min(rows, 1536)
     return pl.pallas_call(
         functools.partial(qkv_kernel, per_block),
@@ -1415,7 +1438,7 @@
                 self.give[yy, xx, zz] = tile_ref[away, : self.wide].astype(BF)
                 return carry
 
-            lax.fori_loop(0, 4 * chips, body, 0)
+            lax.fori_loop(0, 4 * chips, body, 0, unroll=4)
             self.core().start()
 
     parts = [Chunk(q) for q in range(n_chunks)]
@@ -1427,12 +1450,10 @@
 
         def body(k, carry):
             yy, xx, zz = k // (2 * chips), (k // chips) % 2, k % chips
-            p.mine[yy, xx, zz] = (
-                p.mine[yy, xx, zz].astype(F32) + p.other[yy, xx, zz].astype(F32)
-            ).astype(BF)
+            p.mine[yy, xx, zz] = p.mine[yy, xx, zz] + p.other[yy, xx, zz]
             return carry
 
-        lax.fori_loop(0, 4 * chips, body, 0)
+        lax.fori_loop(0, 4 * chips, body, 0, unroll=4)
         p.first_x().start()
         p.first_y().start()
 
@@ -1443,15 +1464,11 @@
         def body(k, carry):
             v, zz = k // chips, k % chips
             a, b = p.half
-            p.mine[v, x, zz, :, a] = (
-                p.mine[v, x, zz, :, a].astype(F32) + p.one[0][v, zz].astype(F32)
-            ).astype(BF)
-            p.mine[y, v, zz, :, b] = (
-                p.mine[y, v, zz, :, b].astype(F32) + p.one[1][v, zz].astype(F32)
-            ).astype(BF)
+            p.mine[v, x, zz, :, a] = p.mine[v, x, zz, :, a] + p.one[0][v, zz]
+            p.mine[y, v, zz, :, b] = p.mine[y, v, zz, :, b] + p.one[1][v, zz]
             return carry
 
-        lax.fori_loop(0, 2 * chips, body, 0)
+        lax.fori_loop(0, 2 * chips, body, 0, unroll=2)
         p.second_y().start()
         p.second_x().start()
 
@@ -1462,12 +1479,10 @@
         def body(zz, carry):
             for w in (0, 1):
                 s = p.half[w]
-                p.mine[y, x, zz, :, s] = (
-                    p.mine[y, x, zz, :, s].astype(F32) + p.two[w][zz].astype(F32)
-                ).astype(BF)
+                p.mine[y, x, zz, :, s] = p.mine[y, x, zz, :, s] + p.two[w][zz]
             return carry
 
-        lax.fori_loop(0, chips, body, 0)
+        lax.fori_loop(0, chips, body, 0, unroll=2)
         for k in range(1, chips):
             p.last(k).start()
 
@@ -1527,30 +1542,32 @@
         mean = jnp.mean(scaled * unit[...], axis=1, keepdims=True)
         input_out[...] = (grad_middle[...] + inverse[...] * (scaled - unit[...] * mean)).astype(BF)
 
+    for k in range(1, chips + 1):
+        zz = lax.rem(z + k, chips)
+        mix_core(zz).start()
+        mix_load(zz).start()
     for p in parts:
         if not p.made:
             p.core().start()
             p.load().start()
     weight_load(0).start()
-    for zz in range(chips):
-        mix_core(zz).start()
-        mix_load(zz).start()
+    mix_settle()
     n_known = sum(not p.made for p in parts)
-    for p in parts[n_known:-1]:
-        k, first = p.first // projected.shape[2], p.first % projected.shape[2]
-        tile_ref[:, : p.wide] = tn(normed[...], projected[k, :, first : first + p.wide])
-        p.take()
-    stages = (stage_one, stage_two, stage_three, stage_four)
-    for t in range(n_chunks + len(stages) - 1):
-        for s, stage in enumerate(stages):
-            if 0 <= t - s < n_chunks:
-                stage(parts[t - s])
-        if t == 1:
-            mix_settle()
-        if t < 3:
-            input_grads(t)
-        if t == 2:
-            parts[-1].take()
+    n_made = n_chunks - 1 - n_known
+    stages = ((0, stage_one), (1, stage_two), (2, stage_three), (6, stage_four))
+    for t in range(n_chunks + stages[-1][0]):
+        for lag, stage in stages:
+            if 0 <= t - lag < n_chunks:
+                stage(parts[t - lag])
+        if t < n_made:
+            p = parts[n_known + t]
+            k, first = p.first // part, p.first % part
+            tile_ref[:, : p.wide] = tn(normed[...], projected[k, :, first : first + p.wide])
+            p.take()
+        elif t < n_made + 3:
+            input_grads(t - n_made)
+            if t == n_made + 2:
+                parts[-1].take()
     total = base[...] + mix_mine[z].astype(F32) + mix_other[z].astype(F32)
     for k in range(1, chips):
         mix_over(k).wait_recv()
@@ -1693,9 +1710,15 @@
         [expert_gate.astype(BF), expert_up.astype(BF), jnp.swapaxes(expert_down.astype(BF), 1, 2)]
     )
     expert_weight = lax.all_gather(expert_shard, "dp", axis=2, tiled=True)
-    qkv_weight, near, tokens_all, routes_all, grads_all = gather(
-        [attn_qkv.astype(BF), near], [tokens[0], routes[0], cotangent[0]], 0
+    shared = jnp.concatenate(
+        [shared_gate.astype(BF), shared_up.astype(BF), shared_down.astype(BF).T], axis=1
     )
+    fits = 2 * width * EXP_DEV * hidden * 3 + 2 * keys * (3 * EXP_DEV * hidden + 5 * width) < MOE_VMEM
+    chained = [tokens[0], routes[0], cotangent[0]] + ([shared] if fits else [])
+    qkv_weight, near, tokens_all, routes_all, grads_all, *early = gather(
+        [attn_qkv.astype(BF), near], chained, 0
+    )
+    shared = early[0] if fits else shared
     grads_all = grads_all.reshape(keys, width)
     qkv_weight = qkv_weight.reshape(width, 3 * H * HD)
     near = near.reshape(width, near.shape[-1])
@@ -1707,9 +1730,6 @@
     route_weight = misc[:, :experts]
     gain_attn = misc[:, experts].astype(F32)
     gain_moe = misc[:, experts + 1].astype(F32)
-    shared = jnp.concatenate(
-        [shared_gate.astype(BF), shared_up.astype(BF), shared_down.astype(BF).T], axis=1
-    )
     first_all, rope_all = doc_starts_of(lengths[0], jnp.arange(keys, dtype=jnp.int32))
     first_own = lax.dynamic_slice_in_dim(first_all, own_first, rows, 0)
     cosine, sine = turn_tables(rope_all)
@@ -1729,7 +1749,8 @@
     unit_two = middle * inverse_two
     normed_moe = (unit_two * gain_moe).astype(BF)
     shared, expert_weight, normed_moe = lax.optimization_barrier((shared, expert_weight, normed_moe))
-    shared = lax.all_gather(shared, everyone, axis=0, tiled=True)
+    shared = lax.all_gather(shared, "dp" if fits else everyone, axis=0, tiled=True)
+    shared = shared.reshape(width, 3 * hidden)
     gate_shared, up_shared, down_t = jnp.split(shared, [hidden, 2 * hidden], axis=1)
 
     def routing(activations, route_ids):
@@ -1755,7 +1776,6 @@
     grad_shared_up_v = (grad_shared_mid * shared_act).astype(BF)
     grad_normed_moe = nt(grad_shared_gate_v, gate_shared) + nt(grad_shared_up_v, up_shared)
 
-    fits = 2 * (2 * expert_weight.size // 2 + 3 * keys * EXP_DEV * hidden + 5 * keys * width) < MOE_VMEM
     if fits:
         row_sum, gate_grads, expert_mid, expert_grads = moe_fused(
             normed_moe, routes_all, grads_all, misc, expert_weight, experts, 1
@@ -1871,7 +1891,6 @@
             (640, hidden, hidden, hidden, 768, 256),
             4,
         )
-    expert_sum = expert_sum.astype(F32)
     return (
         output[None],
         grad_inputs[None],
@@ -1882,9 +1901,9 @@
         down_sum.T,
         misc_sum[:, :experts],
         misc_sum[:, experts : experts + 2].T,
-        expert_sum[0],
-        expert_sum[1],
-        jnp.swapaxes(expert_sum[2], 1, 2),
+        expert_sum[0].astype(F32),
+        expert_sum[1].astype(F32),
+        jnp.swapaxes(expert_sum[2], 1, 2).astype(F32),
     )
 
 

time: 615 us -> 569 us (0.925)
  Pallas kernels: 509 us -> 464 us
    pallas_call x1, Pallas kernels: 147 us -> 119 us  [finish(): pl.pallas_call(functools.partial(finish_kernel, chips, tuple(chunks), n,...]
    pallas_call x1, Pallas kernels: 126 us -> 106 us  [moe_fused(): pl.pallas_call(functools.partial(moe_kernel, chips, experts), out_shape=[...]
  transfers between devices with their start and end apart: 3 -> 3, of which waited for: 0 -> 0; matrix products, arithmetic and copies ran while one was open for 10% -> 11% of each run, Pallas kernels for 84% -> 83%
where the time goes in v3:
time: 569 us; the launch traced here: 559 us
  Pallas kernels  464 us (82%)
  other arithmetic  38.1 us (7%)
  local copies, waits for them, and re-layouts  25.1 us (4%)
  matrix products  17.1 us (3%)
  between operations  14.5 us (3%)
    pallas_call x1, Pallas kernels, gather(): pl.pallas_call(functools.partial(gather_kernel, chips, len(full), len(cha...  131 us
    pallas_call x1, Pallas kernels, finish(): pl.pallas_call(functools.partial(finish_kernel, chips, tuple(chunks), n,...  119 us
    pallas_call x1, Pallas kernels, moe_fused(): pl.pallas_call(functools.partial(moe_kernel, chips, experts), out_shape=[...  106 us
    pallas_call x1, Pallas kernels, spread(): pl.pallas_call(functools.partial(spread_kernel, chips), out_shape=[jax.Sh...  55.6 us
    pallas_call x1, Pallas kernels, project_qkv(): pl.pallas_call(functools.partial(qkv_kernel, per_block), out_shape=jax.Sh...  21.7 us
    pallas_call x1, Pallas kernels, attend_back(): pl.pallas_call(functools.partial(attend_back_kernel, HD ** (-0.5)), out_s...  19.1 us
    pallas_call x1, Pallas kernels, attend(): pl.pallas_call(functools.partial(attend_kernel, HD ** (-0.5)), out_shape=...  12.1 us
  transfers between devices with their start and end apart: 3, of which 0 were waited for; matrix products, arithmetic and copies ran while one was open for 11% of the time, Pallas kernels for 83%

profile of v3, /device:TPU:0, one launch (start us, length us, event | category | flops | bytes accessed | tf_op | source)
XLA Modules:
  0.0 559.1 jit_solution(4049738701954808444)
XLA Ops:
  7.2 1.9 convert_bitcast_fusion.1
  9.5 1.9 convert_bitcast_fusion.2
  11.4 2.0 pad_maximum_fusion
  19.8 131.1 %shard_map.229 = (bf16[32,40,3840]{2,1,0:T(8,128)(2,1)}, bf16[32,40,1408]{2,1,0:T(8,128)(2,1)}, bf16[8,192,1280]{2,1,0:T(8,128)(2,1)}, s32[8,192,7]{2,1,0:T(8,12...) custom-call(bf16[40,3840]{1,0:T(8,128)(2,1)} %convert_element_type.144.refs_0_, ...), custom_call_target="tpu_custom_call" | custom-call | bytes 369000448 | tf_op jit(solution)/shard_map/pallas_call | solution.py:314
  150.9 3.0 multiply_reduce_fusion
  153.9 1.7 convert_reduce_fusion
  156.3 2.8 fusion.33
  160.1 1.6 pad_maximum_fusion.1
  161.7 2.8 fusion.1.x_ref
  164.5 21.7 %shard_map.230.q_ref.k_ref.v_ref.qa_ref.ko_ref.vo_ref = bf16[1536,3840]{1,0:T(8,128)(2,1)} custom-call(bf16[1536,1280]{1,0:T(8,128)(2,1)} %fusion.1.x_ref, bf16[1280,3840]{1,0:T(8,128)(2,1)} %bitcast.111, f32[1536,128]{1,0:T(8,128)} %get-tuple-element.158.cos_ref, f32[1536,128]{1,0:T(8,128)} %get-tuple-element.159.sin_ref), custom_call_target="tpu_custom_call" | custom-call | flops 15099494400 | bytes 25559040 | tf_op jit(solution)/shard_map/pallas_call | solution.py:637
  186.2 12.1 %shard_map.231 = (f32[192,1280]{1,0:T(8,128)}, f32[10,192,8]{2,1,0:T(8,128)}) custom-call(s32[1]{0:T(128)} %bitcast.2.me_ref, bf16[1536,3840]{1,0:T(8,128)(2,1)} %shard_map.230.q_ref.k_ref.v_ref.qa_ref.ko_ref.vo_ref, bf16[1536,3840]{1,0:T(8,128)(2,1)} %shard_map.230.q_ref.k_ref.v_ref.qa_ref.ko_ref.vo_ref, ...), custom_call_target="tpu_custom_call" | custom-call | flops 1509949440 | bytes 7864320 | tf_op jit(solution)/shard_map/pallas_call | solution.py:678
  198.3 1.3 convert_element_type.159.attended_in
  199.6 1.3 multiply_reduce_fusion.3
  202.2 1.7 split.24.misc
  203.9 105.9 %shard_map.232 = (f32[192,1280]{1,0:T(8,128)}, f32[8,8,384]{2,1,0:T(8,128)}, bf16[1536,1792]{1,0:T(8,128)(2,1)}, bf16[3,2,1280,896]{3,2,1,0:T(8,128)(2,1)}) custom-call(bf16[192,1280]{1,0:T(8,128)(2,1)} %multiply_convert_fusion.1.x_own.rows_in, s32[4,384,7]{2,1,0:T(8,128)} %bitcast.148, bf16[4,2,192,1280]{3,2,1,0:T(8,128)(2,1)} %bitcast.147, ...), custom_call_target="tpu_custom_call" | custom-call | flops 56371445760 | bytes 38535168 | tf_op jit(solution)/shard_map/pallas_call | solution.py:1084
  310.5 1.2 fusion.28
  312.5 1.8 copy.81
  314.4 1.8 fusion.35
  316.2 1.3 compare_select_fusion.firsta_ref
  317.4 2.5 convert_multiply_fusion
  321.0 1.2 fusion.51
  322.6 2.5 fusion.15
  325.1 2.9 fusion.23
  328.1 1.6 multiply_convert_fusion.2
  333.2 1.3 fusion.49
  334.5 1.6 convert_multiply_fusion.2
  337.2 55.6 %shard_map.233 = (bf16[8,192,1280]{2,1,0:T(8,128)(2,1)}, f32[8,20,192]{2,1,0:T(8,128)}, bf16[4,2,192,1280]{3,2,1,0:T(8,128)(2,1)}, bf16[1280,896]{1,0:T(8,128)(2...) custom-call(bf16[192,1280]{1,0:T(8,128)(2,1)} %get-tuple-element.157.own.do_ref, ...), custom_call_target="tpu_custom_call" | custom-call | flops 7046430720 | bytes 125829120 | tf_op jit(solution)/shard_map/pallas_call | solution.py:1310
  397.0 3.5 convolution_add_fusion.refs_13_
  400.5 1.3 broadcast_in_dim.38.delta_ref
  401.7 19.1 %shard_map.234.refs_5_ = bf16[3,192,1280]{2,1,0:T(8,128)(2,1)} custom-call(s32[1]{0:T(128)} %bitcast.2.me_ref, bf16[1536,3840]{1,0:T(8,128)(2,1)} %shard_map.230.q_ref.k_ref.v_ref.qa_ref.ko_ref.vo_ref, bf16[1536,3840]{1,0:T(8,128)(2,1)} %shard_map.230.q_ref.k_ref.v_ref.qa_ref.ko_ref.vo_ref, ...), custom_call_target="tpu_custom_call" | custom-call | flops 5284823040 | bytes 15728640 | tf_op jit(solution)/shard_map/pallas_call | solution.py:761
  420.8 118.5 %shard_map.235 = (f32[40,1280]{1,0:T(8,128)}, f32[40,896]{1,0:T(8,128)}, f32[40,896]{1,0:T(8,128)}, f32[40,896]{1,0:T(8,128)}, f32[40,3840]{1,0:T(8,128)}, /*ind...) custom-call(bf16[2,2,4,2,40,1280]{5,4,3,2,1,0:T(8,128)(2,1)} %bitcast.122, ...), custom_call_target="tpu_custom_call" | custom-call | flops 3774873600 | bytes 314572800 | tf_op jit(solution)/shard_map/pallas_call | solution.py:1644
  542.2 5.1 convert_bitcast_fusion
  (148 shorter events, 29.2 us)
Async XLA Ops:
  7.2 2.3 copy-start.10
  7.2 194.7 %all-gather.3.cloned.1.call-start = ((), (), s32[]{:S(2)}) async-start(), calls=%async_computation.1 | async-start | bytes 17203200 | tf_op jit(solution)/shard_map/all_gather | solution.py:1712
  13.4 1.6 copy-start.23
  13.4 1.6 copy-start.24
  13.4 3.4 copy-start.29
  13.4 4.1 copy-start.14
  13.4 5.0 copy-start.21
  13.5 5.6 %copy-start.25 = (f32[896,40]{0,1:T(8,128)S(1)}, f32[896,40]{0,1:T(8,128)}, u32[]{:S(2)}) copy-start(f32[896,40]{0,1:T(8,128)} %param.22) | copy-start | bytes 430084
  13.5 309.1 %all-gather.5.cloned.1.call-start = ((), (), s32[]{:S(2)}) async-start(), calls=%async_computation.2 | async-start | bytes 8601600 | tf_op jit(solution)/shard_map/all_gather | solution.py:1752
  153.9 7.8 %copy-start = (bf16[8,192,1280]{2,1,0:T(8,128)(2,1)S(1)}, bf16[8,192,1280]{2,1,0:T(8,128)(2,1)}, u32[]{:S(2)}) copy-start(bf16[8,192,1280]{2,1,0:T(8,128)(2,1)} %get-tuple-element.42) | copy-start | bytes 11796484
  159.1 2.6 copy-start.3
  186.2 13.3 %copy-start.4 = (bf16[32,40,1408]{2,1,0:T(8,128)(2,1)S(1)}, bf16[32,40,1408]{2,1,0:T(8,128)(2,1)}, u32[]{:S(2)}) copy-start(bf16[32,40,1408]{2,1,0:T(8,128)(2,1)} %get-tuple-element.43) | copy-start | bytes 10813444
  186.2 13.4 %copy-start.7 = (bf16[1,192,1280]{2,1,0:T(8,128)(2,1)S(1)}, bf16[1,192,1280]{2,1,0:T(8,128)(2,1)}, u32[]{:S(2)}) copy-start(bf16[1,192,1280]{2,1,0:T(8,128)(2,1)} %param.14) | copy-start | bytes 1474564
  201.9 340.3 %reduce-scatter.2.cloned.1.call-start = ((), (), s32[]{:S(2)}) async-start(), calls=%async_computation.3 | async-start | bytes 17203200 | tf_op jit(solution)/shard_map/reduce_scatter | solution.py:1796
  309.8 4.5 copy-start.2
  309.9 11.1 %copy-start.6 = (bf16[192,1280]{1,0:T(8,128)(2,1)S(1)}, bf16[192,1280]{1,0:T(8,128)(2,1)}, u32[]{:S(2)}) copy-start(bf16[192,1280]{1,0:T(8,128)(2,1)} %multiply_convert_fusion.1.x_own.rows_in) | copy-start | bytes 1474564
  317.4 7.7 %copy-start.12 = (bf16[1,192,1280]{2,1,0:T(8,128)(2,1)S(1)}, bf16[1,192,1280]{2,1,0:T(8,128)(2,1)}, u32[]{:S(2)}) copy-start(bf16[1,192,1280]{2,1,0:T(8,128)(2,1)} %param.15) | copy-start | bytes 1474564
  322.6 5.4 copy-start.9
  329.7 2.3 copy-start.20
  329.7 2.3 copy-start.33
  329.7 1.5 copy-start.13
  330.5 2.1 copy-start.5
  332.6 1.9 copy-start.8
  334.5 1.6 copy-start.11
  392.8 4.2 copy-start.19
  542.2 5.2 copy-start.18
  542.2 6.0 %copy-start.17 = (bf16[192,1280]{1,0:T(8,128)(2,1)S(1)}, bf16[192,1280]{1,0:T(8,128)(2,1)}, u32[]{:S(2)}) copy-start(bf16[192,1280]{1,0:T(8,128)(2,1)} %get-tuple-element.64) | copy-start | bytes 1474564
  542.2 6.7 %copy-start.15 = (f32[40,3840]{1,0:T(8,128)S(1)}, f32[40,3840]{1,0:T(8,128)}, u32[]{:S(2)}) copy-start(f32[40,3840]{1,0:T(8,128)} %get-tuple-element.178) | copy-start | bytes 1843204
  542.2 7.6 %copy-start.22 = (f32[40,1280]{1,0:T(8,128)S(1)}, f32[40,1280]{1,0:T(8,128)}, u32[]{:S(2)}) copy-start(f32[40,1280]{1,0:T(8,128)} %get-tuple-element.66) | copy-start | bytes 614404
  547.4 3.1 copy-start.28
  547.4 3.7 copy-start.27
  547.4 4.4 copy-start.26
  (5 other events, 5.8 us)
Sparse Core Ops, SparseCore 0:
  13.6 178.9 all-gather.2
  202.0 74.4 all-gather.4
  310.0 134.4 reduce-scatter.1

commit v4 on v3

--- a/solution.py
+++ b/solution.py
@@ -50,12 +50,7 @@
     half = HD // 2
     frequency = 10000.0 ** (-jnp.arange(half, dtype=F32) / half)
     angles = rope_pos.astype(F32)[:, None] * frequency[None, :]
-    cosine = jnp.cos(angles)
-    sine = jnp.sin(angles)
-    return (
-        jnp.concatenate([cosine, cosine], axis=1),
-        jnp.concatenate([-sine, sine], axis=1),
-    )
+    return jnp.cos(angles), jnp.sin(angles)
 
 
 def inverse_rms(values):
@@ -610,27 +605,38 @@
     )(*[a.reshape(2, 2, chips, 2, block, a.shape[1]) for a in arrays])
 
 
-def qkv_kernel(per_block, x_ref, w_ref, cos_ref, sin_ref, o_ref):
+def qkv_kernel(per_block, x_ref, w_ref, gain_ref, cos_ref, sin_ref, o_ref, normed, cosine, sine):
     column = pl.program_id(1)
     rows = x_ref.shape[0]
     step = 384 if rows % 384 == 0 else rows
+
+    @pl.when(column == 0)
+    def _():
+        for r in range(0, rows, step):
+            wide = x_ref[r : r + step, :].astype(F32)
+            normed[r : r + step, :] = (wide * inverse_rms(wide) * gain_ref[...]).astype(BF)
+        cosine[:, : HD // 2] = cos_ref[...]
+        cosine[:, HD // 2 :] = cos_ref[...]
+        sine[:, : HD // 2] = -sin_ref[...]
+        sine[:, HD // 2 :] = sin_ref[...]
+
     for first in range(0, per_block, 2):
         for r in range(0, rows, step):
-            product = nn(x_ref[r : r + step, :], w_ref[:, first * HD : (first + 2) * HD])
+            product = nn(normed[r : r + step, :], w_ref[:, first * HD : (first + 2) * HD])
             for k in (0, 1):
                 part = product[:, k * HD : (k + 1) * HD]
                 head = column * per_block + first + k
                 turned = (
-                    part * cos_ref[r : r + step, :]
-                    + pltpu.roll(part, HD // 2, 1) * sin_ref[r : r + step, :]
+                    part * cosine[r : r + step, :]
+                    + pltpu.roll(part, HD // 2, 1) * sine[r : r + step, :]
                 )
                 o_ref[r : r + step, (first + k) * HD : (first + k + 1) * HD] = jnp.where(
                     head < 2 * H, turned, part
                 ).astype(BF)
 
 
-def project_qkv(normed, weight, cosine, sine):
-    rows, width = normed.shape
+def project_qkv(tokens, weight, gain, cosine, sine):
+    rows, width = tokens.shape
     columns = weight.shape[1]
     per_block = 6
     tile_m = min(rows, 1536)
@@ -641,17 +647,23 @@
         in_specs=[
             pl.BlockSpec((tile_m, width), lambda m, n: (m, 0)),
             pl.BlockSpec((width, per_block * HD), lambda m, n: (0, n)),
-            pl.BlockSpec((tile_m, HD), lambda m, n: (m, 0)),
-            pl.BlockSpec((tile_m, HD), lambda m, n: (m, 0)),
+            pl.BlockSpec((1, width), lambda m, n: (0, 0)),
+            pl.BlockSpec((tile_m, HD // 2), lambda m, n: (m, 0)),
+            pl.BlockSpec((tile_m, HD // 2), lambda m, n: (m, 0)),
         ],
         out_specs=pl.BlockSpec((tile_m, per_block * HD), lambda m, n: (m, n)),
+        scratch_shapes=[
+            pltpu.VMEM((tile_m, width), BF),
+            pltpu.VMEM((tile_m, HD), F32),
+            pltpu.VMEM((tile_m, HD), F32),
+        ],
         compiler_params=params(),
         cost_estimate=pl.CostEstimate(
             flops=2 * rows * width * columns,
             bytes_accessed=2 * (rows * width + width * columns + rows * columns),
             transcendentals=0,
         ),
-    )(normed, weight, cosine, sine)
+    )(tokens, weight, gain[None, :], cosine, sine)
 
 
 def attend_kernel(scale, me_ref, q_ref, k_ref, v_ref, first_ref, o_ref, log_ref, bias):
@@ -754,10 +766,10 @@
     o_ref[1] = unturn(nn(grad, qa_ref[...])).astype(BF)
 
 
-def attend_back(me, qkv, grad_own, grad_all, log_own, delta_own, log_all, delta_all, first, cosine, sine):
+def attend_back(me, qkv, grad_all, log_own, delta_own, log_all, delta_all, first, cosine, sine):
     keys = qkv.shape[0]
-    rows = grad_own.shape[0]
     first_own, first_all = first
+    rows = first_own.shape[0]
     return pl.pallas_call(
         functools.partial(attend_back_kernel, HD**-0.5),
         out_shape=jax.ShapeDtypeStruct((3, rows, H * HD), BF),
@@ -771,7 +783,7 @@
                 pl.BlockSpec((keys, HD), lambda h, me: (0, h)),
                 pl.BlockSpec((rows, HD), lambda h, me: (me[0], H + h)),
                 pl.BlockSpec((rows, HD), lambda h, me: (me[0], 2 * H + h)),
-                pl.BlockSpec((rows, HD), lambda h, me: (0, h)),
+                pl.BlockSpec((rows, HD), lambda h, me: (me[0], h)),
                 pl.BlockSpec((keys, HD), lambda h, me: (0, h)),
                 pl.BlockSpec((1, rows, 8), lambda h, me: (h, 0, 0)),
                 pl.BlockSpec((1, rows, 8), lambda h, me: (h, 0, 0)),
@@ -799,7 +811,7 @@
         qkv,
         qkv,
         qkv,
-        grad_own,
+        grad_all,
         grad_all,
         log_own,
         delta_own,
@@ -818,7 +830,7 @@
     x_own,
     routes,
     grads,
-    misc,
+    near_in,
     weights,
     row_out,
     thin_out,
@@ -833,6 +845,7 @@
     came,
     thin,
     dots,
+    misc,
     s_load,
     s_x,
     r_x,
@@ -911,6 +924,8 @@
     def thin_here(e):
         return sent(thin.at[0], thin_out.at[e], s_thin.at[e], r_thin.at[e], (at.d, e))
 
+    misc_load = pltpu.make_async_copy(near_in.at[:, pl.ds(0, 128)], misc, s_load.at[8])
+    misc_load.start()
     own_load().start()
     sent(x_own, x_all.at[z, c], s_fwd.at[z], r_fwd.at[z], at.sibling).start()
     for j in range(1, chips):
@@ -920,6 +935,7 @@
             weight_load(k, e).start()
     grads_load().start()
     own_load().wait()
+    misc_load.wait()
 
     lanes = lax.broadcasted_iota(jnp.int32, (2 * rows, 128), 1)
 
@@ -1072,7 +1088,7 @@
             grad_store(k, e).wait()
 
 
-def moe_fused(normed, routes_all, grads_all, misc, weights, experts, collective_id):
+def moe_fused(normed, routes_all, grads_all, near, weights, experts, collective_id):
     rows, width = normed.shape
     chain = routes_all.shape[0] // rows
     chips = chain // 2
@@ -1089,7 +1105,7 @@
             jax.ShapeDtypeStruct((chain * rows, both), BF),
             jax.ShapeDtypeStruct(weights.shape, BF),
         ],
-        in_specs=[anywhere, vmem, anywhere, vmem, anywhere],
+        in_specs=[anywhere, vmem, anywhere, anywhere, anywhere],
         out_specs=[vmem, vmem, anywhere, anywhere],
         scratch_shapes=[
             pltpu.VMEM(blocks, BF),
@@ -1101,7 +1117,8 @@
             pltpu.VMEM((chips, rows, width), BF),
             pltpu.VMEM((chips, 8, 2 * rows), F32),
             pltpu.VMEM((2, 2 * rows, 128), F32),
-            dma((8,)),
+            pltpu.VMEM((width, 128), BF),
+            dma((9,)),
         ]
         + [dma((chips,))] * 8
         + [dma((chain,))] * 2,
@@ -1117,7 +1134,7 @@
         normed,
         routes_all.reshape(chips, 2 * rows, TOP),
         grads_all.reshape(blocks),
-        misc,
+        near,
         weights,
     )
 
@@ -1171,17 +1188,20 @@
 
 def spread_kernel(
     chips,
-    own,
-    side,
+    experts,
     mid,
     weights,
-    rows_in,
-    gate_in,
-    up_in,
-    cot_in,
     shared_in,
-    attn_in,
-    attended_in,
+    near_in,
+    normed,
+    cot,
+    row_sum,
+    thin,
+    routes,
+    middle,
+    gain,
+    attended_full,
+    log_own,
     all_out,
     side_out,
     mix_out,
@@ -1189,11 +1209,20 @@
     up_out,
     down_out,
     out_out,
+    base_out,
+    middle_out,
+    misc_out,
+    delta_out,
     mids,
     w,
     mix,
     dense,
     wide,
+    shared,
+    near,
+    own,
+    side,
+    turned,
     s_load,
     s_dense,
     s_chain,
@@ -1207,134 +1236,245 @@
 ):
     at = Place(chips)
     z, c = at.z, at.c
-    hidden = gate_in.shape[1]
-    rows = own.shape[0]
-    others = [(at.d, 2 * lax.rem(z + k, chips) + c) for k in range(1, chips)]
-    greet([at.sibling] + others, [None] * chips)
-
-    pairs = ((own, all_out, s_chain, r_chain, s_core, r_core), (side, side_out, s_side, r_side, s_score, r_score))
-
-    def along(p, k, src=None):
-        source, out, ss, rs = pairs[p][:4]
-        zz = lax.rem(z + k, chips)
-        ref = out.at[2 * z + c]
-        return sent(source if src is None else src, ref, ss.at[zz], rs.at[z], (at.d, 2 * zz + c))
-
-    def along_here(p, zz):
-        source, out, ss, rs = pairs[p][:4]
+    rows, width = normed.shape
+    hidden = shared_in.shape[1] // 3
+    has_up, has_down = z < chips - 1, z > 0
+    loads = [
+        pltpu.make_async_copy(
+            shared_in.at[:, pl.ds(k * hidden, hidden)], shared.at[k], s_load.at[k]
+        )
+        for k in range(3)
+    ]
+    loads.append(pltpu.make_async_copy(near_in, near, s_load.at[3]))
+    late = [
+        pltpu.make_async_copy(weights.at[2, e], w.at[:, pl.ds(e * hidden, hidden)], s_load.at[4 + e])
+        for e in range(EXP_DEV)
+    ]
+    late.append(pltpu.make_async_copy(mid, mids, s_load.at[4 + EXP_DEV]))
+    for copy in loads + late:
+        copy.start()
+    greet([at.sibling, at.up, at.down], [None, has_up, has_down])
+
+    lanes = lax.broadcasted_iota(jnp.int32, (rows, 128), 1)
+    turned[...] = jnp.zeros_like(turned)
+    for e in range(2 * chips):
+        turned[EXP_DEV * e : EXP_DEV * (e + 1), :] = thin[e, :EXP_DEV, :]
+    flipped = turned[...].T
+    grad_gates = jnp.where(c == 0, flipped[:rows], flipped[rows:])
+    loads[3].wait()
+    logits = jnp.where(lanes < experts, nn(normed[...], near[:, :128]), NEG)
+    powers = jnp.exp(logits - jnp.max(logits, axis=1, keepdims=True))
+    probs = powers / jnp.sum(powers, axis=1, keepdims=True)
+    named = routes[:, 0:1] == lanes
+    for j in range(1, TOP):
+        named = named | (routes[:, j : j + 1] == lanes)
+    chosen = jnp.where(named, probs, 0.0)
+    total = jnp.sum(chosen, axis=1, keepdims=True)
+    gates = chosen / total
+    grad_chosen = (grad_gates - jnp.sum(gates * grad_gates, axis=1, keepdims=True)) / total
+    grad_probs = jnp.where(named, grad_chosen, 0.0)
+    grad_logits = (
+        probs * (grad_probs - jnp.sum(probs * grad_probs, axis=1, keepdims=True))
+    ).astype(BF)
+    grad_normed = row_sum[...] + nt(grad_logits, near[:, :128])
+
+    for k in range(3):
+        loads[k].wait()
+    gate_v = nn(normed[...], shared[0])
+    up_v = nn(normed[...], shared[1])
+    back = nn(cot[...], shared[2])
+    act, slope = silu_parts(gate_v)
+    shared_mid = (act * up_v).astype(BF)
+    gate_grad = (back * up_v * slope).astype(BF)
+    up_grad = (back * act).astype(BF)
+    grad_normed = grad_normed + nt(gate_grad, shared[0]) + nt(up_grad, shared[1])
+
+    inverse = inverse_rms(middle[...])
+    unit = middle[...] * inverse
+    gain_grad = jnp.sum(grad_normed * unit, axis=0, keepdims=True)
+    scaled = grad_normed * gain[...]
+    grad_middle = cot[...].astype(F32) + inverse * (
+        scaled - unit * jnp.mean(scaled * unit, axis=-1, keepdims=True)
+    )
+    middle_out[...] = grad_middle
+    attn = grad_middle.astype(BF)
+    own[...] = nn(attn, near[:, 128:]).astype(BF)
+    columns = jnp.zeros((rows, 128), F32)
+    for h in range(H):
+        s = slice(h * HD, (h + 1) * HD)
+        delta = jnp.sum(own[:, s].astype(F32) * attended_full[:, s], axis=1, keepdims=True)
+        delta_out[h] = jnp.broadcast_to(delta, (rows, 8))
+        columns = jnp.where(lanes == h, log_own[h][:, :1], columns)
+        columns = jnp.where(lanes == H + h, delta, columns)
+    tall = side.shape[1]
+    columns = jnp.concatenate([columns, jnp.zeros((tall - rows, 128), F32)], axis=0)
+    side[...] = columns.T[: side.shape[0]]
+
+    pairs = (
+        (own, all_out, s_chain, r_chain, s_core, r_core),
+        (side, side_out, s_side, r_side, s_score, r_score),
+    )
+
+    def along(p, zz, direction, src=None):
+        out, ss, rs = pairs[p][1:4]
         ref = out.at[2 * zz + c]
-        return sent(ref, ref, ss.at[zz], rs.at[zz], (at.d, 2 * zz + c))
+        device = at.up if direction == 0 else at.down
+        return sent(ref if src is None else src, ref, ss.at[direction, zz], rs.at[zz], device)
 
     def over(p, zz, core, src=None):
         out, ss, rs = pairs[p][1], pairs[p][4], pairs[p][5]
         ref = out.at[2 * zz + core]
         return sent(ref if src is None else src, ref, ss.at[zz], rs.at[zz], at.sibling)
 
-    near = jnp.minimum(z, chips - 1 - z)
-
-    def order(j):
-        step = (j + 1) // 2
-        around = jnp.where(j % 2 == 1, z - step, z + step)
-        return jnp.where(j <= 2 * near, around, jnp.where(2 * z < chips, j, chips - 1 - j))
-
-    for j in range(1, chips):
-        for p in (1, 0):
-            along(p, lax.rem(order(j) - z + chips, chips)).start()
     locals_ = []
     for p in (1, 0):
+
+        @pl.when(has_up)
+        def _(p=p):
+            along(p, z, 0, pairs[p][0]).start()
+
+        @pl.when(has_down)
+        def _(p=p):
+            along(p, z, 1, pairs[p][0]).start()
+
         over(p, z, c, pairs[p][0]).start()
-        copy = pltpu.make_async_copy(pairs[p][0], pairs[p][1].at[2 * z + c], s_load.at[p])
+        copy = pltpu.make_async_copy(
+            pairs[p][0], pairs[p][1].at[2 * z + c], s_load.at[5 + EXP_DEV + p]
+        )
         copy.start()
         locals_.append(copy)
-    loads = [
-        pltpu.make_async_copy(weights.at[2, e], w.at[:, pl.ds(e * hidden, hidden)], s_load.at[2 + e])
-        for e in range(EXP_DEV)
-    ]
-    loads.append(pltpu.make_async_copy(mid, mids, s_load.at[2 + EXP_DEV]))
-    for copy in loads:
-        copy.start()
+
+    def arrived(zz, direction):
+        for p in (1, 0):
+            along(p, zz, direction).wait_recv()
+
+            @pl.when(has_up if direction == 0 else has_down)
+            def _(p=p):
+                along(p, zz, direction).start()
+
+            over(p, zz, c).start()
+
+    def at_distance(k):
+        @pl.when(z - k >= 0)
+        def _():
+            arrived(z - k, 0)
+
+        @pl.when(z + k < chips)
+        def _():
+            arrived(z + k, 1)
 
     stores = []
-    dense[0] = tn(rows_in[...], gate_in[...]).astype(BF)
-    dense[1] = tn(rows_in[...], up_in[...]).astype(BF)
-    dense[2] = tn(cot_in[...], shared_in[...]).astype(BF)
-    wide[...] = tn(attn_in[...], attended_in[...]).astype(BF)
-    for k, (src, dst) in enumerate(
-        ((dense.at[0], gate_out), (dense.at[1], up_out), (dense.at[2], down_out), (wide, out_out))
-    ):
+
+    def store(src, dst, k):
         copy = pltpu.make_async_copy(src, dst, s_dense.at[k])
         copy.start()
         stores.append(copy)
-    for copy in loads:
-        copy.wait()
 
     def mix_chip(zz):
         here = pl.ds(zz * 2 * rows, 2 * rows)
-        for n in range(0, own.shape[1], 256):
+        for n in range(0, width, 256):
             tile = nt(mids[here, :], w[n : n + 256, :]).astype(BF)
             mix[zz, 0, :, n : n + 256] = tile[:rows]
             mix[zz, 1, :, n : n + 256] = tile[rows:]
-        copy = pltpu.make_async_copy(mix.at[zz], mix_out.at[zz], s_dense.at[4 + zz])
-        copy.start()
-        stores.append(copy)
-
-    for j in range(chips):
+        store(mix.at[zz], mix_out.at[zz], 4 + zz)
+
+    dense[0] = tn(normed[...], gate_grad).astype(BF)
+    store(dense.at[0], gate_out, 0)
+    dense[1] = tn(normed[...], up_grad).astype(BF)
+    store(dense.at[1], up_out, 1)
+    dense[2] = tn(cot[...], shared_mid).astype(BF)
+    store(dense.at[2], down_out, 2)
+    wide[...] = tn(attn, attended_full[...].astype(BF)).astype(BF)
+    store(wide, out_out, 3)
+    base_out[...] = middle[...] + nt(shared_mid, shared[2])
+    at_distance(1)
+    for copy in late:
+        copy.wait()
+    half = (chips + 1) // 2
+    for j in range(half):
         mix_chip(j)
-        if j >= 1:
-            zz = order(j)
-            for p in (1, 0):
-                along_here(p, zz).wait_recv()
-                over(p, zz, c).start()
+    for k in range(2, chips):
+        at_distance(k)
+        if k == 2:
+            for j in range(half, chips):
+                mix_chip(j)
+            all_lanes = lax.broadcasted_iota(jnp.int32, (width, 128), 1)
+            column = jnp.broadcast_to(gain_grad, (8, width)).T[:, :1]
+            misc_out[:, :128] = jnp.where(
+                all_lanes == experts + 1, column, tn(normed[...], grad_logits)
+            )
+            misc_out[:, 128:] = jnp.zeros((width, 128), F32)
     for p in (1, 0):
         for zz in range(chips):
             over(p, zz, 1 - c).wait_recv()
             over(p, zz, c).wait_send()
 
-            @pl.when(zz != z)
+            @pl.when((zz <= z) & has_up)
             def _(p=p, zz=zz):
-                along_here(p, zz).wait_send()
+                along(p, zz, 0).wait_send()
+
+            @pl.when((zz >= z) & has_down)
+            def _(p=p, zz=zz):
+                along(p, zz, 1).wait_send()
 
     for copy in locals_ + stores:
         copy.wait()
 
 
-def spread(own, side, mid, weights, normed, gate_grad, up_grad, cot, shared_mid, attn, attended, collective_id):
-    rows, width = own.shape
+def spread(
+    mid, weights, shared, near, normed, cot, row_sum, thin, routes, middle, gain, attended, log_own, experts, collective_id
+):
+    rows, width = normed.shape
     keys, both = mid.shape
     chain = keys // rows
     chips = chain // 2
-    hidden = gate_grad.shape[1]
+    hidden = both // EXP_DEV
+    assert experts + 2 <= 128 and chips > 2
+    tall = 128 * (-(-rows // 128))
+    lines = 8 * (-(-2 * H // 8))
     dma = pltpu.SemaphoreType.DMA
     anywhere = pl.BlockSpec(memory_space=pl.ANY)
     vmem = pl.BlockSpec(memory_space=pltpu.VMEM)
+    out = jax.ShapeDtypeStruct
     return pl.pallas_call(
-        functools.partial(spread_kernel, chips),
+        functools.partial(spread_kernel, chips, experts),
         out_shape=[
-            jax.ShapeDtypeStruct((chain,) + own.shape, BF),
-            jax.ShapeDtypeStruct((chain,) + side.shape, F32),
-            jax.ShapeDtypeStruct((chips, 2, rows, width), BF),
-            jax.ShapeDtypeStruct((width, hidden), BF),
-            jax.ShapeDtypeStruct((width, hidden), BF),
-            jax.ShapeDtypeStruct((width, hidden), BF),
-            jax.ShapeDtypeStruct((width, width), BF),
+            out((chain, rows, width), BF),
+            out((chain, lines, tall), F32),
+            out((chips, 2, rows, width), BF),
+            out((width, hidden), BF),
+            out((width, hidden), BF),
+            out((width, hidden), BF),
+            out((width, width), BF),
+            out((rows, width), F32),
+            out((rows, width), F32),
+            out((width, 256), F32),
+            out((H, rows, 8), F32),
         ],
-        in_specs=[anywhere] * 4 + [vmem] * 7,
-        out_specs=[anywhere] * 7,
+        in_specs=[anywhere] * 4 + [vmem] * 9,
+        out_specs=[anywhere] * 7 + [vmem] * 4,
         scratch_shapes=[
             pltpu.VMEM((keys, both), BF),
             pltpu.VMEM((width, both), BF),
             pltpu.VMEM((chips, 2, rows, width), BF),
             pltpu.VMEM((3, width, hidden), BF),
             pltpu.VMEM((width, width), BF),
-            dma((3 + EXP_DEV,)),
+            pltpu.VMEM((3, width, hidden), BF),
+            pltpu.VMEM(near.shape, BF),
+            pltpu.VMEM((rows, width), BF),
+            pltpu.VMEM((lines, tall), F32),
+            pltpu.VMEM((128, 2 * rows), F32),
+            dma((7 + EXP_DEV,)),
             dma((4 + chips,)),
         ]
-        + [dma((chips,))] * 8,
-        compiler_params=params(collective_id=collective_id, has_side_effects=True),
+        + [dma((2, chips)), dma((chips,)), dma((chips,)), dma((chips,))] * 2,
+        compiler_params=pltpu.CompilerParams(
+            vmem_limit_bytes=MOE_VMEM, collective_id=collective_id, has_side_effects=True
+        ),
         cost_estimate=pl.CostEstimate(
             flops=2 * keys * both * width, bytes_accessed=64 * keys * width, transcendentals=0
         ),
-    )(own, side, mid, weights, normed, gate_grad, up_grad, cot, shared_mid, attn, attended)
+    )(mid, weights, shared, near, normed, cot, row_sum, thin, routes, middle, gain, attended, log_own)
 
 
 def finish_kernel(chips, chunks, n_in, experts, *refs):
@@ -1735,13 +1875,13 @@
     cosine, sine = turn_tables(rope_all)
     cosine_own = lax.dynamic_slice_in_dim(cosine, own_first, rows, 0)
     sine_own = lax.dynamic_slice_in_dim(sine, own_first, rows, 0)
-    wide = tokens_all.astype(F32)
-    normed_all = (wide * inverse_rms(wide) * gain_attn).astype(BF)
+    cosine_own = jnp.concatenate([cosine_own, cosine_own], axis=1)
+    sine_own = jnp.concatenate([-sine_own, sine_own], axis=1)
     inputs = tokens[0].astype(F32)
     inverse_one = inverse_rms(inputs)
     unit_one = inputs * inverse_one
     normed = (unit_one * gain_attn).astype(BF)
-    qkv = project_qkv(normed_all, qkv_weight, cosine, sine)
+    qkv = project_qkv(tokens_all, qkv_weight, gain_attn, cosine, sine)
     attended_full, log_own = attend(me, qkv, first_own)
     attended = attended_full.astype(BF)
     middle = inputs + nt(attended, out_t)
@@ -1762,28 +1902,55 @@
         total = jnp.sum(chosen, axis=1, keepdims=True)
         return probs, named, chosen / total, total
 
-    probs, named, gates, chosen_total = routing(normed_moe, routes[0])
-
-    shared_gate_v = nn(normed_moe, gate_shared)
-    shared_up_v = nn(normed_moe, up_shared)
-    shared_act, shared_slope = silu_parts(shared_gate_v)
-    shared_mid = (shared_act * shared_up_v).astype(BF)
-    shared_out = nt(shared_mid, down_t)
-    grad_out = cotangent[0].astype(F32)
-    grad_bf = cotangent[0]
-    grad_shared_mid = nn(grad_bf, down_t)
-    grad_shared_gate_v = (grad_shared_mid * shared_up_v * shared_slope).astype(BF)
-    grad_shared_up_v = (grad_shared_mid * shared_act).astype(BF)
-    grad_normed_moe = nt(grad_shared_gate_v, gate_shared) + nt(grad_shared_up_v, up_shared)
-
     if fits:
         row_sum, gate_grads, expert_mid, expert_grads = moe_fused(
-            normed_moe, routes_all, grads_all, misc, expert_weight, experts, 1
-        )
-        core = index % 2
-        gate_grads = gate_grads[:, :EXP_DEV].reshape(chain, EXP_DEV, 2, rows)
-        gate_grads = jnp.where(core == 0, gate_grads[:, :, 0], gate_grads[:, :, 1])
+            normed_moe, routes_all, grads_all, near, expert_weight, experts, 1
+        )
+        (
+            grad_all,
+            side_all,
+            mixture,
+            grad_gate_shared,
+            grad_up_shared,
+            grad_down_t,
+            grad_out_t,
+            base,
+            grad_middle,
+            grad_misc,
+            delta_own,
+        ) = spread(
+            expert_mid,
+            expert_weight,
+            shared,
+            near,
+            normed_moe,
+            cotangent[0],
+            row_sum,
+            gate_grads,
+            routes[0],
+            middle,
+            gain_moe[None, :],
+            attended_full,
+            log_own,
+            experts,
+            3,
+        )
+        side_all = side_all[:, : 2 * H, :rows]
     else:
+        probs, named, gates, chosen_total = routing(normed_moe, routes[0])
+
+        shared_gate_v = nn(normed_moe, gate_shared)
+        shared_up_v = nn(normed_moe, up_shared)
+        shared_act, shared_slope = silu_parts(shared_gate_v)
+        shared_mid = (shared_act * shared_up_v).astype(BF)
+        shared_out = nt(shared_mid, down_t)
+        grad_out = cotangent[0].astype(F32)
+        grad_bf = cotangent[0]
+        grad_shared_mid = nn(grad_bf, down_t)
+        grad_shared_gate_v = (grad_shared_mid * shared_up_v * shared_slope).astype(BF)
+        grad_shared_up_v = (grad_shared_mid * shared_act).astype(BF)
+        grad_normed_moe = nt(grad_shared_gate_v, gate_shared) + nt(grad_shared_up_v, up_shared)
+
         moe_all = gather([], [normed_moe], 1)[0].reshape(keys, width)
         unused, unused, gates_all, unused = routing(moe_all, routes_all)
         gates_here = lax.dynamic_slice_in_dim(gates_all, index * EXP_DEV, EXP_DEV, 1)
@@ -1792,61 +1959,41 @@
         )
         gate_grads = jnp.transpose(gate_grads.T.reshape(EXP_DEV, chain, rows), (1, 0, 2))
         row_sum, gate_grads = to_owner(row_part.reshape(chain, rows, width), gate_grads, 2)
-    gate_grads = gate_grads.reshape(experts, rows).T
+        gate_grads = gate_grads.reshape(experts, rows).T
+        grad_chosen = (gate_grads - jnp.sum(gates * gate_grads, axis=1, keepdims=True)) / chosen_total
+        grad_probs = jnp.where(named, grad_chosen, 0.0)
+        grad_logits = (
+            probs * (grad_probs - jnp.sum(probs * grad_probs, axis=1, keepdims=True))
+        ).astype(BF)
+        grad_route = tn(normed_moe, grad_logits)
+        grad_normed_moe = grad_normed_moe + row_sum + nt(grad_logits, route_weight)
+        grad_gain_moe = jnp.sum(grad_normed_moe * unit_two, axis=0)
+        scaled_two = grad_normed_moe * gain_moe
+        grad_middle = grad_out + inverse_two * (
+            scaled_two - unit_two * jnp.mean(scaled_two * unit_two, axis=-1, keepdims=True)
+        )
+        grad_attn = grad_middle.astype(BF)
+        grad_attended = nn(grad_attn, out_t).astype(BF)
+
+        delta = jnp.sum((grad_attended.astype(F32) * attended_full).reshape(rows, H, HD), axis=-1).T
+        side = jnp.concatenate([log_own[:, :, 0], delta], axis=0)
+        grad_all, side_all = gather([], [grad_attended, side], 3)
+        delta_own = jnp.broadcast_to(delta[:, :, None], (H, rows, 8))
     expert_sum = lax.psum_scatter(expert_grads, "dp", scatter_dimension=2, tiled=True)
-    grad_chosen = (gate_grads - jnp.sum(gates * gate_grads, axis=1, keepdims=True)) / chosen_total
-    grad_probs = jnp.where(named, grad_chosen, 0.0)
-    grad_logits = (
-        probs * (grad_probs - jnp.sum(probs * grad_probs, axis=1, keepdims=True))
-    ).astype(BF)
-    grad_route = tn(normed_moe, grad_logits)
-    grad_normed_moe = grad_normed_moe + row_sum + nt(grad_logits, route_weight)
-    grad_gain_moe = jnp.sum(grad_normed_moe * unit_two, axis=0)
-    scaled_two = grad_normed_moe * gain_moe
-    grad_middle = grad_out + inverse_two * (
-        scaled_two - unit_two * jnp.mean(scaled_two * unit_two, axis=-1, keepdims=True)
-    )
-    grad_attn = grad_middle.astype(BF)
-    grad_attended = nn(grad_attn, out_t).astype(BF)
-
-    delta = jnp.sum((grad_attended.astype(F32) * attended_full).reshape(rows, H, HD), axis=-1).T
-    side = jnp.concatenate([log_own[:, :, 0], delta], axis=0)
-    if fits:
-        grad_all, side_all, mixture, grad_gate_shared, grad_up_shared, grad_down_t, grad_out_t = spread(
-            grad_attended,
-            side,
-            expert_mid,
-            expert_weight,
-            normed_moe,
-            grad_shared_gate_v,
-            grad_shared_up_v,
-            grad_bf,
-            shared_mid,
-            grad_attn,
-            attended,
-            3,
-        )
-    else:
-        grad_all, side_all = gather([], [grad_attended, side], 3)
     grad_all = grad_all.reshape(keys, H * HD)
     side_all = jnp.transpose(side_all, (1, 0, 2)).reshape(2, H, 1, keys)
     grads = attend_back(
         me,
         qkv,
-        grad_attended,
         grad_all,
         log_own,
-        jnp.broadcast_to(delta[:, :, None], (H, rows, 8)),
+        delta_own,
         side_all[0],
         side_all[1],
         (first_own, first_all),
         cosine_own,
         sine_own,
     )
-    grad_misc = jnp.concatenate(
-        [grad_route, jnp.zeros((width, 1), F32), grad_gain_moe[:, None]], axis=1
-    )
-    grad_misc = jnp.pad(grad_misc, ((0, 0), (0, 256 - experts - 2)))
     if fits:
         out_sum, gate_sum, up_sum, down_sum, qkv_sum, misc_sum, grad_inputs, output = finish(
             [grad_out_t, grad_gate_shared, grad_up_shared, grad_down_t],
@@ -1861,10 +2008,14 @@
             gain_attn[None, :],
             grad_middle,
             mixture,
-            middle + shared_out,
+            base,
             4,
         )
     else:
+        grad_misc = jnp.concatenate(
+            [grad_route, jnp.zeros((width, 1), F32), grad_gain_moe[:, None]], axis=1
+        )
+        grad_misc = jnp.pad(grad_misc, ((0, 0), (0, 256 - experts - 2)))
         down = expert_weight[2]
         mixture = nt(expert_mid[:, :hidden], down[0])
         for e in range(1, EXP_DEV):

time: 569 us -> 561 us (0.986)
  Pallas kernels: 464 us -> 493 us
  matrix products: 17.1 us -> 2.54 us
  other arithmetic: 38.1 us -> 26.4 us
  local copies, waits for them, and re-layouts: 25.1 us -> 16.6 us
    pallas_call x1, Pallas kernels: 119 us -> 145 us  [finish(): pl.pallas_call(functools.partial(finish_kernel, chips, tuple(chunks), n,...]
    dot_general x6 -> x0, matrix products: 10 us -> none  [the longest x5 9.82 us: nn(): return jnp.dot(a, b, preferred_element_type=F32)]
  transfers between devices with their start and end apart: 3 -> 3, of which waited for: 0 -> 0; matrix products, arithmetic and copies ran while one was open for 11% -> 5% of each run, Pallas kernels for 83% -> 89%
where the time goes in v4:
time: 561 us; the launch traced here: 553 us
  Pallas kernels  493 us (88%)
  other arithmetic  26.4 us (5%)
  local copies, waits for them, and re-layouts  16.6 us (3%)
  between operations  14.2 us (3%)
    pallas_call x1, Pallas kernels, finish(): pl.pallas_call(functools.partial(finish_kernel, chips, tuple(chunks), n,...  145 us
    pallas_call x1, Pallas kernels, gather(): pl.pallas_call(functools.partial(gather_kernel, chips, len(full), len(cha...  131 us
    pallas_call x1, Pallas kernels, moe_fused(): pl.pallas_call(functools.partial(moe_kernel, chips, experts), out_shape=[...  106 us
    pallas_call x1, Pallas kernels, spread(): pl.pallas_call(functools.partial(spread_kernel, chips, experts), out_shap...  56.5 us
    pallas_call x1, Pallas kernels, project_qkv(): pl.pallas_call(functools.partial(qkv_kernel, per_block), out_shape=jax.Sh...  23.8 us
    pallas_call x1, Pallas kernels, attend_back(): pl.pallas_call(functools.partial(attend_back_kernel, HD ** (-0.5)), out_s...  18.8 us
    pallas_call x1, Pallas kernels, attend(): pl.pallas_call(functools.partial(attend_kernel, HD ** (-0.5)), out_shape=...  12.1 us
  transfers between devices with their start and end apart: 3, of which 0 were waited for; matrix products, arithmetic and copies ran while one was open for 5% of the time, Pallas kernels for 89%

profile of v4, /device:TPU:0, one launch (start us, length us, event | category | flops | bytes accessed | tf_op | source)
XLA Modules:
  0.0 553.1 jit_solution(13551971510164176370)
XLA Ops:
  7.2 1.9 convert_bitcast_fusion.1
  9.5 1.9 convert_bitcast_fusion.2
  11.4 2.0 pad_maximum_fusion
  14.1 0.8 copy.65
  14.9 0.8 convert_element_type.113.refs_0_
  17.4 131.1 %shard_map.229 = (bf16[32,40,3840]{2,1,0:T(8,128)(2,1)}, bf16[32,40,1408]{2,1,0:T(8,128)(2,1)}, bf16[8,192,1280]{2,1,0:T(8,128)(2,1)}, s32[8,192,7]{2,1,0:T(8,12...) custom-call(bf16[40,3840]{1,0:T(8,128)(2,1)} %convert_element_type.113.refs_0_, ...), custom_call_target="tpu_custom_call" | custom-call | bytes 369000448 | tf_op jit(solution)/shard_map/pallas_call | solution.py:309
  148.4 1.7 convert_reduce_fusion
  152.4 0.8 copy.66.first_ref
  153.8 4.4 multiply_sine_fusion
  158.2 23.8 %shard_map.230.q_ref.k_ref.v_ref.qa_ref.ko_ref.vo_ref = bf16[1536,3840]{1,0:T(8,128)(2,1)} custom-call(bf16[1536,1280]{1,0:T(8,128)(2,1)} %bitcast.96, bf16[1280,3840]{1,0:T(8,128)(2,1)} %bitcast.71, f32[1,1280]{1,0:T(1,128)} %reshape.182.gain_ref.refs_10_, f32[1536,64]{1,0:T(8,128)} %get-tuple-element.152.cos_ref, f32[1536,64]{1,0:T(8,128)} %get-tuple-element.151.sin_ref), custom_call_target="tpu_custom_call" | custom-call | flops 15099494400 | bytes 25559040 | tf_op jit(solution)/shard_map/pallas_call | solution.py:643
  182.0 12.1 %shard_map.231 = (f32[192,1280]{1,0:T(8,128)}, f32[10,192,8]{2,1,0:T(8,128)}) custom-call(s32[1]{0:T(128)} %bitcast.10.me_ref, bf16[1536,3840]{1,0:T(8,128)(2,1)} %shard_map.230.q_ref.k_ref.v_ref.qa_ref.ko_ref.vo_ref, bf16[1536,3840]{1,0:T(8,128)(2,1)} %shard_map.230.q_ref.k_ref.v_ref.qa_ref.ko_ref.vo_ref, ...), custom_call_target="tpu_custom_call" | custom-call | flops 1509949440 | bytes 7864320 | tf_op jit(solution)/shard_map/pallas_call | solution.py:690
  194.1 2.5 multiply_reduce_fusion
  196.6 1.1 multiply_convert_fusion.1.x_own.normed
  198.0 105.8 %shard_map.232 = (f32[192,1280]{1,0:T(8,128)}, f32[8,8,384]{2,1,0:T(8,128)}, bf16[1536,1792]{1,0:T(8,128)(2,1)}, bf16[3,2,1280,896]{3,2,1,0:T(8,128)(2,1)}) custom-call(bf16[192,1280]{1,0:T(8,128)(2,1)} %multiply_convert_fusion.1.x_own.normed, s32[4,384,7]{2,1,0:T(8,128)} %bitcast.97, bf16[4,2,192,1280]{3,2,1,0:T(8,128)(2,1)} %bitcast.95, ...), custom_call_target="tpu_custom_call" | custom-call | flops 56371445760 | bytes 38535168 | tf_op jit(solution)/shard_map/pallas_call | solution.py:1100
  304.6 0.8 copy.70.refs_9_
  305.4 0.9 constant_dynamic-slice_fusion
  306.3 0.9 fusion.13
  307.2 0.8 pad_maximum_fusion.3
  308.0 1.2 compare_select_fusion.firsta_ref
  309.2 1.3 convert_multiply_fusion
  310.5 56.5 %shard_map.233 = (bf16[8,192,1280]{2,1,0:T(8,128)(2,1)}, f32[8,24,256]{2,1,0:T(8,128)}, bf16[4,2,192,1280]{3,2,1,0:T(8,128)(2,1)}, bf16[1280,896]{1,0:T(8,128)(2...) custom-call(bf16[1536,1792]{1,0:T(8,128)(2,1)} %get-tuple-element.55, ...), custom_call_target="tpu_custom_call" | custom-call | flops 7046430720 | bytes 125829120 | tf_op jit(solution)/shard_map/pallas_call | solution.py:1439
  367.1 0.9 slice_bitcast_fusion.3
  368.1 0.7 squeeze.31.loga_ref
  368.9 0.7 squeeze.32.deltaa_ref
  369.6 18.8 %shard_map.234.refs_5_ = bf16[3,192,1280]{2,1,0:T(8,128)(2,1)} custom-call(s32[1]{0:T(128)} %bitcast.10.me_ref, bf16[1536,3840]{1,0:T(8,128)(2,1)} %shard_map.230.q_ref.k_ref.v_ref.qa_ref.ko_ref.vo_ref, bf16[1536,3840]{1,0:T(8,128)(2,1)} %shard_map.230.q_ref.k_ref.v_ref.qa_ref.ko_ref.vo_ref, ...), custom_call_target="tpu_custom_call" | custom-call | flops 5284823040 | bytes 15728640 | tf_op jit(solution)/shard_map/pallas_call | solution.py:773
  388.4 144.9 %shard_map.235 = (f32[40,1280]{1,0:T(8,128)}, f32[40,896]{1,0:T(8,128)}, f32[40,896]{1,0:T(8,128)}, f32[40,896]{1,0:T(8,128)}, f32[40,3840]{1,0:T(8,128)}, /*ind...) custom-call(bf16[2,2,4,2,40,1280]{5,4,3,2,1,0:T(8,128)(2,1)} %bitcast.79, ...), custom_call_target="tpu_custom_call" | custom-call | flops 3774873600 | bytes 314572800 | tf_op jit(solution)/shard_map/pallas_call | solution.py:1784
  533.4 0.7 slice.44
  534.8 0.8 slice_bitcast_fusion.4
  536.2 5.1 convert_bitcast_fusion
  541.3 0.8 copy.80
  542.1 0.8 copy.81
  542.9 0.8 copy.82
  (83 shorter events, 10.9 us)
Async XLA Ops:
  7.2 2.3 copy-start.3
  7.2 190.5 %all-gather.3.cloned.1.call-start = ((), (), s32[]{:S(2)}) async-start(), calls=%async_computation.1 | async-start | bytes 17203200 | tf_op jit(solution)/shard_map/all_gather | solution.py:1852
  13.4 0.7 copy-start.17
  13.4 1.5 copy-start.10
  13.4 1.5 copy-start.11
  13.4 1.5 copy-start.4
  13.4 2.3 copy-start.16
  13.4 2.4 copy-start.18
  13.4 2.5 copy-start.8
  13.4 3.2 copy-start.12
  13.5 297.0 %all-gather.5.cloned.1.call-start = ((), (), s32[]{:S(2)}) async-start(), calls=%async_computation.2 | async-start | bytes 8601600 | tf_op jit(solution)/shard_map/all_gather | solution.py:1892
  14.9 135.8 %copy-start.19 = (s32[1,4]{1,0:T(1,128)S(1)}, s32[1,4]{1,0:T(1,128)}, u32[]{:S(2)}) copy-start(s32[1,4]{1,0:T(1,128)} %param.16) | copy-start | bytes 52
  182.0 12.1 %copy-start = (bf16[32,40,1408]{2,1,0:T(8,128)(2,1)S(1)}, bf16[32,40,1408]{2,1,0:T(8,128)(2,1)}, u32[]{:S(2)}) copy-start(bf16[32,40,1408]{2,1,0:T(8,128)(2,1)} %get-tuple-element.49) | copy-start | bytes 10813444
  182.0 12.1 %copy-start.1 = (bf16[1,192,1280]{2,1,0:T(8,128)(2,1)S(1)}, bf16[1,192,1280]{2,1,0:T(8,128)(2,1)}, u32[]{:S(2)}) copy-start(bf16[1,192,1280]{2,1,0:T(8,128)(2,1)} %param.14) | copy-start | bytes 1474564
  196.6 107.2 %copy-start.2 = (f32[192,1280]{1,0:T(8,128)}, f32[192,1280]{1,0:T(8,128)S(1)}, u32[]{:S(2)}) copy-start(f32[192,1280]{1,0:T(8,128)S(1)} %get-tuple-element.154.middle) | copy-start | bytes 2949124
  197.7 338.5 %reduce-scatter.2.cloned.1.call-start = ((), (), s32[]{:S(2)}) async-start(), calls=%async_computation.3 | async-start | bytes 17203200 | tf_op jit(solution)/shard_map/reduce_scatter | solution.py:1982
  536.2 5.1 copy-start.7
  536.2 5.9 %copy-start.6 = (bf16[192,1280]{1,0:T(8,128)(2,1)S(1)}, bf16[192,1280]{1,0:T(8,128)(2,1)}, u32[]{:S(2)}) copy-start(bf16[192,1280]{1,0:T(8,128)(2,1)} %get-tuple-element.72) | copy-start | bytes 1474564
  541.3 1.6 copy-start.5
  541.3 2.4 copy-start.9
  541.3 3.1 copy-start.15
  541.3 3.8 copy-start.14
  541.3 4.4 copy-start.13
Sparse Core Ops, SparseCore 0:
  13.6 178.5 all-gather.2
  197.9 74.4 all-gather.4
  303.9 160.9 reduce-scatter.1

commit v5 on v4

--- a/solution.py
+++ b/solution.py
@@ -1854,7 +1854,7 @@
         [shared_gate.astype(BF), shared_up.astype(BF), shared_down.astype(BF).T], axis=1
     )
     fits = 2 * width * EXP_DEV * hidden * 3 + 2 * keys * (3 * EXP_DEV * hidden + 5 * width) < MOE_VMEM
-    chained = [tokens[0], routes[0], cotangent[0]] + ([shared] if fits else [])
+    chained = [tokens[0], routes[0].T, cotangent[0]] + ([shared] if fits else [])
     qkv_weight, near, tokens_all, routes_all, grads_all, *early = gather(
         [attn_qkv.astype(BF), near], chained, 0
     )
@@ -1863,7 +1863,7 @@
     qkv_weight = qkv_weight.reshape(width, 3 * H * HD)
     near = near.reshape(width, near.shape[-1])
     tokens_all = tokens_all.reshape(keys, width)
-    routes_all = routes_all.reshape(keys, TOP)
+    routes_all = jnp.swapaxes(routes_all, 1, 2).reshape(keys, TOP)
     cuts = [route_pad, route_pad + width]
     cuts += [cuts[-1] + hidden, cuts[-1] + 2 * hidden]
     misc, out_t = jnp.split(near, cuts[:1], axis=1)

time: 561 us -> 557 us (level)
  Pallas kernels: 493 us -> 486 us
    pallas_call x1, Pallas kernels: 131 us -> 125 us  [gather(): pl.pallas_call(functools.partial(gather_kernel, chips, len(full), len(cha...]
  transfers between devices with their start and end apart: 3 -> 3, of which waited for: 0 -> 0; matrix products, arithmetic and copies ran while one was open for 5% -> 6% of each run, Pallas kernels for 89% -> 89%
where the time goes in v5:
time: 557 us; the launch traced here: 549 us
  Pallas kernels  486 us (87%)
  other arithmetic  26.3 us (5%)
  local copies, waits for them, and re-layouts  18.9 us (3%)
  between operations  14.2 us (3%)
    pallas_call x1, Pallas kernels, finish(): pl.pallas_call(functools.partial(finish_kernel, chips, tuple(chunks), n,...  144 us
    pallas_call x1, Pallas kernels, gather(): pl.pallas_call(functools.partial(gather_kernel, chips, len(full), len(cha...  125 us
    pallas_call x1, Pallas kernels, moe_fused(): pl.pallas_call(functools.partial(moe_kernel, chips, experts), out_shape=[...  106 us
    pallas_call x1, Pallas kernels, spread(): pl.pallas_call(functools.partial(spread_kernel, chips, experts), out_shap...  56.6 us
    pallas_call x1, Pallas kernels, project_qkv(): pl.pallas_call(functools.partial(qkv_kernel, per_block), out_shape=jax.Sh...  23.8 us
    pallas_call x1, Pallas kernels, attend_back(): pl.pallas_call(functools.partial(attend_back_kernel, HD ** (-0.5)), out_s...  18.8 us
    pallas_call x1, Pallas kernels, attend(): pl.pallas_call(functools.partial(attend_kernel, HD ** (-0.5)), out_shape=...  12.1 us
  transfers between devices with their start and end apart: 3, of which 0 were waited for; matrix products, arithmetic and copies ran while one was open for 6% of the time, Pallas kernels for 89%

profile of v5, /device:TPU:0, one launch (start us, length us, event | category | flops | bytes accessed | tf_op | source)
XLA Modules:
  0.0 548.7 jit_solution(16572415170589814019)
XLA Ops:
  7.2 1.9 convert_bitcast_fusion.1
  9.5 1.9 convert_bitcast_fusion.2
  11.4 2.0 pad_maximum_fusion
  13.5 0.8 copy-done.10
  14.6 0.8 convert_element_type.113.refs_0_
  17.7 125.3 %shard_map.229 = (bf16[32,40,3840]{2,1,0:T(8,128)(2,1)}, bf16[32,40,1408]{2,1,0:T(8,128)(2,1)}, bf16[8,192,1280]{2,1,0:T(8,128)(2,1)}, s32[8,7,192]{2,1,0:T(8,12...) custom-call(bf16[40,3840]{1,0:T(8,128)(2,1)} %convert_element_type.113.refs_0_, ...), custom_call_target="tpu_custom_call" | custom-call | bytes 369000448 | tf_op jit(solution)/shard_map/pallas_call | solution.py:309
  142.9 1.6 convert_reduce_fusion
  146.9 0.8 copy.75.first_ref
  148.3 4.3 multiply_sine_fusion
  152.6 23.8 %shard_map.230.q_ref.k_ref.v_ref.qa_ref.ko_ref.vo_ref = bf16[1536,3840]{1,0:T(8,128)(2,1)} custom-call(bf16[1536,1280]{1,0:T(8,128)(2,1)} %bitcast.103, bf16[1280,3840]{1,0:T(8,128)(2,1)} %bitcast.76, f32[1,1280]{1,0:T(1,128)} %reshape.182.gain_ref.refs_10_, f32[1536,64]{1,0:T(8,128)} %get-tuple-element.152.cos_ref, f32[1536,64]{1,0:T(8,128)} %get-tuple-element.151.sin_ref), custom_call_target="tpu_custom_call" | custom-call | flops 15099494400 | bytes 25559040 | tf_op jit(solution)/shard_map/pallas_call | solution.py:643
  176.4 12.1 %shard_map.231 = (f32[192,1280]{1,0:T(8,128)}, f32[10,192,8]{2,1,0:T(8,128)}) custom-call(s32[1]{0:T(128)} %bitcast.12.me_ref, bf16[1536,3840]{1,0:T(8,128)(2,1)} %shard_map.230.q_ref.k_ref.v_ref.qa_ref.ko_ref.vo_ref, bf16[1536,3840]{1,0:T(8,128)(2,1)} %shard_map.230.q_ref.k_ref.v_ref.qa_ref.ko_ref.vo_ref, ...), custom_call_target="tpu_custom_call" | custom-call | flops 1509949440 | bytes 7864320 | tf_op jit(solution)/shard_map/pallas_call | solution.py:690
  188.5 2.5 multiply_reduce_fusion
  191.1 1.1 multiply_convert_fusion.1.x_own.normed
  192.4 1.2 copy.76
  193.7 105.8 %shard_map.232 = (f32[192,1280]{1,0:T(8,128)}, f32[8,8,384]{2,1,0:T(8,128)}, bf16[1536,1792]{1,0:T(8,128)(2,1)}, bf16[3,2,1280,896]{3,2,1,0:T(8,128)(2,1)}) custom-call(bf16[192,1280]{1,0:T(8,128)(2,1)} %multiply_convert_fusion.1.x_own.normed, s32[4,384,7]{2,1,0:T(8,128)} %bitcast.90, bf16[4,2,192,1280]{3,2,1,0:T(8,128)(2,1)} %bitcast.102, ...), custom_call_target="tpu_custom_call" | custom-call | flops 56371445760 | bytes 38535168 | tf_op jit(solution)/shard_map/pallas_call | solution.py:1100
  300.1 0.8 copy.73
  301.0 0.8 copy.80.refs_9_
  301.8 0.9 constant_dynamic-slice_fusion
  302.7 0.9 fusion.13
  303.6 0.8 pad_maximum_fusion.3
  304.4 1.2 compare_select_fusion.firsta_ref
  305.7 1.3 convert_multiply_fusion
  306.9 56.6 %shard_map.233 = (bf16[8,192,1280]{2,1,0:T(8,128)(2,1)}, f32[8,24,256]{2,1,0:T(8,128)}, bf16[4,2,192,1280]{3,2,1,0:T(8,128)(2,1)}, bf16[1280,896]{1,0:T(8,128)(2...) custom-call(bf16[1536,1792]{1,0:T(8,128)(2,1)} %get-tuple-element.55, ...), custom_call_target="tpu_custom_call" | custom-call | flops 7046430720 | bytes 125829120 | tf_op jit(solution)/shard_map/pallas_call | solution.py:1439
  363.6 0.9 slice_bitcast_fusion.3
  364.6 0.7 squeeze.31.loga_ref
  366.2 18.8 %shard_map.234.refs_5_ = bf16[3,192,1280]{2,1,0:T(8,128)(2,1)} custom-call(s32[1]{0:T(128)} %bitcast.12.me_ref, bf16[1536,3840]{1,0:T(8,128)(2,1)} %shard_map.230.q_ref.k_ref.v_ref.qa_ref.ko_ref.vo_ref, bf16[1536,3840]{1,0:T(8,128)(2,1)} %shard_map.230.q_ref.k_ref.v_ref.qa_ref.ko_ref.vo_ref, ...), custom_call_target="tpu_custom_call" | custom-call | flops 5284823040 | bytes 15728640 | tf_op jit(solution)/shard_map/pallas_call | solution.py:773
  384.9 144.0 %shard_map.235 = (f32[40,1280]{1,0:T(8,128)}, f32[40,896]{1,0:T(8,128)}, f32[40,896]{1,0:T(8,128)}, f32[40,896]{1,0:T(8,128)}, f32[40,3840]{1,0:T(8,128)}, /*ind...) custom-call(bf16[2,2,4,2,40,1280]{5,4,3,2,1,0:T(8,128)(2,1)} %bitcast.84, ...), custom_call_target="tpu_custom_call" | custom-call | flops 3774873600 | bytes 314572800 | tf_op jit(solution)/shard_map/pallas_call | solution.py:1784
  530.3 0.8 slice_bitcast_fusion.4
  531.8 5.1 convert_bitcast_fusion
  536.9 0.8 copy.93
  537.7 0.8 copy.94
  538.5 0.8 copy.95
  (87 shorter events, 12.7 us)
Async XLA Ops:
  7.2 2.3 copy-start.3
  7.2 185.0 %all-gather.3.cloned.1.call-start = ((), (), s32[]{:S(2)}) async-start(), calls=%async_computation.1 | async-start | bytes 17203200 | tf_op jit(solution)/shard_map/all_gather | solution.py:1852
  13.4 0.9 copy-start.10
  13.4 1.0 copy-start.11
  13.4 1.2 copy-start.4
  13.4 2.0 copy-start.18
  13.4 2.1 copy-start.19
  13.4 2.2 copy-start.17
  13.4 2.8 copy-start.8
  13.4 3.5 copy-start.12
  13.5 293.5 %all-gather.5.cloned.1.call-start = ((), (), s32[]{:S(2)}) async-start(), calls=%async_computation.2 | async-start | bytes 8601600 | tf_op jit(solution)/shard_map/all_gather | solution.py:1892
  14.6 130.5 %copy-start.20 = (s32[1,4]{1,0:T(1,128)S(1)}, s32[1,4]{1,0:T(1,128)}, u32[]{:S(2)}) copy-start(s32[1,4]{1,0:T(1,128)} %param.16) | copy-start | bytes 52
  176.4 12.1 %copy-start = (bf16[32,40,1408]{2,1,0:T(8,128)(2,1)S(1)}, bf16[32,40,1408]{2,1,0:T(8,128)(2,1)}, u32[]{:S(2)}) copy-start(bf16[32,40,1408]{2,1,0:T(8,128)(2,1)} %get-tuple-element.49) | copy-start | bytes 10813444
  176.4 12.1 %copy-start.1 = (bf16[1,192,1280]{2,1,0:T(8,128)(2,1)S(1)}, bf16[1,192,1280]{2,1,0:T(8,128)(2,1)}, u32[]{:S(2)}) copy-start(bf16[1,192,1280]{2,1,0:T(8,128)(2,1)} %param.14) | copy-start | bytes 1474564
  191.0 108.4 %copy-start.2 = (f32[192,1280]{1,0:T(8,128)}, f32[192,1280]{1,0:T(8,128)S(1)}, u32[]{:S(2)}) copy-start(f32[192,1280]{1,0:T(8,128)S(1)} %get-tuple-element.154.middle) | copy-start | bytes 2949124
  191.1 1.4 copy-start.16
  192.2 339.6 %reduce-scatter.2.cloned.1.call-start = ((), (), s32[]{:S(2)}) async-start(), calls=%async_computation.3 | async-start | bytes 17203200 | tf_op jit(solution)/shard_map/reduce_scatter | solution.py:1982
  531.8 5.1 copy-start.7
  531.8 5.9 %copy-start.6 = (bf16[192,1280]{1,0:T(8,128)(2,1)S(1)}, bf16[192,1280]{1,0:T(8,128)(2,1)}, u32[]{:S(2)}) copy-start(bf16[192,1280]{1,0:T(8,128)(2,1)} %get-tuple-element.72) | copy-start | bytes 1474564
  536.9 1.6 copy-start.5
  536.9 2.4 copy-start.9
  536.9 3.1 copy-start.15
  536.9 3.8 copy-start.14
  536.9 4.4 copy-start.13
Sparse Core Ops, SparseCore 0:
  13.6 176.6 all-gather.2
  192.3 74.8 all-gather.4
  299.6 160.5 reduce-scatter.1
